TPU v7x, 256 devices: a whole 4x4x8 slice. The times are simulated.
256 devices in a mesh: rep: 64 (over z, y, x_hi), tp: 4 (over x_lo, core).
Axes of the slice: x: 4 (x_hi: 2, x_lo: 2; x = x_hi * 2 + x_lo), y: 4, z: 8, core: 2. Of those that a mesh axis runs over, the one named last changes fastest.
Arguments:
- momentum: bfloat16 [64, 128, 13824], P('rep', None, 'tp'), may hold values from -6 to 6
- grad: bfloat16 [64, 128, 13824], P('rep', None, 'tp'), may hold values from -64 to 64
- freq_rows: int32 [8], replicated, may hold values from 0 to 15, as said below
- freq_cols: int32 [8], replicated, may hold values from 0 to 15, as said below
Outputs:
- momentum_out: bfloat16 [64, 128, 13824], P('rep', None, 'tp')
- update: float32 [128, 13824], P(None, 'tp')
Inputs may be any that keep to these rules, and one draw needn't show every extreme that they name: `freq_rows`: 8 distinct frequencies, among them 0 and 15. `freq_cols`: 8 distinct frequencies, among them 0 and 15.
All inputs are finite; a program needn't handle non-finite values.
Results may differ from a plain program's by a relative error of at most 0.001.
Values sent between devices are 32-bit elements; how exact they have to be, the bound alone decides.
No kernel may reach another device: no remote copies, remote signals or barrier semaphores. Data moves between devices by JAX's collectives and lax.ppermute only.
A program may use at most 64 MiB of HBM per device.

v0:
```python
import math

import jax
import jax.numpy as jnp
from jax import lax
from jax.sharding import PartitionSpec as P

BLOCK = 64
KEEP = 8


def basis(freqs):
    points = jnp.arange(BLOCK, dtype=jnp.float32)
    waves = freqs.astype(jnp.float32)[:, None]
    scale = jnp.where(freqs == 0, math.sqrt(1.0 / BLOCK), math.sqrt(2.0 / BLOCK)).astype(
        jnp.float32
    )
    return scale[:, None] * jnp.cos(math.pi * (2.0 * points[None, :] + 1.0) * waves / (2.0 * BLOCK))


def forward(fresh, row_basis, col_basis):
    nrows, ncols = fresh.shape
    blocks = fresh.reshape(nrows, ncols // BLOCK, BLOCK)
    right = jnp.einsum("rcq,jq->rcj", blocks, col_basis, precision=lax.Precision.HIGHEST)
    right = right.reshape(nrows // BLOCK, BLOCK, -1)
    return jnp.einsum("ip,bpx->bix", row_basis, right, precision=lax.Precision.HIGHEST)


def inverse(coeffs, row_basis, col_basis):
    left = jnp.einsum("ip,bix->bpx", row_basis, coeffs, precision=lax.Precision.HIGHEST)
    left = left.reshape(coeffs.shape[0] * BLOCK, -1, KEEP)
    image = jnp.einsum("rcj,jq->rcq", left, col_basis, precision=lax.Precision.HIGHEST)
    return image.reshape(coeffs.shape[0] * BLOCK, -1)


def body(momentum, grad, freq_rows, freq_cols):
    row_basis = basis(freq_rows)
    col_basis = basis(freq_cols)
    fresh = 0.9 * momentum[0].astype(jnp.float32) + grad[0].astype(jnp.float32)
    own_coeffs = forward(fresh, row_basis, col_basis)
    flat = own_coeffs.reshape(-1)
    total_flat = lax.psum(flat, "rep")
    momentum_out = (fresh - inverse(own_coeffs, row_basis, col_basis)).astype(jnp.bfloat16)[None]
    field = inverse(total_flat.reshape(own_coeffs.shape), row_basis, col_basis)
    squares = lax.psum(jnp.sum(field * field), "tp")
    entries = field.shape[0] * field.shape[1] * lax.axis_size("tp")
    update = field / jnp.sqrt(squares / entries + 1e-06)
    return (momentum_out, update)


def solution(mesh):
    placed = (P("rep", None, "tp"), P("rep", None, "tp"), P(), P())
    return jax.shard_map(
        body,
        mesh=mesh,
        in_specs=placed,
        out_specs=(P("rep", None, "tp"), P(None, "tp")),
        check_vma=False,
    )
```

profile of v0, /device:TPU:1, one launch (start us, length us, event | category | flops | bytes accessed | tf_op | source)
XLA Modules:
  0.0 389.0 jit_solution(15306103861069716563)
XLA Ops:
  0.6 0.0 copy-start.1
  0.7 0.7 convert_element_type.25
  1.4 0.7 compare_select_fusion
  2.0 0.7 convert_element_type.24
  2.7 0.7 compare_select_fusion.1
  3.4 1.9 copy.12
  5.2 0.0 copy-done.1
  5.3 1.0 copy.13
  6.3 0.2 convert_add_fusion
  6.5 1.1 fusion.9
  7.6 0.3 reshape.47
  7.8 0.7 convolution_bitcast_fusion.2
  8.5 306.9 %psum.14 = f32[2,8,432]{2,1,0:T(8,128)S(1)} all-reduce(f32[2,8,432]{2,1,0:T(8,128)S(1)} %convolution_bitcast_fusion.2), channel_id=1, replica_groups=mesh['rep'=64,'tp'=4] {'rep'}, use_global_device_ids=true, to_apply=%region_0.1 | all-reduce | flops 6912 | bytes 55296 | tf_op jit(solution)/shard_map/psum | solution.py:42
  315.4 0.5 convolution_bitcast_fusion.1
  315.9 0.2 copy.15
  316.2 0.3 reshape.48
  316.4 0.5 convolution_bitcast_fusion
  317.0 0.2 copy.16
  317.2 0.9 reshape.52
  318.1 1.7 fusion.7
  319.8 0.4 fusion
  320.2 0.0 copy-start
  320.2 1.6 copy.17
  321.9 0.0 copy-done
  321.9 2.5 multiply_reduce_fusion
  324.3 61.8 %psum.15 = f32[]{:T(128)} all-reduce(f32[]{:T(128)} %get-tuple-element.6), channel_id=1, replica_groups=mesh['rep'=64,'tp'=4] {'tp'}, use_global_device_ids=true, to_apply=%region_2.3 | all-reduce | flops 1 | bytes 8 | tf_op jit(solution)/shard_map/psum | solution.py:45
  386.9 0.2 broadcast_divide_fusion
  387.1 1.9 copy.18
  (1 shorter events, 0.0 us)
Async XLA Ops:
  0.6 4.6 %copy-start.1 = (bf16[1,128,3456]{2,1,0:T(8,128)(2,1)S(1)}, bf16[1,128,3456]{2,1,0:T(8,128)(2,1)}, u32[]{:S(2)}) copy-start(bf16[1,128,3456]{2,1,0:T(8,128)(2,1)} %param.5) | copy-start | bytes 2654212
  320.2 1.7 copy-start
where the time goes:
time: 389 us
  blocking collectives  369 us (95%)
  local copies, waits for them, and re-layouts  8.37 us (2%)
  matrix products  6.95 us (2%)
    psum x1, blocking collectives, body(): total_flat = lax.psum(flat, 'rep')  307 us
    psum x1, blocking collectives, body(): squares = lax.psum(jnp.sum(field * field), 'tp')  61.8 us

commit v1 on v0

v1 whole, which is shorter than its diff:
```python
import functools
import math

import jax
import jax.numpy as jnp
from jax import lax
from jax.experimental import pallas as pl
from jax.experimental.pallas import tpu as pltpu
from jax.sharding import PartitionSpec as P

BLOCK = 64
KEEP = 8
LANES = 128
SPAN = 1024
VMEM_BYTES = 16 * 1024 * 1024


def spans(cols):
    return [(start, min(SPAN, cols - start)) for start in range(0, cols, SPAN)]


def basis_tile(freq_ref):
    row = lax.broadcasted_iota(jnp.int32, (KEEP, LANES), 0)
    point = lax.broadcasted_iota(jnp.int32, (KEEP, LANES), 1) & (BLOCK - 1)
    freq = jnp.zeros((KEEP, LANES), jnp.int32)
    for k in range(KEEP):
        freq = jnp.where(row == k, freq_ref[k], freq)
    turn = ((2 * point + 1) * freq) & (4 * BLOCK - 1)
    turn = jnp.minimum(turn, 4 * BLOCK - turn)
    x = (BLOCK - turn).astype(jnp.float32) * (math.pi / (2 * BLOCK))
    y = x * x
    series = jnp.full_like(x, 1.0 / math.factorial(13))
    for n in (11, 9, 7, 5, 3, 1):
        series = 1.0 / math.factorial(n) - series * y
    scale = jnp.where(freq == 0, math.sqrt(1.0 / BLOCK), math.sqrt(2.0 / BLOCK))
    return x * series * scale


def split(v):
    high = v.astype(jnp.bfloat16)
    return high, (v - high.astype(jnp.float32)).astype(jnp.bfloat16)


def row_matrix(freq_ref):
    tile = basis_tile(freq_ref)
    lane = lax.broadcasted_iota(jnp.int32, (KEEP, LANES), 1)
    return jnp.concatenate([jnp.where(lane < BLOCK, tile, 0.0), jnp.where(lane >= BLOCK, tile, 0.0)], axis=0)


def col_matrix(freq_ref):
    tile = basis_tile(freq_ref)
    lane = lax.broadcasted_iota(jnp.int32, (KEEP, LANES), 1)
    left = jnp.where(lane < BLOCK, tile, 0.0)
    right = jnp.where(lane >= BLOCK, tile, 0.0)
    pair = jnp.concatenate([left, right], axis=0)
    none = jnp.zeros_like(pair)
    rows = []
    for t in range(SPAN // LANES):
        rows.append(jnp.concatenate([pair if u == t else none for u in range(SPAN // LANES)], axis=1))
    return split(jnp.concatenate(rows, axis=0))


def dot(a, b, dims):
    return lax.dot_general(a, b, (dims, ((), ())), preferred_element_type=jnp.float32)


def forward_kernel(fr_ref, fc_ref, m_ref, g_ref, out_ref, both, sems):
    cols = m_ref.shape[1]
    copies = []
    for n, (start, width) in enumerate(spans(cols)):
        for k, src in enumerate((m_ref, g_ref)):
            copy = pltpu.make_async_copy(
                src.at[:, pl.ds(start, width)], both.at[pl.ds(LANES * k, LANES), pl.ds(start, width)], sems.at[n, k]
            )
            copy.start()
            copies.append(copy)
    rows = row_matrix(fr_ref)
    high, low = split(jnp.concatenate([0.9 * rows, rows], axis=1))
    lhs = jnp.concatenate([high, low], axis=0)
    wide_high, wide_low = col_matrix(fc_ref)
    for n, (start, width) in enumerate(spans(cols)):
        copies[2 * n].wait()
        copies[2 * n + 1].wait()
        y = dot(lhs, both[:, start : start + width], ((1,), (0,)))
        y_high, y_low = split(y[:16] + y[16:])
        c = dot(jnp.concatenate([y_high, y_low], axis=0), wide_high[:, :width], ((1,), (1,)))
        c = c[:16] + c[16:] + dot(y_high, wide_low[:, :width], ((1,), (1,)))
        out_ref[:, n * LANES : (n + 1) * LANES] = c


def image_of(coeffs, row_stack, wide_high, wide_low, width):
    high, low = split(coeffs)
    z = dot(jnp.concatenate([high, low], axis=0), wide_high[:, :width], ((1,), (0,)))
    z = z[:16] + z[16:] + dot(high, wide_low[:, :width], ((1,), (0,)))
    z_high, z_low = split(z)
    return dot(row_stack, jnp.concatenate([z_high, z_low, z_high], axis=0), ((0,), (0,)))


def stack_rows(freq_ref):
    high, low = split(row_matrix(freq_ref))
    return jnp.concatenate([high, high, low], axis=0)


def momentum_kernel(fr_ref, fc_ref, m_ref, g_ref, c_ref, out_ref):
    row_stack = stack_rows(fr_ref)
    wide_high, wide_low = col_matrix(fc_ref)
    for n, (start, width) in enumerate(spans(m_ref.shape[1])):
        here = slice(start, start + width)
        image = image_of(c_ref[:, n * LANES : (n + 1) * LANES], row_stack, wide_high, wide_low, width)
        fresh = 0.9 * m_ref[:, here].astype(jnp.float32) + g_ref[:, here].astype(jnp.float32)
        out_ref[:, here] = (fresh - image).astype(jnp.bfloat16)


def update_kernel(entries, fr_ref, fc_ref, total_ref, p0, p1, p2, p3, out_ref, held, sems):
    row_stack = stack_rows(fr_ref)
    wide_high, wide_low = col_matrix(fc_ref)
    squares = jnp.sum(p0[...] + p1[...] + p2[...] + p3[...])
    scale = lax.rsqrt(jnp.full((16, LANES), squares, jnp.float32) * (1.0 / entries) + 1e-06)
    copies = []
    for n, (start, width) in enumerate(spans(out_ref.shape[1])):
        here = slice(start, start + width)
        part = total_ref[:, n * LANES : (n + 1) * LANES] * scale
        held[:, here] = image_of(part, row_stack, wide_high, wide_low, width)
        copy = pltpu.make_async_copy(held.at[:, pl.ds(start, width)], out_ref.at[:, pl.ds(start, width)], sems.at[n])
        copy.start()
        copies.append(copy)
    for copy in copies:
        copy.wait()


SMEM = pl.BlockSpec(memory_space=pltpu.SMEM)
VMEM = pl.BlockSpec(memory_space=pltpu.VMEM)
ANY = pl.BlockSpec(memory_space=pl.ANY)


def forward(freq_rows, freq_cols, m, g):
    rows, cols = m.shape
    n = len(spans(cols))
    return pl.pallas_call(
        forward_kernel,
        out_shape=jax.ShapeDtypeStruct((2 * KEEP, n * LANES), jnp.float32),
        in_specs=[SMEM, SMEM, ANY, ANY],
        out_specs=VMEM,
        scratch_shapes=[pltpu.VMEM((2 * rows, cols), jnp.bfloat16), pltpu.SemaphoreType.DMA((n, 2))],
        compiler_params=pltpu.CompilerParams(vmem_limit_bytes=VMEM_BYTES),
        cost_estimate=pl.CostEstimate(flops=2 * 48 * rows * cols, bytes_accessed=4 * rows * cols, transcendentals=0),
        name="forward",
    )(freq_rows, freq_cols, m, g)


def momentum_left(freq_rows, freq_cols, m, g, coeffs):
    rows, cols = m.shape
    return pl.pallas_call(
        momentum_kernel,
        out_shape=jax.ShapeDtypeStruct((rows, cols), jnp.bfloat16),
        in_specs=[SMEM, SMEM, VMEM, VMEM, VMEM],
        out_specs=VMEM,
        compiler_params=pltpu.CompilerParams(vmem_limit_bytes=VMEM_BYTES),
        cost_estimate=pl.CostEstimate(flops=2 * 48 * rows * cols, bytes_accessed=6 * rows * cols, transcendentals=0),
        name="momentum",
    )(freq_rows, freq_cols, m, g, coeffs)


def updated(freq_rows, freq_cols, total, parts, rows, cols, entries):
    n = len(spans(cols))
    return pl.pallas_call(
        functools.partial(update_kernel, entries),
        out_shape=jax.ShapeDtypeStruct((rows, cols), jnp.float32),
        in_specs=[SMEM, SMEM] + [VMEM] * 5,
        out_specs=ANY,
        scratch_shapes=[pltpu.VMEM((rows, cols), jnp.float32), pltpu.SemaphoreType.DMA((n,))],
        compiler_params=pltpu.CompilerParams(vmem_limit_bytes=VMEM_BYTES),
        cost_estimate=pl.CostEstimate(flops=2 * 48 * rows * cols, bytes_accessed=4 * rows * cols, transcendentals=0),
        name="update",
    )(freq_rows, freq_cols, total, *parts)


def exchange_sum(v, axes, members):
    return jnp.sum(lax.all_to_all(jnp.broadcast_to(v, (members,) + v.shape), axes, 0, 0, tiled=True), axis=0)


def body(momentum, grad, freq_rows, freq_cols):
    m, g = momentum[0], grad[0]
    rows, cols = m.shape
    tp = lax.axis_size("tp")
    own = forward(freq_rows, freq_cols, m, g)
    total = exchange_sum(exchange_sum(own, ("y", "x"), 8), ("z",), 8)
    tiles = (total * total).reshape(2, KEEP, total.shape[1])
    squares = tiles[0] + tiles[1]
    squares = sum(squares[:, k : k + LANES] for k in range(0, total.shape[1], LANES))
    parts = [squares] + [lax.ppermute(squares, "tp", [(i, i ^ k) for i in range(tp)]) for k in range(1, tp)]
    kept = momentum_left(freq_rows, freq_cols, m, g, own)
    update = updated(freq_rows, freq_cols, total, parts, rows, cols, float(rows * cols * tp))
    return kept[None], update


def solution(mesh):
    rep = ("z", "y", "x")
    fine = jax.sharding.Mesh(mesh.devices.reshape(8, 4, 2, 4), rep + ("tp",))
    placed = (P(rep, None, "tp"), P(rep, None, "tp"), P(), P())
    return jax.shard_map(
        body,
        mesh=fine,
        in_specs=placed,
        out_specs=(P(rep, None, "tp"), P(None, "tp")),
        check_vma=False,
    )
```

time: 389 us -> 49.9 us (0.13)
  blocking collectives: 369 us -> 32.3 us
  Pallas kernels: 0 us -> 7.59 us
  matrix products: 6.95 us -> 0 us
  starting transfers between devices: 0 us -> 5.25 us
  local copies, waits for them, and re-layouts: 8.37 us -> 3.69 us
    psum x2 -> x0, blocking collectives: 369 us -> none  [the longest x1 307 us: body(): total_flat = lax.psum(flat, 'rep')]
    all_to_all x0 -> x2, blocking collectives: none -> 32.3 us  [exchange_sum(): lax.all_to_all(jnp.broadcast_to(v, (members,) + v.shape), axes, 0, 0, til...]
    pallas_call x0 -> x3, Pallas kernels: none -> 7.59 us  [the longest x1 2.69 us: forward(): pl.pallas_call(forward_kernel, out_shape=jax.ShapeDtypeStruct((2 * KEEP,...]
    dot_general x6 -> x0, matrix products: 6.95 us -> none  [the longest x2 4.16 us: inverse(): jnp.einsum('rcj,jq->rcq', left, col_basis, precision=lax.Precision.HIGHEST)]
    ppermute x0 -> x3, starting transfers between devices: none -> 5.25 us  [body(): lax.ppermute(squares, 'tp', [(i, i ^ k) for i in range(tp)])]
  transfers between devices with their start and end apart: 0 -> 3, of which waited for: 0 -> 0; matrix products, arithmetic and copies ran while one was open for 0% -> 0% of each run, Pallas kernels for 0% -> 5%
where the time goes in v1:
time: 49.9 us; the launch traced here: 49.6 us
  blocking collectives  32.3 us (65%)
  Pallas kernels  7.59 us (15%)
  starting transfers between devices  5.25 us (11%)
  local copies, waits for them, and re-layouts  3.69 us (7%)
  between operations  0.71 us (1%)
    all_to_all x2, blocking collectives, exchange_sum(): lax.all_to_all(jnp.broadcast_to(v, (members,) + v.shape), axes, 0, 0, til...  32.3 us
    ppermute x3, starting transfers between devices, body(): lax.ppermute(squares, 'tp', [(i, i ^ k) for i in range(tp)])  5.25 us
    unnamed x16, local copies, waits for them, and re-layouts  3.65 us
    pallas_call x1, Pallas kernels, forward(): pl.pallas_call(forward_kernel, out_shape=jax.ShapeDtypeStruct((2 * KEEP,...  2.69 us
    pallas_call x1, Pallas kernels, momentum_left(): pl.pallas_call(momentum_kernel, out_shape=jax.ShapeDtypeStruct((rows, col...  2.5 us
    pallas_call x1, Pallas kernels, updated(): pl.pallas_call(functools.partial(update_kernel, entries), out_shape=jax.S...  2.4 us
  transfers between devices with their start and end apart: 3, of which 0 were waited for; matrix products, arithmetic and copies ran while one was open for 0% of the time, Pallas kernels for 5%

profile of v1, /device:TPU:1, one launch (start us, length us, event | category | flops | bytes accessed | tf_op | source)
XLA Modules:
  0.0 49.6 jit_solution(16928419350799845926)
XLA Ops:
  0.6 0.0 copy-start
  0.6 1.2 %copy-done = bf16[1,128,3456]{2,1,0:T(8,128)(2,1)S(1)} copy-done((bf16[1,128,3456]{2,1,0:T(8,128)(2,1)S(1)}, bf16[1,128,3456]{2,1,0:T(8,128)(2,1)}, u32[]{:S(2)}) %copy-start) | copy-done | bytes 884760
  1.8 0.0 copy-start.2
  1.8 1.2 %copy-done.2 = bf16[1,128,3456]{2,1,0:T(8,128)(2,1)S(1)} copy-done((bf16[1,128,3456]{2,1,0:T(8,128)(2,1)S(1)}, bf16[1,128,3456]{2,1,0:T(8,128)(2,1)}, u32[]{:S(2)}) %copy-start.2) | copy-done | bytes 884760
  3.0 0.0 copy-start.4
  3.0 0.7 %copy-done.4 = s32[8]{0:T(128)S(1)} copy-done((s32[8]{0:T(128)S(1)}, s32[8]{0:T(128)}, u32[]{:S(2)}) %copy-start.4) | copy-done | bytes 56
  3.6 0.0 copy-start.6
  3.6 0.7 %copy-done.6 = s32[8]{0:T(128)S(1)} copy-done((s32[8]{0:T(128)S(1)}, s32[8]{0:T(128)}, u32[]{:S(2)}) %copy-start.6) | copy-done | bytes 56
  4.3 0.0 copy-start.1
  4.3 0.0 copy-start.3
  4.3 0.0 copy-start.5
  4.3 0.0 copy-start.7
  4.3 2.7 %forward.1.c_ref = f32[16,512]{1,0:T(8,128)S(1)} custom-call(s32[8]{0:T(128)S(1)} %copy-done.4, s32[8]{0:T(128)S(1)} %copy-done.6, bf16[128,3456]{1,0:T(8,128)(2,1)S(1)} %bitcast.3, bf16[128,3456]{1,0:T(8,128)(2,1)S(1)} %bitcast.5), custom_call_target="tpu_custom_call" | custom-call | flops 42467328 | bytes 1769472 | tf_op jit(solution)/shard_map/forward/pallas_call | solution.py:139
  7.0 14.9 %all_to_all.10 = f32[8,16,512]{2,1,0:T(8,128)S(1)} all-to-all(f32[8,16,512]{2,1,0:T(8,128)S(1)} %broadcast_in_dim.10), channel_id=1, replica_groups=mesh['z'=8,'y'=4,'x'=2,'tp'=4] {'y','x'}, dimensions={0} | all-to-all | bytes 524288 | tf_op jit(solution)/shard_map/all_to_all | solution.py:179
  22.0 17.4 %all_to_all.11 = f32[8,16,512]{2,1,0:T(8,128)S(1)} all-to-all(f32[8,16,512]{2,1,0:T(8,128)S(1)} %broadcast_in_dim.11), channel_id=1, replica_groups=mesh['z'=8,'y'=4,'x'=2,'tp'=4] {'z'}, dimensions={0} | all-to-all | bytes 524288 | tf_op jit(solution)/shard_map/all_to_all | solution.py:179
  39.5 3.5 %collective-permute-start = (f32[8,128]{1,0:T(8,128)S(1)}, f32[8,128]{1,0:T(8,128)S(1)}, u32[]{:S(2)}, u32[]{:S(2)}) collective-permute-start(f32[8,128]{1,0:T(8,128)S(1)} %slice_add_fusion.1.p0), channel_id=1, source_target_pairs={{0,1},{1,0},{2,3},{3,2},{4,5},{5,4},{6,7},{7,6},{8,9},{9,8},{10,11... | collective-permute-start | bytes 12296 | tf_op jit(solution)/shard_map/ppermute | solution.py:191
  43.0 0.3 collective-permute-start.1
  43.3 1.4 %collective-permute-start.2 = (f32[8,128]{1,0:T(8,128)S(1)}, f32[8,128]{1,0:T(8,128)S(1)}, u32[]{:S(2)}, u32[]{:S(2)}) collective-permute-start(f32[8,128]{1,0:T(8,128)S(1)} %slice_add_fusion.1.p0), channel_id=1, source_target_pairs={{0,3},{1,2},{2,1},{3,0},{4,7},{5,6},{6,5},{7,4},{8,11},{9,10},{10,... | collective-permute-start | bytes 12296 | tf_op jit(solution)/shard_map/ppermute | solution.py:191
  44.7 0.0 copy-done.1
  44.7 0.0 copy-done.3
  44.7 0.0 copy-done.5
  44.7 0.0 copy-done.7
  44.7 2.5 %momentum.1 = bf16[128,3456]{1,0:T(8,128)(2,1)} custom-call(s32[8]{0:T(128)S(1)} %copy-done.5, s32[8]{0:T(128)S(1)} %copy-done.7, bf16[128,3456]{1,0:T(8,128)(2,1)S(1)} %bitcast.4, bf16[128,3456]{1,0:T(8,128)(2,1)S(1)} %bitcast.6, f32[16,512]{1,0:T(8,128)S(1)} %forward.1.c_ref), custom_call_target="tpu_custom_call" | custom-call | flops 42467328 | bytes 2654208 | tf_op jit(solution)/shard_map/momentum/pallas_call | solution.py:153
  47.2 0.0 collective-permute-done.p1
  47.2 0.0 collective-permute-done.1.p2
  47.2 0.0 collective-permute-done.2.p3
  47.2 2.4 %update.1 = f32[128,3456]{1,0:T(8,128)} custom-call(s32[8]{0:T(128)S(1)} %copy-done.5, s32[8]{0:T(128)S(1)} %copy-done.7, f32[16,512]{1,0:T(8,128)S(1)} %reduce_sum.19.total_ref, f32[8,128]{1,0:T(8,128)S(1)} %slice_add_fusion.1.p0, f32[8,128]{1,0:T(8,128)S(1)} %collective-permute-done.p1, f32[8,128]{1,0:T(8,128)S(1)} %collective-permute-done.1.p2, ...), custom_call_target="tpu_custom_call" | custom-call | flops 42467328 | bytes 1769472 | tf_op jit(solution)/shard_map/update/pallas_call | solution.py:166
  (7 shorter events, 0.1 us)
Async XLA Ops:
  0.6 1.2 %copy-start = (bf16[1,128,3456]{2,1,0:T(8,128)(2,1)S(1)}, bf16[1,128,3456]{2,1,0:T(8,128)(2,1)}, u32[]{:S(2)}) copy-start(bf16[1,128,3456]{2,1,0:T(8,128)(2,1)} %param.4) | copy-start | bytes 2654212
  1.8 1.2 %copy-start.2 = (bf16[1,128,3456]{2,1,0:T(8,128)(2,1)S(1)}, bf16[1,128,3456]{2,1,0:T(8,128)(2,1)}, u32[]{:S(2)}) copy-start(bf16[1,128,3456]{2,1,0:T(8,128)(2,1)} %param.5) | copy-start | bytes 2654212
  3.0 0.7 %copy-start.4 = (s32[8]{0:T(128)S(1)}, s32[8]{0:T(128)}, u32[]{:S(2)}) copy-start(s32[8]{0:T(128)} %fr_ref.5) | copy-start | bytes 100
  3.6 0.7 %copy-start.6 = (s32[8]{0:T(128)S(1)}, s32[8]{0:T(128)}, u32[]{:S(2)}) copy-start(s32[8]{0:T(128)} %fc_ref.5) | copy-start | bytes 100
  4.3 40.4 %copy-start.1 = (bf16[1,128,3456]{2,1,0:T(8,128)(2,1)S(1)}, bf16[1,128,3456]{2,1,0:T(8,128)(2,1)}, u32[]{:S(2)}) copy-start(bf16[1,128,3456]{2,1,0:T(8,128)(2,1)} %param.4) | copy-start | bytes 2654212
  4.3 40.4 %copy-start.3 = (bf16[1,128,3456]{2,1,0:T(8,128)(2,1)S(1)}, bf16[1,128,3456]{2,1,0:T(8,128)(2,1)}, u32[]{:S(2)}) copy-start(bf16[1,128,3456]{2,1,0:T(8,128)(2,1)} %param.5) | copy-start | bytes 2654212
  4.3 40.4 %copy-start.5 = (s32[8]{0:T(128)S(1)}, s32[8]{0:T(128)}, u32[]{:S(2)}) copy-start(s32[8]{0:T(128)} %fr_ref.5) | copy-start | bytes 100
  4.3 40.4 %copy-start.7 = (s32[8]{0:T(128)S(1)}, s32[8]{0:T(128)}, u32[]{:S(2)}) copy-start(s32[8]{0:T(128)} %fc_ref.5) | copy-start | bytes 100
  39.5 7.8 %collective-permute-start = (f32[8,128]{1,0:T(8,128)S(1)}, f32[8,128]{1,0:T(8,128)S(1)}, u32[]{:S(2)}, u32[]{:S(2)}) collective-permute-start(f32[8,128]{1,0:T(8,128)S(1)} %slice_add_fusion.1.p0), channel_id=1, source_target_pairs={{0,1},{1,0},{2,3},{3,2},{4,5},{5,4},{6,7},{7,6},{8,9},{9,8},{10,11... | collective-permute-start | bytes 12296 | tf_op jit(solution)/shard_map/ppermute | solution.py:191
  43.0 4.3 %collective-permute-start.1 = (f32[8,128]{1,0:T(8,128)S(1)}, f32[8,128]{1,0:T(8,128)S(1)}, u32[]{:S(2)}, u32[]{:S(2)}) collective-permute-start(f32[8,128]{1,0:T(8,128)S(1)} %slice_add_fusion.1.p0), channel_id=1, source_target_pairs={{0,2},{1,3},{2,0},{3,1},{4,6},{5,7},{6,4},{7,5},{8,10},{9,11},{10,... | collective-permute-start | bytes 12296 | tf_op jit(solution)/shard_map/ppermute | solution.py:191
  43.3 3.9 %collective-permute-start.2 = (f32[8,128]{1,0:T(8,128)S(1)}, f32[8,128]{1,0:T(8,128)S(1)}, u32[]{:S(2)}, u32[]{:S(2)}) collective-permute-start(f32[8,128]{1,0:T(8,128)S(1)} %slice_add_fusion.1.p0), channel_id=1, source_target_pairs={{0,3},{1,2},{2,1},{3,0},{4,7},{5,6},{6,5},{7,4},{8,11},{9,10},{10,... | collective-permute-start | bytes 12296 | tf_op jit(solution)/shard_map/ppermute | solution.py:191

commit v2 on v1

v2 whole, which is shorter than its diff:
```python
import functools
import math

import jax
import jax.numpy as jnp
from jax import lax
from jax.experimental import pallas as pl
from jax.experimental.pallas import tpu as pltpu
from jax.sharding import PartitionSpec as P

BLOCK = 64
KEEP = 8
LANES = 128
SPAN = 1024
VMEM_BYTES = 16 * 1024 * 1024


def spans(cols):
    return [(start, min(SPAN, cols - start)) for start in range(0, cols, SPAN)]


def basis_tile(freq_ref):
    row = lax.broadcasted_iota(jnp.int32, (KEEP, LANES), 0)
    point = lax.broadcasted_iota(jnp.int32, (KEEP, LANES), 1) & (BLOCK - 1)
    freq = jnp.zeros((KEEP, LANES), jnp.int32)
    for k in range(KEEP):
        freq = jnp.where(row == k, freq_ref[k], freq)
    turn = ((2 * point + 1) * freq) & (4 * BLOCK - 1)
    turn = jnp.minimum(turn, 4 * BLOCK - turn)
    x = (BLOCK - turn).astype(jnp.float32) * (math.pi / (2 * BLOCK))
    y = x * x
    series = jnp.full_like(x, 1.0 / math.factorial(13))
    for n in (11, 9, 7, 5, 3, 1):
        series = 1.0 / math.factorial(n) - series * y
    scale = jnp.where(freq == 0, math.sqrt(1.0 / BLOCK), math.sqrt(2.0 / BLOCK))
    return x * series * scale


def split(v):
    high = v.astype(jnp.bfloat16)
    return high, (v - high.astype(jnp.float32)).astype(jnp.bfloat16)


def row_matrix(freq_ref):
    tile = basis_tile(freq_ref)
    lane = lax.broadcasted_iota(jnp.int32, (KEEP, LANES), 1)
    return jnp.concatenate([jnp.where(lane < BLOCK, tile, 0.0), jnp.where(lane >= BLOCK, tile, 0.0)], axis=0)


def col_matrix(freq_ref):
    tile = basis_tile(freq_ref)
    lane = lax.broadcasted_iota(jnp.int32, (KEEP, LANES), 1)
    left = jnp.where(lane < BLOCK, tile, 0.0)
    right = jnp.where(lane >= BLOCK, tile, 0.0)
    pair = jnp.concatenate([left, right], axis=0)
    none = jnp.zeros_like(pair)
    rows = []
    for t in range(SPAN // LANES):
        rows.append(jnp.concatenate([pair if u == t else none for u in range(SPAN // LANES)], axis=1))
    return split(jnp.concatenate(rows, axis=0))


def dot(a, b, dims):
    return lax.dot_general(a, b, (dims, ((), ())), preferred_element_type=jnp.float32)


def packed_rows(cols):
    whole, left = divmod(cols, SPAN)
    assert 0 < left <= SPAN // 2
    return 16 * whole + 8


def pack(spans16):
    last = spans16[-1]
    return jnp.concatenate(spans16[:-1] + [last[:8] + pltpu.roll(last[8:], LANES // 2, 1)], axis=0)


def unpack(rows):
    last = rows[-8:]
    return jnp.concatenate([rows, pltpu.roll(last, LANES // 2, 1)], axis=0)


def forward_kernel(
    fr_ref, fc_ref, m_ref, g_ref, out_ref, row_ref, high_ref, low_ref, both, fr_smem, fc_smem, fsems, sems
):
    cols = m_ref.shape[1]
    freqs = [
        pltpu.make_async_copy(src, dst, fsems.at[k]) for k, (src, dst) in enumerate(((fr_ref, fr_smem), (fc_ref, fc_smem)))
    ]
    for copy in freqs:
        copy.start()
    copies = []
    for n, (start, width) in enumerate(spans(cols)):
        for k, src in enumerate((m_ref, g_ref)):
            copy = pltpu.make_async_copy(
                src.at[:, pl.ds(start, width)], both.at[pl.ds(LANES * k, LANES), pl.ds(start, width)], sems.at[n, k]
            )
            copy.start()
            copies.append(copy)
    for copy in freqs:
        copy.wait()
    rows = row_matrix(fr_smem)
    high, low = split(jnp.concatenate([0.9 * rows, rows], axis=1))
    lhs = jnp.concatenate([high, low], axis=0)
    wide_high, wide_low = col_matrix(fc_smem)
    high_ref[...] = wide_high
    low_ref[...] = wide_low
    high, low = split(rows)
    stack = jnp.concatenate([high, high, low], axis=0).astype(jnp.float32)
    row_ref[...] = jnp.transpose(stack).astype(jnp.bfloat16)
    y_high, y_low = [], []
    for n, (start, width) in enumerate(spans(cols)):
        copies[2 * n].wait()
        copies[2 * n + 1].wait()
        y = dot(lhs, both[:, start : start + width], ((1,), (0,)))
        y = y[:16] + y[16:]
        if width < SPAN:
            y = jnp.concatenate([y, jnp.zeros((16, SPAN - width), jnp.float32)], axis=1)
        high, low = split(y)
        y_high.append(high)
        y_low.append(low)
    count = 16 * len(y_high)
    c = dot(jnp.concatenate(y_high + y_low, axis=0), wide_high, ((1,), (1,)))
    c = c[:count] + c[count:] + dot(jnp.concatenate(y_high, axis=0), wide_low, ((1,), (1,)))
    out_ref[...] = pack([c[k : k + 16] for k in range(0, count, 16)])


def half_image(rows, wide_high, wide_low):
    c = unpack(rows)
    count = c.shape[0]
    high, low = split(c)
    z = dot(jnp.concatenate([high, low], axis=0), wide_high, ((1,), (0,)))
    z = z[:count] + z[count:] + dot(high, wide_low, ((1,), (0,)))
    z_high, z_low = split(z)
    return [
        jnp.concatenate([z_high[k : k + 16], z_low[k : k + 16], z_high[k : k + 16]], axis=0) for k in range(0, count, 16)
    ]


def momentum_kernel(both, c_ref, row_ref, high_ref, low_ref, out_ref, held, sems):
    rows = row_ref[...]
    halves = half_image(c_ref[...], high_ref[...], low_ref[...])
    copies = []
    for n, (start, width) in enumerate(spans(out_ref.shape[1])):
        here = slice(start, start + width)
        image = dot(rows, halves[n][:, :width], ((1,), (0,)))
        fresh = 0.9 * both[:LANES, here].astype(jnp.float32) + both[LANES:, here].astype(jnp.float32)
        held[:, here] = (fresh - image).astype(jnp.bfloat16)
        copy = pltpu.make_async_copy(held.at[:, pl.ds(start, width)], out_ref.at[:, pl.ds(start, width)], sems.at[n])
        copy.start()
        copies.append(copy)
    for copy in copies:
        copy.wait()


def half_kernel(c_ref, high_ref, low_ref, out_ref):
    halves = half_image(c_ref[...], high_ref[...], low_ref[...])
    for n, (start, width) in enumerate(spans(out_ref.shape[1])):
        out_ref[:, start : start + width] = halves[n][:, :width]


def update_kernel(entries, row_ref, half_ref, p0, p1, p2, p3, out_ref, held, sems):
    rows = row_ref[...]
    squares = jnp.sum(p0[...] + p1[...] + p2[...] + p3[...])
    scale = lax.rsqrt(jnp.full((LANES, LANES), squares, jnp.float32) * (1.0 / entries) + 1e-06)
    copies = []
    for n, (start, width) in enumerate(spans(out_ref.shape[1])):
        here = slice(start, start + width)
        image = dot(rows, half_ref[:, here], ((1,), (0,)))
        held[:, here] = image * jnp.concatenate([scale] * (width // LANES), axis=1)
        copy = pltpu.make_async_copy(held.at[:, pl.ds(start, width)], out_ref.at[:, pl.ds(start, width)], sems.at[n])
        copy.start()
        copies.append(copy)
    for copy in copies:
        copy.wait()


VMEM = pl.BlockSpec(memory_space=pltpu.VMEM)
ANY = pl.BlockSpec(memory_space=pl.ANY)
PARAMS = pltpu.CompilerParams(vmem_limit_bytes=VMEM_BYTES)


def hbm(x):
    return pltpu.with_memory_space_constraint(x, pltpu.HBM)


def forward(freq_rows, freq_cols, m, g):
    rows, cols = m.shape
    n = len(spans(cols))
    return pl.pallas_call(
        forward_kernel,
        out_shape=[
            jax.ShapeDtypeStruct((packed_rows(cols), LANES), jnp.float32),
            pltpu.VMEM((rows, 48), jnp.bfloat16),
            pltpu.VMEM((LANES, SPAN), jnp.bfloat16),
            pltpu.VMEM((LANES, SPAN), jnp.bfloat16),
            pltpu.VMEM((2 * rows, cols), jnp.bfloat16),
        ],
        in_specs=[ANY] * 4,
        out_specs=[VMEM] * 5,
        scratch_shapes=[
            pltpu.SMEM((KEEP,), jnp.int32),
            pltpu.SMEM((KEEP,), jnp.int32),
            pltpu.SemaphoreType.DMA((2,)),
            pltpu.SemaphoreType.DMA((n, 2)),
        ],
        compiler_params=PARAMS,
        cost_estimate=pl.CostEstimate(flops=2 * 48 * rows * cols, bytes_accessed=4 * rows * cols, transcendentals=0),
        name="forward",
    )(hbm(freq_rows), hbm(freq_cols), hbm(m), hbm(g))


def momentum_left(both, coeffs, row, high, low):
    rows, cols = both.shape[0] // 2, both.shape[1]
    n = len(spans(cols))
    return pl.pallas_call(
        momentum_kernel,
        out_shape=jax.ShapeDtypeStruct((rows, cols), jnp.bfloat16),
        in_specs=[VMEM] * 5,
        out_specs=ANY,
        scratch_shapes=[pltpu.VMEM((rows, cols), jnp.bfloat16), pltpu.SemaphoreType.DMA((n,))],
        compiler_params=PARAMS,
        cost_estimate=pl.CostEstimate(flops=2 * 48 * rows * cols, bytes_accessed=2 * rows * cols, transcendentals=0),
        name="momentum",
    )(both, coeffs, row, high, low)


def half(total, high, low, cols):
    return pl.pallas_call(
        half_kernel,
        out_shape=pltpu.VMEM((48, cols), jnp.bfloat16),
        in_specs=[VMEM] * 3,
        out_specs=VMEM,
        compiler_params=PARAMS,
        cost_estimate=pl.CostEstimate(flops=2 * 48 * LANES * cols, bytes_accessed=1024, transcendentals=0),
        name="half",
    )(total, high, low)


def updated(row, halves, parts, entries):
    rows, cols = row.shape[0], halves.shape[1]
    n = len(spans(cols))
    return pl.pallas_call(
        functools.partial(update_kernel, entries),
        out_shape=jax.ShapeDtypeStruct((rows, cols), jnp.float32),
        in_specs=[VMEM] * 6,
        out_specs=ANY,
        scratch_shapes=[pltpu.VMEM((rows, cols), jnp.float32), pltpu.SemaphoreType.DMA((n,))],
        compiler_params=PARAMS,
        cost_estimate=pl.CostEstimate(flops=2 * 48 * rows * cols, bytes_accessed=4 * rows * cols, transcendentals=0),
        name="update",
    )(row, halves, *parts)


def moved(v, axis, pairs):
    return lax.ppermute(v, axis, pairs)


def replica_pairs(z, y, x):
    flip = (z * 4 + y) * 2 + x
    return [(r, r ^ flip) for r in range(64)]


def y_ring(step):
    return [(r, r // 8 * 8 + (r % 8 + 2 * step) % 8) for r in range(64)]


def four_way(v, a, b):
    both = tuple(i ^ j for i, j in zip(a, b))
    return (v + moved(v, "rep", replica_pairs(*a))) + (
        moved(v, "rep", replica_pairs(*b)) + moved(v, "rep", replica_pairs(*both))
    )


def body(momentum, grad, freq_rows, freq_cols):
    m, g = momentum[0], grad[0]
    rows, cols = m.shape
    tp = lax.axis_size("tp")
    own, row, high, low, both = forward(freq_rows, freq_cols, m, g)
    total = own + moved(own, "rep", y_ring(1)) + moved(own, "rep", y_ring(3)) + moved(own, "rep", y_ring(2))
    total = four_way(total, (1, 0, 0), (2, 0, 0))
    total = total + moved(total, "rep", replica_pairs(6, 0, 0))
    total = total + moved(total, "rep", replica_pairs(0, 0, 1))
    squares = total * total
    squares = sum(squares[k : k + KEEP] for k in range(0, total.shape[0], KEEP))
    parts = [squares] + [moved(squares, "tp", [(i, i ^ k) for i in range(tp)]) for k in range(1, tp)]
    kept = momentum_left(both, own, row, high, low)
    update = updated(row, half(total, high, low, cols), parts, float(rows * cols * tp))
    return kept[None], update


def solution(mesh):
    placed = (P("rep", None, "tp"), P("rep", None, "tp"), P(), P())
    return jax.shard_map(
        body,
        mesh=mesh,
        in_specs=placed,
        out_specs=(P("rep", None, "tp"), P(None, "tp")),
        check_vma=False,
    )
```

time: 49.9 us -> 40.2 us (0.81)
  blocking collectives: 32.3 us -> 0 us
  starting transfers between devices: 5.25 us -> 23.8 us
  waiting for transfers between devices: 0.01 us -> 9.93 us
  local copies, waits for them, and re-layouts: 3.69 us -> 0 us
  Pallas kernels: 7.59 us -> 5.59 us
    all_to_all x2 -> x0, blocking collectives: 32.3 us -> none  [exchange_sum(): lax.all_to_all(jnp.broadcast_to(v, (members,) + v.shape), axes, 0, 0, til...]
    ppermute x3 -> x11, starting transfers between devices: 5.25 us -> 23.8 us  [moved(): return lax.ppermute(v, axis, pairs)]
    ppermute x3 -> x11, waiting for transfers between devices: 0.01 us -> 9.93 us  [moved(): return lax.ppermute(v, axis, pairs)]
    unnamed x16 -> x0, local copies, waits for them, and re-layouts: 3.65 us -> none
    pallas_call x1, Pallas kernels: 2.5 us -> 1.44 us  [momentum_left(): pl.pallas_call(momentum_kernel, out_shape=jax.ShapeDtypeStruct((rows, col...]
    pallas_call x1, Pallas kernels: 2.4 us -> 1.45 us  [updated(): pl.pallas_call(functools.partial(update_kernel, entries), out_shape=jax.S...]
    pallas_call x1 -> x2, Pallas kernels: 2.69 us -> 2.7 us  [the longest x1 2.41 us: forward(): pl.pallas_call(forward_kernel, out_shape=[jax.ShapeDtypeStruct((packed_ro...]
  transfers between devices with their start and end apart: 3 -> 11, of which waited for: 0 -> 7; matrix products, arithmetic and copies ran while one was open for 0% -> 0% of each run, Pallas kernels for 5% -> 4%
where the time goes in v2:
time: 40.2 us; the launch traced here: 40.1 us
  starting transfers between devices  23.8 us (59%)
  waiting for transfers between devices  9.93 us (25%)
  Pallas kernels  5.59 us (14%)
  between operations  0.67 us (2%)
    ppermute x11, starting transfers between devices, moved(): return lax.ppermute(v, axis, pairs)  23.8 us
    ppermute x11, waiting for transfers between devices, moved(): return lax.ppermute(v, axis, pairs)  9.93 us
    pallas_call x1, Pallas kernels, forward(): pl.pallas_call(forward_kernel, out_shape=[jax.ShapeDtypeStruct((packed_ro...  2.41 us
    pallas_call x1, Pallas kernels, updated(): pl.pallas_call(functools.partial(update_kernel, entries), out_shape=jax.S...  1.45 us
    pallas_call x1, Pallas kernels, momentum_left(): pl.pallas_call(momentum_kernel, out_shape=jax.ShapeDtypeStruct((rows, col...  1.44 us
  transfers between devices with their start and end apart: 11, of which 7 were waited for; matrix products, arithmetic and copies ran while one was open for 0% of the time, Pallas kernels for 4%

profile of v2, /device:TPU:1, one launch (start us, length us, event | category | flops | bytes accessed | tf_op | source)
XLA Modules:
  0.0 40.1 jit_solution(3155169175190844033)
XLA Ops:
  0.6 2.4 %forward.1 = (f32[56,128]{1,0:T(8,128)S(1)}, bf16[128,48]{1,0:T(8,128)(2,1)S(1)}, bf16[128,1024]{1,0:T(8,128)(2,1)S(1)}, bf16[128,1024]{1,0:T(8,128)(2,1)S(1)}, bf16[256,3456]{1,0:T(8,128)(2,1)S(1)}) custom-call(s32[8]{0:T(128)} %fr_ref.1, s32[8]{0:T(128)} %fc_ref.1, bf16[128,3456]{1,0:T(8,128)(2,1)} %bitcast.3, bf16[128,3456]{1,0:T(8,128)(2,1)} %bitcast.4), custom_call_target="tpu_custom_call" | custom-call | flops 42467328 | bytes 1769472 | tf_op jit(solution)/shard_map/forward/pallas_call | solution.py:190
  3.1 3.8 %collective-permute-start.2 = (f32[56,128]{1,0:T(8,128)S(1)}, f32[56,128]{1,0:T(8,128)S(1)}, u32[]{:S(2)}, u32[]{:S(2)}) collective-permute-start(f32[56,128]{1,0:T(8,128)S(1)} %get-tuple-element.8.c_ref), channel_id=1, source_target_pairs={{0,16},{4,20},{8,24},{12,28},{16,0},{20,4},{24,8},{28,12},{32,48},... | collective-permute-start | bytes 86024 | tf_op jit(solution)/shard_map/ppermute | solution.py:256
  6.9 0.8 %collective-permute-start.1 = (f32[56,128]{1,0:T(8,128)S(1)}, f32[56,128]{1,0:T(8,128)S(1)}, u32[]{:S(2)}, u32[]{:S(2)}) collective-permute-start(f32[56,128]{1,0:T(8,128)S(1)} %get-tuple-element.8.c_ref), channel_id=1, source_target_pairs={{0,24},{4,28},{8,0},{12,4},{16,8},{20,12},{24,16},{28,20},{32,56},... | collective-permute-start | bytes 86024 | tf_op jit(solution)/shard_map/ppermute | solution.py:256
  7.7 0.7 %collective-permute-start = (f32[56,128]{1,0:T(8,128)S(1)}, f32[56,128]{1,0:T(8,128)S(1)}, u32[]{:S(2)}, u32[]{:S(2)}) collective-permute-start(f32[56,128]{1,0:T(8,128)S(1)} %get-tuple-element.8.c_ref), channel_id=1, source_target_pairs={{0,8},{4,12},{8,16},{12,20},{16,24},{20,28},{24,0},{28,4},{32,40},... | collective-permute-start | bytes 86024 | tf_op jit(solution)/shard_map/ppermute | solution.py:256
  8.3 0.0 collective-permute-done.2
  8.4 1.5 %collective-permute-done.1 = f32[56,128]{1,0:T(8,128)S(1)} collective-permute-done((f32[56,128]{1,0:T(8,128)S(1)}, f32[56,128]{1,0:T(8,128)S(1)}, u32[]{:S(2)}, u32[]{:S(2)}) %collective-permute-start.1) | collective-permute-done | bytes 28704 | tf_op jit(solution)/shard_map/ppermute | solution.py:256
  9.8 1.7 %collective-permute-done = f32[56,128]{1,0:T(8,128)S(1)} collective-permute-done((f32[56,128]{1,0:T(8,128)S(1)}, f32[56,128]{1,0:T(8,128)S(1)}, u32[]{:S(2)}, u32[]{:S(2)}) %collective-permute-start) | collective-permute-done | bytes 28704 | tf_op jit(solution)/shard_map/ppermute | solution.py:256
  11.6 4.4 %collective-permute-start.5 = (f32[56,128]{1,0:T(8,128)S(1)}, f32[56,128]{1,0:T(8,128)S(1)}, u32[]{:S(2)}, u32[]{:S(2)}) collective-permute-start(f32[56,128]{1,0:T(8,128)S(1)} %add_add_fusion.1), channel_id=1, source_target_pairs={{0,96},{4,100},{8,104},{12,108},{16,112},{20,116},{24,120},{28,124... | collective-permute-start | bytes 86024 | tf_op jit(solution)/shard_map/ppermute | solution.py:256
  16.0 0.0 collective-permute-start.4
  16.0 0.4 collective-permute-start.3
  16.4 0.9 %collective-permute-done.5 = f32[56,128]{1,0:T(8,128)S(1)} collective-permute-done((f32[56,128]{1,0:T(8,128)S(1)}, f32[56,128]{1,0:T(8,128)S(1)}, u32[]{:S(2)}, u32[]{:S(2)}) %collective-permute-start.5) | collective-permute-done | bytes 28704 | tf_op jit(solution)/shard_map/ppermute | solution.py:256
  17.3 2.7 %collective-permute-done.4 = f32[56,128]{1,0:T(8,128)S(1)} collective-permute-done((f32[56,128]{1,0:T(8,128)S(1)}, f32[56,128]{1,0:T(8,128)S(1)}, u32[]{:S(2)}, u32[]{:S(2)}) %collective-permute-start.4) | collective-permute-done | bytes 28704 | tf_op jit(solution)/shard_map/ppermute | solution.py:256
  20.0 0.0 collective-permute-done.3
  20.0 3.7 %collective-permute-start.6 = (f32[56,128]{1,0:T(8,128)S(1)}, f32[56,128]{1,0:T(8,128)S(1)}, u32[]{:S(2)}, u32[]{:S(2)}) collective-permute-start(f32[56,128]{1,0:T(8,128)S(1)} %add_add_fusion), channel_id=1, source_target_pairs={{0,192},{4,196},{8,200},{12,204},{16,208},{20,212},{24,216},{28,22... | collective-permute-start | bytes 86024 | tf_op jit(solution)/shard_map/ppermute | solution.py:256
  23.6 1.5 %collective-permute-done.6 = f32[56,128]{1,0:T(8,128)S(1)} collective-permute-done((f32[56,128]{1,0:T(8,128)S(1)}, f32[56,128]{1,0:T(8,128)S(1)}, u32[]{:S(2)}, u32[]{:S(2)}) %collective-permute-start.6) | collective-permute-done | bytes 28704 | tf_op jit(solution)/shard_map/ppermute | solution.py:256
  25.1 2.8 %collective-permute-start.7 = (f32[56,128]{1,0:T(8,128)S(1)}, f32[56,128]{1,0:T(8,128)S(1)}, u32[]{:S(2)}, u32[]{:S(2)}) collective-permute-start(f32[56,128]{1,0:T(8,128)S(1)} %add.48), channel_id=1, source_target_pairs={{0,4},{4,0},{8,12},{12,8},{16,20},{20,16},{24,28},{28,24},{32,36},... | collective-permute-start | bytes 86024 | tf_op jit(solution)/shard_map/ppermute | solution.py:256
  27.9 1.4 %momentum.1 = bf16[128,3456]{1,0:T(8,128)(2,1)} custom-call(bf16[256,3456]{1,0:T(8,128)(2,1)S(1)} %get-tuple-element.7.both, f32[56,128]{1,0:T(8,128)S(1)} %get-tuple-element.8.c_ref, bf16[128,48]{1,0:T(8,128)(2,1)S(1)} %get-tuple-element.9.row_ref, bf16[128,1024]{1,0:T(8,128)(2,1)S(1)} %get-tuple-element.10.high_ref, ...), custom_call_target="tpu_custom_call" | custom-call | flops 42467328 | bytes 884736 | tf_op jit(solution)/shard_map/momentum/pallas_call | solution.py:216
  29.3 0.0 collective-permute-done.7
  29.3 6.8 %collective-permute-start.10 = (f32[8,128]{1,0:T(8,128)S(1)}, f32[8,128]{1,0:T(8,128)S(1)}, u32[]{:S(2)}, u32[]{:S(2)}) collective-permute-start(f32[8,128]{1,0:T(8,128)S(1)} %slice_add_fusion.p0), channel_id=1, source_target_pairs={{0,3},{1,2},{2,1},{3,0},{4,7},{5,6},{6,5},{7,4},{8,11},{9,10},{10,... | collective-permute-start | bytes 12296 | tf_op jit(solution)/shard_map/ppermute | solution.py:256
  36.2 0.3 collective-permute-start.9
  36.4 0.2 collective-permute-start.8
  36.7 0.3 half.1.half_ref
  36.9 0.8 %collective-permute-done.10.p3 = f32[8,128]{1,0:T(8,128)S(1)} collective-permute-done((f32[8,128]{1,0:T(8,128)S(1)}, f32[8,128]{1,0:T(8,128)S(1)}, u32[]{:S(2)}, u32[]{:S(2)}) %collective-permute-start.10) | collective-permute-done | bytes 4128 | tf_op jit(solution)/shard_map/ppermute | solution.py:256
  37.7 0.9 %collective-permute-done.9.p2 = f32[8,128]{1,0:T(8,128)S(1)} collective-permute-done((f32[8,128]{1,0:T(8,128)S(1)}, f32[8,128]{1,0:T(8,128)S(1)}, u32[]{:S(2)}, u32[]{:S(2)}) %collective-permute-start.9) | collective-permute-done | bytes 4128 | tf_op jit(solution)/shard_map/ppermute | solution.py:256
  38.6 0.0 collective-permute-done.8.p1
  38.6 1.5 %update.1 = f32[128,3456]{1,0:T(8,128)} custom-call(bf16[128,48]{1,0:T(8,128)(2,1)S(1)} %get-tuple-element.9.row_ref, bf16[48,3456]{1,0:T(8,128)(2,1)S(1)} %half.1.half_ref, f32[8,128]{1,0:T(8,128)S(1)} %slice_add_fusion.p0, f32[8,128]{1,0:T(8,128)S(1)} %collective-permute-done.8.p1, f32[8,128]{1,0:T(8,128)S(1)} %collective-permute-done.9.p2, ...), custom_call_target="tpu_custom_call" | custom-call | flops 42467328 | bytes 1769472 | tf_op jit(solution)/shard_map/update/pallas_call | solution.py:243
  (5 shorter events, 0.0 us)
Async XLA Ops:
  3.1 5.3 %collective-permute-start.2 = (f32[56,128]{1,0:T(8,128)S(1)}, f32[56,128]{1,0:T(8,128)S(1)}, u32[]{:S(2)}, u32[]{:S(2)}) collective-permute-start(f32[56,128]{1,0:T(8,128)S(1)} %get-tuple-element.8.c_ref), channel_id=1, source_target_pairs={{0,16},{4,20},{8,24},{12,28},{16,0},{20,4},{24,8},{28,12},{32,48},... | collective-permute-start | bytes 86024 | tf_op jit(solution)/shard_map/ppermute | solution.py:256
  6.9 3.0 %collective-permute-start.1 = (f32[56,128]{1,0:T(8,128)S(1)}, f32[56,128]{1,0:T(8,128)S(1)}, u32[]{:S(2)}, u32[]{:S(2)}) collective-permute-start(f32[56,128]{1,0:T(8,128)S(1)} %get-tuple-element.8.c_ref), channel_id=1, source_target_pairs={{0,24},{4,28},{8,0},{12,4},{16,8},{20,12},{24,16},{28,20},{32,56},... | collective-permute-start | bytes 86024 | tf_op jit(solution)/shard_map/ppermute | solution.py:256
  7.7 3.9 %collective-permute-start = (f32[56,128]{1,0:T(8,128)S(1)}, f32[56,128]{1,0:T(8,128)S(1)}, u32[]{:S(2)}, u32[]{:S(2)}) collective-permute-start(f32[56,128]{1,0:T(8,128)S(1)} %get-tuple-element.8.c_ref), channel_id=1, source_target_pairs={{0,8},{4,12},{8,16},{12,20},{16,24},{20,28},{24,0},{28,4},{32,40},... | collective-permute-start | bytes 86024 | tf_op jit(solution)/shard_map/ppermute | solution.py:256
  11.6 5.7 %collective-permute-start.5 = (f32[56,128]{1,0:T(8,128)S(1)}, f32[56,128]{1,0:T(8,128)S(1)}, u32[]{:S(2)}, u32[]{:S(2)}) collective-permute-start(f32[56,128]{1,0:T(8,128)S(1)} %add_add_fusion.1), channel_id=1, source_target_pairs={{0,96},{4,100},{8,104},{12,108},{16,112},{20,116},{24,120},{28,124... | collective-permute-start | bytes 86024 | tf_op jit(solution)/shard_map/ppermute | solution.py:256
  16.0 3.9 %collective-permute-start.4 = (f32[56,128]{1,0:T(8,128)S(1)}, f32[56,128]{1,0:T(8,128)S(1)}, u32[]{:S(2)}, u32[]{:S(2)}) collective-permute-start(f32[56,128]{1,0:T(8,128)S(1)} %add_add_fusion.1), channel_id=1, source_target_pairs={{0,64},{4,68},{8,72},{12,76},{16,80},{20,84},{24,88},{28,92},{32,9... | collective-permute-start | bytes 86024 | tf_op jit(solution)/shard_map/ppermute | solution.py:256
  16.0 3.9 %collective-permute-start.3 = (f32[56,128]{1,0:T(8,128)S(1)}, f32[56,128]{1,0:T(8,128)S(1)}, u32[]{:S(2)}, u32[]{:S(2)}) collective-permute-start(f32[56,128]{1,0:T(8,128)S(1)} %add_add_fusion.1), channel_id=1, source_target_pairs={{0,32},{4,36},{8,40},{12,44},{16,48},{20,52},{24,56},{28,60},{32,0... | collective-permute-start | bytes 86024 | tf_op jit(solution)/shard_map/ppermute | solution.py:256
  20.0 5.1 %collective-permute-start.6 = (f32[56,128]{1,0:T(8,128)S(1)}, f32[56,128]{1,0:T(8,128)S(1)}, u32[]{:S(2)}, u32[]{:S(2)}) collective-permute-start(f32[56,128]{1,0:T(8,128)S(1)} %add_add_fusion), channel_id=1, source_target_pairs={{0,192},{4,196},{8,200},{12,204},{16,208},{20,212},{24,216},{28,22... | collective-permute-start | bytes 86024 | tf_op jit(solution)/shard_map/ppermute | solution.py:256
  25.1 4.2 %collective-permute-start.7 = (f32[56,128]{1,0:T(8,128)S(1)}, f32[56,128]{1,0:T(8,128)S(1)}, u32[]{:S(2)}, u32[]{:S(2)}) collective-permute-start(f32[56,128]{1,0:T(8,128)S(1)} %add.48), channel_id=1, source_target_pairs={{0,4},{4,0},{8,12},{12,8},{16,20},{20,16},{24,28},{28,24},{32,36},... | collective-permute-start | bytes 86024 | tf_op jit(solution)/shard_map/ppermute | solution.py:256
  29.3 8.3 %collective-permute-start.10 = (f32[8,128]{1,0:T(8,128)S(1)}, f32[8,128]{1,0:T(8,128)S(1)}, u32[]{:S(2)}, u32[]{:S(2)}) collective-permute-start(f32[8,128]{1,0:T(8,128)S(1)} %slice_add_fusion.p0), channel_id=1, source_target_pairs={{0,3},{1,2},{2,1},{3,0},{4,7},{5,6},{6,5},{7,4},{8,11},{9,10},{10,... | collective-permute-start | bytes 12296 | tf_op jit(solution)/shard_map/ppermute | solution.py:256
  36.2 2.5 %collective-permute-start.9 = (f32[8,128]{1,0:T(8,128)S(1)}, f32[8,128]{1,0:T(8,128)S(1)}, u32[]{:S(2)}, u32[]{:S(2)}) collective-permute-start(f32[8,128]{1,0:T(8,128)S(1)} %slice_add_fusion.p0), channel_id=1, source_target_pairs={{0,2},{1,3},{2,0},{3,1},{4,6},{5,7},{6,4},{7,5},{8,10},{9,11},{10,... | collective-permute-start | bytes 12296 | tf_op jit(solution)/shard_map/ppermute | solution.py:256
  36.4 2.2 %collective-permute-start.8 = (f32[8,128]{1,0:T(8,128)S(1)}, f32[8,128]{1,0:T(8,128)S(1)}, u32[]{:S(2)}, u32[]{:S(2)}) collective-permute-start(f32[8,128]{1,0:T(8,128)S(1)} %slice_add_fusion.p0), channel_id=1, source_target_pairs={{0,1},{1,0},{2,3},{3,2},{4,5},{5,4},{6,7},{7,6},{8,9},{9,8},{10,11... | collective-permute-start | bytes 12296 | tf_op jit(solution)/shard_map/ppermute | solution.py:256

commit v3 on v2

--- a/solution.py
+++ b/solution.py
@@ -159,9 +159,9 @@
         out_ref[:, start : start + width] = halves[n][:, :width]
 
 
-def update_kernel(entries, row_ref, half_ref, p0, p1, p2, p3, out_ref, held, sems):
+def update_kernel(entries, row_ref, half_ref, squares_ref, out_ref, held, sems):
     rows = row_ref[...]
-    squares = jnp.sum(p0[...] + p1[...] + p2[...] + p3[...])
+    squares = jnp.sum(squares_ref[...])
     scale = lax.rsqrt(jnp.full((LANES, LANES), squares, jnp.float32) * (1.0 / entries) + 1e-06)
     copies = []
     for n, (start, width) in enumerate(spans(out_ref.shape[1])):
@@ -237,55 +237,75 @@
     )(total, high, low)
 
 
-def updated(row, halves, parts, entries):
+def updated(row, halves, squares, entries):
     rows, cols = row.shape[0], halves.shape[1]
     n = len(spans(cols))
     return pl.pallas_call(
         functools.partial(update_kernel, entries),
         out_shape=jax.ShapeDtypeStruct((rows, cols), jnp.float32),
-        in_specs=[VMEM] * 6,
+        in_specs=[VMEM] * 3,
         out_specs=ANY,
         scratch_shapes=[pltpu.VMEM((rows, cols), jnp.float32), pltpu.SemaphoreType.DMA((n,))],
         compiler_params=PARAMS,
         cost_estimate=pl.CostEstimate(flops=2 * 48 * rows * cols, bytes_accessed=4 * rows * cols, transcendentals=0),
         name="update",
-    )(row, halves, *parts)
-
-
-def moved(v, axis, pairs):
-    return lax.ppermute(v, axis, pairs)
-
-
-def replica_pairs(z, y, x):
-    flip = (z * 4 + y) * 2 + x
-    return [(r, r ^ flip) for r in range(64)]
-
-
-def y_ring(step):
-    return [(r, r // 8 * 8 + (r % 8 + 2 * step) % 8) for r in range(64)]
+    )(row, halves, squares)
+
+
+def moved(v, partner):
+    pairs = []
+    for d in range(256):
+        z, y, x, near, core = d // 32, d // 8 % 4, d // 4 % 2, d // 2 % 2, d % 2
+        z, y, x, near, core = partner(z, y, x, near, core)
+        pairs.append((d, (((z * 4 + y) * 2 + x) * 2 + near) * 2 + core))
+    return lax.ppermute(v, ("rep", "tp"), pairs)
+
+
+def replica(dz, dy, dx):
+    def partner(z, y, x, near, core):
+        if core == 0:
+            return (z ^ 1, y, x, near, core) if dy else (z, y ^ 1, x, near, core)
+        return z ^ dz, y ^ dy, x ^ dx, near, core
+
+    return partner
+
+
+def other_core(z, y, x, near, core):
+    return z, y, x, near, 1 - core
+
+
+def next_chip(z, y, x, near, core):
+    return z, y, x, 1 - near, core
 
 
 def four_way(v, a, b):
     both = tuple(i ^ j for i, j in zip(a, b))
-    return (v + moved(v, "rep", replica_pairs(*a))) + (
-        moved(v, "rep", replica_pairs(*b)) + moved(v, "rep", replica_pairs(*both))
-    )
+    return (v + moved(v, replica(*a))) + (moved(v, replica(*b)) + moved(v, replica(*both)))
 
 
 def body(momentum, grad, freq_rows, freq_cols):
     m, g = momentum[0], grad[0]
     rows, cols = m.shape
     tp = lax.axis_size("tp")
+    core = lax.axis_index("tp") % 2
     own, row, high, low, both = forward(freq_rows, freq_cols, m, g)
-    total = own + moved(own, "rep", y_ring(1)) + moved(own, "rep", y_ring(3)) + moved(own, "rep", y_ring(2))
-    total = four_way(total, (1, 0, 0), (2, 0, 0))
-    total = total + moved(total, "rep", replica_pairs(6, 0, 0))
-    total = total + moved(total, "rep", replica_pairs(0, 0, 1))
-    squares = total * total
-    squares = sum(squares[k : k + KEEP] for k in range(0, total.shape[0], KEEP))
-    parts = [squares] + [moved(squares, "tp", [(i, i ^ k) for i in range(tp)]) for k in range(1, tp)]
+    count = own.shape[0]
+    other = moved(own, other_core)
+    pair = jnp.concatenate([jnp.where(core == 1, other, own), jnp.where(core == 1, own, other)], axis=0)
+    pair = four_way(pair, (0, 1, 0), (0, 2, 0))
+    pair = four_way(pair, (1, 0, 0), (3, 0, 0))
+    pair = pair + moved(pair, replica(6, 0, 0))
     kept = momentum_left(both, own, row, high, low)
-    update = updated(row, half(total, high, low, cols), parts, float(rows * cols * tp))
+    other, kept = lax.optimization_barrier((moved(pair, replica(0, 0, 1)), kept))
+    pair = pair + other
+    squares = pair * pair
+    squares = sum(squares[k : k + KEEP] for k in range(0, 2 * count, KEEP))
+    squares = squares + moved(squares, next_chip)
+    sent = jnp.concatenate([pair[:count], squares], axis=0)
+    sent = jnp.where(core == 1, jnp.concatenate([pair[count:], squares], axis=0), moved(sent, other_core))
+    halves = half(sent[:count], high, low, cols)
+    squares = sent[count:]
+    update = updated(row, halves, squares, float(rows * cols * tp))
     return kept[None], update
 
 

time: 40.2 us -> 36.7 us (0.913)
  starting transfers between devices: 23.8 us -> 18.7 us
  waiting for transfers between devices: 9.93 us -> 11.5 us
    ppermute x11, starting transfers between devices: 23.8 us -> 18.7 us  [moved(): return lax.ppermute(v, ('rep', 'tp'), pairs)]
    ppermute x11, waiting for transfers between devices: 9.93 us -> 11.5 us  [moved(): return lax.ppermute(v, ('rep', 'tp'), pairs)]
  transfers between devices with their start and end apart: 11 -> 11, of which waited for: 7 -> 9; matrix products, arithmetic and copies ran while one was open for 0% -> 0% of each run, Pallas kernels for 4% -> 4%
where the time goes in v3:
time: 36.7 us; the launch traced here: 36.6 us
  starting transfers between devices  18.7 us (51%)
  waiting for transfers between devices  11.5 us (31%)
  Pallas kernels  5.58 us (15%)
  between operations  0.7 us (2%)
    ppermute x11, starting transfers between devices, moved(): return lax.ppermute(v, ('rep', 'tp'), pairs)  18.7 us
    ppermute x11, waiting for transfers between devices, moved(): return lax.ppermute(v, ('rep', 'tp'), pairs)  11.5 us
    pallas_call x1, Pallas kernels, forward(): pl.pallas_call(forward_kernel, out_shape=[jax.ShapeDtypeStruct((packed_ro...  2.41 us
    pallas_call x1, Pallas kernels, updated(): pl.pallas_call(functools.partial(update_kernel, entries), out_shape=jax.S...  1.46 us
    pallas_call x1, Pallas kernels, momentum_left(): pl.pallas_call(momentum_kernel, out_shape=jax.ShapeDtypeStruct((rows, col...  1.43 us
  transfers between devices with their start and end apart: 11, of which 9 were waited for; matrix products, arithmetic and copies ran while one was open for 0% of the time, Pallas kernels for 4%

profile of v3, /device:TPU:1, one launch (start us, length us, event | category | flops | bytes accessed | tf_op | source)
XLA Modules:
  0.0 36.6 jit_solution(11145692774101303376)
XLA Ops:
  0.6 2.4 %forward.1 = (f32[56,128]{1,0:T(8,128)S(1)}, bf16[128,48]{1,0:T(8,128)(2,1)S(1)}, bf16[128,1024]{1,0:T(8,128)(2,1)S(1)}, bf16[128,1024]{1,0:T(8,128)(2,1)S(1)}, bf16[256,3456]{1,0:T(8,128)(2,1)S(1)}) custom-call(s32[8]{0:T(128)} %fr_ref.1, s32[8]{0:T(128)} %fc_ref.1, bf16[128,3456]{1,0:T(8,128)(2,1)} %bitcast.3, bf16[128,3456]{1,0:T(8,128)(2,1)} %bitcast.4), custom_call_target="tpu_custom_call" | custom-call | flops 42467328 | bytes 1769472 | tf_op jit(solution)/shard_map/forward/pallas_call | solution.py:190
  3.0 3.3 %collective-permute-start = (f32[56,128]{1,0:T(8,128)S(1)}, f32[56,128]{1,0:T(8,128)S(1)}, u32[]{:S(2)}, u32[]{:S(2)}) collective-permute-start(f32[56,128]{1,0:T(8,128)S(1)} %get-tuple-element.9.c_ref), channel_id=1, source_target_pairs={{0,1},{1,0},{2,3},{3,2},{4,5},{5,4},{6,7},{7,6},{8,9},{9,8},{10,11... | collective-permute-start | bytes 86024 | tf_op jit(solution)/shard_map/ppermute | solution.py:261
  6.4 0.9 %collective-permute-done = f32[56,128]{1,0:T(8,128)S(1)} collective-permute-done((f32[56,128]{1,0:T(8,128)S(1)}, f32[56,128]{1,0:T(8,128)S(1)}, u32[]{:S(2)}, u32[]{:S(2)}) %collective-permute-start) | collective-permute-done | bytes 28704 | tf_op jit(solution)/shard_map/ppermute | solution.py:261
  7.2 1.3 %collective-permute-start.2 = (f32[112,128]{1,0:T(8,128)S(1)}, f32[112,128]{1,0:T(8,128)S(1)}, u32[]{:S(2)}, u32[]{:S(2)}) collective-permute-start(f32[112,128]{1,0:T(8,128)S(1)} %pad_maximum_fusion), channel_id=1, source_target_pairs={{0,32},{1,17},{2,34},{3,19},{4,36},{5,21},{6,38},{7,23},{8,40},{9,... | collective-permute-start | bytes 172040 | tf_op jit(solution)/shard_map/ppermute | solution.py:261
  8.5 0.8 %collective-permute-start.3 = (f32[112,128]{1,0:T(8,128)S(1)}, f32[112,128]{1,0:T(8,128)S(1)}, u32[]{:S(2)}, u32[]{:S(2)}) collective-permute-start(f32[112,128]{1,0:T(8,128)S(1)} %pad_maximum_fusion), channel_id=1, source_target_pairs={{0,32},{1,25},{2,34},{3,27},{4,36},{5,29},{6,38},{7,31},{8,40},{9,... | collective-permute-start | bytes 172040 | tf_op jit(solution)/shard_map/ppermute | solution.py:261
  9.3 0.7 %collective-permute-start.1 = (f32[112,128]{1,0:T(8,128)S(1)}, f32[112,128]{1,0:T(8,128)S(1)}, u32[]{:S(2)}, u32[]{:S(2)}) collective-permute-start(f32[112,128]{1,0:T(8,128)S(1)} %pad_maximum_fusion), channel_id=1, source_target_pairs={{0,32},{1,9},{2,34},{3,11},{4,36},{5,13},{6,38},{7,15},{8,40},{9,1... | collective-permute-start | bytes 172040 | tf_op jit(solution)/shard_map/ppermute | solution.py:261
  10.0 1.9 %collective-permute-done.2 = f32[112,128]{1,0:T(8,128)S(1)} collective-permute-done((f32[112,128]{1,0:T(8,128)S(1)}, f32[112,128]{1,0:T(8,128)S(1)}, u32[]{:S(2)}, u32[]{:S(2)}) %collective-permute-start.2) | collective-permute-done | bytes 57376 | tf_op jit(solution)/shard_map/ppermute | solution.py:261
  11.9 0.9 %collective-permute-done.3 = f32[112,128]{1,0:T(8,128)S(1)} collective-permute-done((f32[112,128]{1,0:T(8,128)S(1)}, f32[112,128]{1,0:T(8,128)S(1)}, u32[]{:S(2)}, u32[]{:S(2)}) %collective-permute-start.3) | collective-permute-done | bytes 57376 | tf_op jit(solution)/shard_map/ppermute | solution.py:261
  12.8 0.0 collective-permute-done.1
  12.8 3.1 %collective-permute-start.6 = (f32[112,128]{1,0:T(8,128)S(1)}, f32[112,128]{1,0:T(8,128)S(1)}, u32[]{:S(2)}, u32[]{:S(2)}) collective-permute-start(f32[112,128]{1,0:T(8,128)S(1)} %add_add_fusion.1), channel_id=1, source_target_pairs={{0,8},{1,65},{2,10},{3,67},{4,12},{5,69},{6,14},{7,71},{8,0},{9,73... | collective-permute-start | bytes 172040 | tf_op jit(solution)/shard_map/ppermute | solution.py:261
  15.9 1.4 %collective-permute-start.5 = (f32[112,128]{1,0:T(8,128)S(1)}, f32[112,128]{1,0:T(8,128)S(1)}, u32[]{:S(2)}, u32[]{:S(2)}) collective-permute-start(f32[112,128]{1,0:T(8,128)S(1)} %add_add_fusion.1), channel_id=1, source_target_pairs={{0,8},{1,97},{2,10},{3,99},{4,12},{5,101},{6,14},{7,103},{8,0},{9,... | collective-permute-start | bytes 172040 | tf_op jit(solution)/shard_map/ppermute | solution.py:261
  17.3 0.2 collective-permute-start.4
  17.5 0.0 collective-permute-done.6
  17.5 3.3 %collective-permute-done.5 = f32[112,128]{1,0:T(8,128)S(1)} collective-permute-done((f32[112,128]{1,0:T(8,128)S(1)}, f32[112,128]{1,0:T(8,128)S(1)}, u32[]{:S(2)}, u32[]{:S(2)}) %collective-permute-start.5) | collective-permute-done | bytes 57376 | tf_op jit(solution)/shard_map/ppermute | solution.py:261
  20.8 0.1 collective-permute-done.4
  21.0 3.7 %collective-permute-start.7 = (f32[112,128]{1,0:T(8,128)S(1)}, f32[112,128]{1,0:T(8,128)S(1)}, u32[]{:S(2)}, u32[]{:S(2)}) collective-permute-start(f32[112,128]{1,0:T(8,128)S(1)} %add_add_fusion), channel_id=1, source_target_pairs={{0,8},{1,193},{2,10},{3,195},{4,12},{5,197},{6,14},{7,199},{8,0},{... | collective-permute-start | bytes 172040 | tf_op jit(solution)/shard_map/ppermute | solution.py:261
  24.7 1.6 %collective-permute-done.7 = f32[112,128]{1,0:T(8,128)S(1)} collective-permute-done((f32[112,128]{1,0:T(8,128)S(1)}, f32[112,128]{1,0:T(8,128)S(1)}, u32[]{:S(2)}, u32[]{:S(2)}) %collective-permute-start.7) | collective-permute-done | bytes 57376 | tf_op jit(solution)/shard_map/ppermute | solution.py:261
  26.3 2.8 %collective-permute-start.8 = (f32[112,128]{1,0:T(8,128)S(1)}, f32[112,128]{1,0:T(8,128)S(1)}, u32[]{:S(2)}, u32[]{:S(2)}) collective-permute-start(f32[112,128]{1,0:T(8,128)S(1)} %add.77), channel_id=1, source_target_pairs={{0,8},{1,5},{2,10},{3,7},{4,12},{5,1},{6,14},{7,3},{8,0},{9,13},{1... | collective-permute-start | bytes 172040 | tf_op jit(solution)/shard_map/ppermute | solution.py:261
  29.2 1.4 %momentum.1 = bf16[128,3456]{1,0:T(8,128)(2,1)} custom-call(bf16[256,3456]{1,0:T(8,128)(2,1)S(1)} %get-tuple-element.10.both, f32[56,128]{1,0:T(8,128)S(1)} %get-tuple-element.9.c_ref, bf16[128,48]{1,0:T(8,128)(2,1)S(1)} %get-tuple-element.11.row_ref, bf16[128,1024]{1,0:T(8,128)(2,1)S(1)} %get-tuple-element.12.high_ref, ...), custom_call_target="tpu_custom_call" | custom-call | flops 42467328 | bytes 884736 | tf_op jit(solution)/shard_map/momentum/pallas_call | solution.py:216
  30.6 0.4 collective-permute-done.8
  31.0 1.3 %collective-permute-start.9 = (f32[8,128]{1,0:T(8,128)S(1)}, f32[8,128]{1,0:T(8,128)S(1)}, u32[]{:S(2)}, u32[]{:S(2)}) collective-permute-start(f32[8,128]{1,0:T(8,128)S(1)} %slice_add_fusion), channel_id=1, source_target_pairs={{0,2},{1,3},{2,0},{3,1},{4,6},{5,7},{6,4},{7,5},{8,10},{9,11},{10,... | collective-permute-start | bytes 12296 | tf_op jit(solution)/shard_map/ppermute | solution.py:261
  32.3 1.2 %collective-permute-done.9 = f32[8,128]{1,0:T(8,128)S(1)} collective-permute-done((f32[8,128]{1,0:T(8,128)S(1)}, f32[8,128]{1,0:T(8,128)S(1)}, u32[]{:S(2)}, u32[]{:S(2)}) %collective-permute-start.9) | collective-permute-done | bytes 4128 | tf_op jit(solution)/shard_map/ppermute | solution.py:261
  33.5 0.1 collective-permute-start.10
  33.6 1.2 %collective-permute-done.10 = f32[64,128]{1,0:T(8,128)S(1)} collective-permute-done((f32[64,128]{1,0:T(8,128)S(1)}, f32[64,128]{1,0:T(8,128)S(1)}, u32[]{:S(2)}, u32[]{:S(2)}) %collective-permute-start.10) | collective-permute-done | bytes 32800 | tf_op jit(solution)/shard_map/ppermute | solution.py:261
  34.9 0.3 half.1.half_ref
  35.2 1.5 %update.1 = f32[128,3456]{1,0:T(8,128)} custom-call(bf16[128,48]{1,0:T(8,128)(2,1)S(1)} %get-tuple-element.11.row_ref, bf16[48,3456]{1,0:T(8,128)(2,1)S(1)} %half.1.half_ref, f32[8,128]{1,0:T(8,128)S(1)} %slice.89.squares_ref), custom_call_target="tpu_custom_call" | custom-call | flops 42467328 | bytes 1769472 | tf_op jit(solution)/shard_map/update/pallas_call | solution.py:243
  (13 shorter events, 0.1 us)
Async XLA Ops:
  3.0 4.2 %collective-permute-start = (f32[56,128]{1,0:T(8,128)S(1)}, f32[56,128]{1,0:T(8,128)S(1)}, u32[]{:S(2)}, u32[]{:S(2)}) collective-permute-start(f32[56,128]{1,0:T(8,128)S(1)} %get-tuple-element.9.c_ref), channel_id=1, source_target_pairs={{0,1},{1,0},{2,3},{3,2},{4,5},{5,4},{6,7},{7,6},{8,9},{9,8},{10,11... | collective-permute-start | bytes 86024 | tf_op jit(solution)/shard_map/ppermute | solution.py:261
  7.2 4.6 %collective-permute-start.2 = (f32[112,128]{1,0:T(8,128)S(1)}, f32[112,128]{1,0:T(8,128)S(1)}, u32[]{:S(2)}, u32[]{:S(2)}) collective-permute-start(f32[112,128]{1,0:T(8,128)S(1)} %pad_maximum_fusion), channel_id=1, source_target_pairs={{0,32},{1,17},{2,34},{3,19},{4,36},{5,21},{6,38},{7,23},{8,40},{9,... | collective-permute-start | bytes 172040 | tf_op jit(solution)/shard_map/ppermute | solution.py:261
  8.5 4.2 %collective-permute-start.3 = (f32[112,128]{1,0:T(8,128)S(1)}, f32[112,128]{1,0:T(8,128)S(1)}, u32[]{:S(2)}, u32[]{:S(2)}) collective-permute-start(f32[112,128]{1,0:T(8,128)S(1)} %pad_maximum_fusion), channel_id=1, source_target_pairs={{0,32},{1,25},{2,34},{3,27},{4,36},{5,29},{6,38},{7,31},{8,40},{9,... | collective-permute-start | bytes 172040 | tf_op jit(solution)/shard_map/ppermute | solution.py:261
  9.3 3.5 %collective-permute-start.1 = (f32[112,128]{1,0:T(8,128)S(1)}, f32[112,128]{1,0:T(8,128)S(1)}, u32[]{:S(2)}, u32[]{:S(2)}) collective-permute-start(f32[112,128]{1,0:T(8,128)S(1)} %pad_maximum_fusion), channel_id=1, source_target_pairs={{0,32},{1,9},{2,34},{3,11},{4,36},{5,13},{6,38},{7,15},{8,40},{9,1... | collective-permute-start | bytes 172040 | tf_op jit(solution)/shard_map/ppermute | solution.py:261
  12.8 4.7 %collective-permute-start.6 = (f32[112,128]{1,0:T(8,128)S(1)}, f32[112,128]{1,0:T(8,128)S(1)}, u32[]{:S(2)}, u32[]{:S(2)}) collective-permute-start(f32[112,128]{1,0:T(8,128)S(1)} %add_add_fusion.1), channel_id=1, source_target_pairs={{0,8},{1,65},{2,10},{3,67},{4,12},{5,69},{6,14},{7,71},{8,0},{9,73... | collective-permute-start | bytes 172040 | tf_op jit(solution)/shard_map/ppermute | solution.py:261
  15.9 5.0 %collective-permute-start.5 = (f32[112,128]{1,0:T(8,128)S(1)}, f32[112,128]{1,0:T(8,128)S(1)}, u32[]{:S(2)}, u32[]{:S(2)}) collective-permute-start(f32[112,128]{1,0:T(8,128)S(1)} %add_add_fusion.1), channel_id=1, source_target_pairs={{0,8},{1,97},{2,10},{3,99},{4,12},{5,101},{6,14},{7,103},{8,0},{9,... | collective-permute-start | bytes 172040 | tf_op jit(solution)/shard_map/ppermute | solution.py:261
  17.3 3.6 %collective-permute-start.4 = (f32[112,128]{1,0:T(8,128)S(1)}, f32[112,128]{1,0:T(8,128)S(1)}, u32[]{:S(2)}, u32[]{:S(2)}) collective-permute-start(f32[112,128]{1,0:T(8,128)S(1)} %add_add_fusion.1), channel_id=1, source_target_pairs={{0,8},{1,33},{2,10},{3,35},{4,12},{5,37},{6,14},{7,39},{8,0},{9,41... | collective-permute-start | bytes 172040 | tf_op jit(solution)/shard_map/ppermute | solution.py:261
  21.0 5.3 %collective-permute-start.7 = (f32[112,128]{1,0:T(8,128)S(1)}, f32[112,128]{1,0:T(8,128)S(1)}, u32[]{:S(2)}, u32[]{:S(2)}) collective-permute-start(f32[112,128]{1,0:T(8,128)S(1)} %add_add_fusion), channel_id=1, source_target_pairs={{0,8},{1,193},{2,10},{3,195},{4,12},{5,197},{6,14},{7,199},{8,0},{... | collective-permute-start | bytes 172040 | tf_op jit(solution)/shard_map/ppermute | solution.py:261
  26.3 4.6 %collective-permute-start.8 = (f32[112,128]{1,0:T(8,128)S(1)}, f32[112,128]{1,0:T(8,128)S(1)}, u32[]{:S(2)}, u32[]{:S(2)}) collective-permute-start(f32[112,128]{1,0:T(8,128)S(1)} %add.77), channel_id=1, source_target_pairs={{0,8},{1,5},{2,10},{3,7},{4,12},{5,1},{6,14},{7,3},{8,0},{9,13},{1... | collective-permute-start | bytes 172040 | tf_op jit(solution)/shard_map/ppermute | solution.py:261
  31.0 2.5 %collective-permute-start.9 = (f32[8,128]{1,0:T(8,128)S(1)}, f32[8,128]{1,0:T(8,128)S(1)}, u32[]{:S(2)}, u32[]{:S(2)}) collective-permute-start(f32[8,128]{1,0:T(8,128)S(1)} %slice_add_fusion), channel_id=1, source_target_pairs={{0,2},{1,3},{2,0},{3,1},{4,6},{5,7},{6,4},{7,5},{8,10},{9,11},{10,... | collective-permute-start | bytes 12296 | tf_op jit(solution)/shard_map/ppermute | solution.py:261
  33.5 1.3 %collective-permute-start.10 = (f32[64,128]{1,0:T(8,128)S(1)}, f32[64,128]{1,0:T(8,128)S(1)}, u32[]{:S(2)}, u32[]{:S(2)}) collective-permute-start(f32[64,128]{1,0:T(8,128)S(1)} %pad_maximum_fusion.1), channel_id=1, source_target_pairs={{0,1},{1,0},{2,3},{3,2},{4,5},{5,4},{6,7},{7,6},{8,9},{9,8},{10,11... | collective-permute-start | bytes 98312 | tf_op jit(solution)/shard_map/ppermute | solution.py:261

commit v4 on v3

v4 whole, which is shorter than its diff:
```python
import functools
import math

import jax
import jax.numpy as jnp
from jax import lax
from jax.experimental import pallas as pl
from jax.experimental.pallas import tpu as pltpu
from jax.sharding import PartitionSpec as P

BLOCK = 64
KEEP = 8
LANES = 128
SPAN = 1024
VMEM_BYTES = 16 * 1024 * 1024
TILES = SPAN // LANES
WRITES = [(0, 512), (512, 1024), (1536, 1920)]
READS = [(0, 2048), (2048, 1408)]


def spans(cols):
    return [(start, min(SPAN, cols - start)) for start in range(0, cols, SPAN)]


def basis_tiles(fr_ref, fc_ref):
    row = lax.broadcasted_iota(jnp.int32, (2 * KEEP, LANES), 0)
    point = lax.broadcasted_iota(jnp.int32, (2 * KEEP, LANES), 1) & (BLOCK - 1)
    freq = jnp.zeros((2 * KEEP, LANES), jnp.int32)
    for k in range(KEEP):
        freq = jnp.where(row == k, fr_ref[k], freq)
        freq = jnp.where(row == KEEP + k, fc_ref[k], freq)
    turn = ((2 * point + 1) * freq) & (4 * BLOCK - 1)
    turn = jnp.minimum(turn, 4 * BLOCK - turn)
    x = (BLOCK - turn).astype(jnp.float32) * (math.pi / (2 * BLOCK))
    y = x * x
    series = jnp.full_like(x, 1.0 / math.factorial(13))
    for n in (11, 9, 7, 5, 3, 1):
        series = 1.0 / math.factorial(n) - series * y
    scale = jnp.where(freq == 0, math.sqrt(1.0 / BLOCK), math.sqrt(2.0 / BLOCK))
    return x * series * scale


def split(v):
    high = v.astype(jnp.bfloat16)
    return high, (v - high.astype(jnp.float32)).astype(jnp.bfloat16)


def two_blocks(tile):
    lane = lax.broadcasted_iota(jnp.int32, (KEEP, LANES), 1)
    return jnp.concatenate([jnp.where(lane < BLOCK, tile, 0.0), jnp.where(lane >= BLOCK, tile, 0.0)], axis=0)


def only(t, v):
    lane = lax.broadcasted_iota(jnp.int32, v.shape, 1)
    return jnp.where((lane >> 4) == t, v, 0.0)


def dot(a, b, dims):
    return lax.dot_general(a, b, (dims, ((), ())), preferred_element_type=jnp.float32)


def packed_rows(cols):
    whole, left = divmod(cols, SPAN)
    assert 0 < left <= SPAN // 2
    return 16 * whole + 8


def pack(spans16):
    last = spans16[-1]
    return jnp.concatenate(spans16[:-1] + [last[:8] + pltpu.roll(last[8:], LANES // 2, 1)], axis=0)


def unpack(rows):
    last = rows[-8:]
    return jnp.concatenate([rows, pltpu.roll(last, LANES // 2, 1)], axis=0)


def forward_kernel(
    fr_ref, fc_ref, m_ref, g_ref, out_ref, row_ref, high_ref, low_ref, both, fr_smem, fc_smem, fsems, sems
):
    cols = m_ref.shape[1]
    freqs = [
        pltpu.make_async_copy(src, dst, fsems.at[k]) for k, (src, dst) in enumerate(((fr_ref, fr_smem), (fc_ref, fc_smem)))
    ]
    for copy in freqs:
        copy.start()
    copies = []
    for n, (start, width) in enumerate(READS):
        for k, src in enumerate((m_ref, g_ref)):
            copy = pltpu.make_async_copy(
                src.at[:, pl.ds(start, width)], both.at[pl.ds(LANES * k, LANES), pl.ds(start, width)], sems.at[n, k]
            )
            copy.start()
            copies.append(copy)
    for copy in freqs:
        copy.wait()
    tiles = basis_tiles(fr_smem, fc_smem)
    rows = two_blocks(tiles[:KEEP])
    row_ref[...] = rows
    high, low = split(jnp.concatenate([0.9 * rows, rows], axis=1))
    lhs = jnp.concatenate([high, low], axis=0)
    high, low = split(two_blocks(tiles[KEEP:]))
    high_ref[...] = jnp.concatenate([high] * TILES, axis=0)
    low_ref[...] = jnp.concatenate([low] * TILES, axis=0)
    high_tiles, low_tiles = [], []
    for n, (start, width) in enumerate(READS):
        copies[2 * n].wait()
        copies[2 * n + 1].wait()
        y = dot(lhs, both[:, start : start + width], ((1,), (0,)))
        high, low = split(y[:16] + y[16:])
        high_tiles += [high[:, k : k + LANES] for k in range(0, width, LANES)]
        low_tiles += [low[:, k : k + LANES] for k in range(0, width, LANES)]
    y_high = jnp.concatenate(high_tiles, axis=0)
    c = dot(jnp.concatenate([y_high] + low_tiles, axis=0), high_ref[...], ((1,), (1,)))
    c = c[: y_high.shape[0]] + c[y_high.shape[0] :] + dot(y_high, low_ref[...], ((1,), (1,)))
    sums = []
    for first in range(0, cols // LANES, TILES):
        parts = [only(t - first, c[16 * t : 16 * t + 16]) for t in range(first, min(first + TILES, cols // LANES))]
        while len(parts) > 1:
            parts = [sum(parts[k : k + 2]) for k in range(0, len(parts), 2)]
        sums.append(parts[0])
    out_ref[...] = pack(sums)


def half_image(c, high_ref, low_ref, tiles):
    high = c.astype(jnp.bfloat16).astype(jnp.float32)
    low = c - high

    def spread(v):
        return jnp.concatenate(
            [only(t % TILES, v[t // TILES * 16 : t // TILES * 16 + 16]).astype(jnp.bfloat16) for t in tiles], axis=0
        )

    high = spread(high)
    count = high.shape[0]
    z = dot(jnp.concatenate([high, spread(low)], axis=0), high_ref[...], ((1,), (0,)))
    z = z[:count] + z[count:] + dot(high, low_ref[...], ((1,), (0,)))
    z_high, z_low = split(z)
    return jnp.concatenate(
        [jnp.concatenate([z_high[k : k + 16], z_low[k : k + 16], z_high[k : k + 16]], axis=0) for k in range(0, count, 16)],
        axis=1,
    )


def momentum_kernel(both, c_ref, row_ref, high_ref, low_ref, out_ref, turned_ref, held, sems):
    high, low = split(jnp.transpose(jnp.concatenate([row_ref[...]] * 3, axis=0)))
    third = lax.broadcasted_iota(jnp.int32, high.shape, 1) >= 32
    rows = jnp.where(third, low.astype(jnp.float32), high.astype(jnp.float32)).astype(jnp.bfloat16)
    turned_ref[...] = rows
    halves = half_image(unpack(c_ref[...]), high_ref, low_ref, range(out_ref.shape[1] // LANES))
    copies = []
    for n, (start, width) in enumerate(spans(out_ref.shape[1])):
        here = slice(start, start + width)
        image = dot(rows, halves[:, here], ((1,), (0,)))
        fresh = 0.9 * both[:LANES, here].astype(jnp.float32) + both[LANES:, here].astype(jnp.float32)
        held[:, here] = (fresh - image).astype(jnp.bfloat16)
        copy = pltpu.make_async_copy(held.at[:, pl.ds(start, width)], out_ref.at[:, pl.ds(start, width)], sems.at[n])
        copy.start()
        copies.append(copy)
    for copy in copies:
        copy.wait()


def update_kernel(entries, sent_ref, row_ref, high_ref, low_ref, out_ref, held, sems):
    rows = row_ref[...]
    count = sent_ref.shape[0] - KEEP
    c = unpack(sent_ref[:count])
    squares = jnp.sum(sent_ref[count:])
    scale = lax.rsqrt(jnp.full((LANES, LANES), squares, jnp.float32) * (1.0 / entries) + 1e-06)
    first = WRITES[0][1]
    halves = [
        half_image(c, high_ref, low_ref, range(first // LANES)),
        half_image(c, high_ref, low_ref, range(first // LANES, out_ref.shape[1] // LANES)),
    ]
    copies = []
    for n, (start, width) in enumerate(WRITES):
        here = slice(start, start + width)
        half = halves[0] if n == 0 else halves[1][:, start - first : start - first + width]
        image = dot(rows, half, ((1,), (0,)))
        held[:, here] = image * jnp.concatenate([scale] * (width // LANES), axis=1)
        copy = pltpu.make_async_copy(held.at[:, pl.ds(start, width)], out_ref.at[:, pl.ds(start, width)], sems.at[n])
        copy.start()
        copies.append(copy)
    for copy in copies:
        copy.wait()


VMEM = pl.BlockSpec(memory_space=pltpu.VMEM)
ANY = pl.BlockSpec(memory_space=pl.ANY)
PARAMS = pltpu.CompilerParams(vmem_limit_bytes=VMEM_BYTES)


def hbm(x):
    return pltpu.with_memory_space_constraint(x, pltpu.HBM)


def forward(freq_rows, freq_cols, m, g):
    rows, cols = m.shape
    return pl.pallas_call(
        forward_kernel,
        out_shape=[
            jax.ShapeDtypeStruct((packed_rows(cols), LANES), jnp.float32),
            pltpu.VMEM((16, LANES), jnp.float32),
            pltpu.VMEM((LANES, LANES), jnp.bfloat16),
            pltpu.VMEM((LANES, LANES), jnp.bfloat16),
            pltpu.VMEM((2 * rows, cols), jnp.bfloat16),
        ],
        in_specs=[ANY] * 4,
        out_specs=[VMEM] * 5,
        scratch_shapes=[
            pltpu.SMEM((KEEP,), jnp.int32),
            pltpu.SMEM((KEEP,), jnp.int32),
            pltpu.SemaphoreType.DMA((2,)),
            pltpu.SemaphoreType.DMA((len(READS), 2)),
        ],
        compiler_params=PARAMS,
        cost_estimate=pl.CostEstimate(flops=2 * 48 * rows * cols, bytes_accessed=4 * rows * cols, transcendentals=0),
        name="forward",
    )(hbm(freq_rows), hbm(freq_cols), hbm(m), hbm(g))


def momentum_left(both, coeffs, row, high, low):
    rows, cols = both.shape[0] // 2, both.shape[1]
    n = len(spans(cols))
    return pl.pallas_call(
        momentum_kernel,
        out_shape=[jax.ShapeDtypeStruct((rows, cols), jnp.bfloat16), pltpu.VMEM((rows, 48), jnp.bfloat16)],
        in_specs=[VMEM] * 5,
        out_specs=[ANY, VMEM],
        scratch_shapes=[pltpu.VMEM((rows, cols), jnp.bfloat16), pltpu.SemaphoreType.DMA((len(spans(cols)),))],
        compiler_params=PARAMS,
        cost_estimate=pl.CostEstimate(flops=2 * 48 * rows * cols, bytes_accessed=2 * rows * cols, transcendentals=0),
        name="momentum",
    )(both, coeffs, row, high, low)


def updated(sent, row, high, low, cols, entries):
    rows = row.shape[0]
    return pl.pallas_call(
        functools.partial(update_kernel, entries),
        out_shape=jax.ShapeDtypeStruct((rows, cols), jnp.float32),
        in_specs=[VMEM] * 4,
        out_specs=ANY,
        scratch_shapes=[pltpu.VMEM((rows, cols), jnp.float32), pltpu.SemaphoreType.DMA((len(WRITES),))],
        compiler_params=PARAMS,
        cost_estimate=pl.CostEstimate(flops=2 * 48 * rows * cols, bytes_accessed=4 * rows * cols, transcendentals=0),
        name="update",
    )(sent, row, high, low)


def moved(v, partner):
    pairs = []
    for d in range(256):
        z, y, x, near, core = d // 32, d // 8 % 4, d // 4 % 2, d // 2 % 2, d % 2
        z, y, x, near, core = partner(z, y, x, near, core)
        pairs.append((d, (((z * 4 + y) * 2 + x) * 2 + near) * 2 + core))
    return lax.ppermute(v, ("rep", "tp"), pairs)


def replica(dz, dy, dx):
    def partner(z, y, x, near, core):
        if core == 0:
            return (z ^ 1, y, x, near, core) if dy else (z, y ^ 1, x, near, core)
        return z ^ dz, y ^ dy, x ^ dx, near, core

    return partner


def other_core(z, y, x, near, core):
    return z, y, x, near, 1 - core


def next_chip(z, y, x, near, core):
    return z, y, x, 1 - near, core


def four_way(v, a, b):
    both = tuple(i ^ j for i, j in zip(a, b))
    return (v + moved(v, replica(*a))) + (moved(v, replica(*b)) + moved(v, replica(*both)))


def body(momentum, grad, freq_rows, freq_cols):
    m, g = momentum[0], grad[0]
    rows, cols = m.shape
    tp = lax.axis_size("tp")
    core = lax.axis_index("tp") % 2
    own, row, high, low, both = forward(freq_rows, freq_cols, m, g)
    count = own.shape[0]
    other = moved(own, other_core)
    pair = jnp.concatenate([jnp.where(core == 1, other, own), jnp.where(core == 1, own, other)], axis=0)
    pair = four_way(pair, (0, 1, 0), (0, 2, 0))
    pair = four_way(pair, (1, 0, 0), (3, 0, 0))
    pair = pair + moved(pair, replica(6, 0, 0))
    kept, turned = momentum_left(both, own, row, high, low)
    other, kept, turned = lax.optimization_barrier((moved(pair, replica(0, 0, 1)), kept, turned))
    pair = pair + other
    squares = pair * pair
    squares = sum(squares[k : k + KEEP] for k in range(0, 2 * count, KEEP))
    squares = squares + moved(squares, next_chip)
    sent = jnp.concatenate([pair[:count], squares], axis=0)
    sent = jnp.where(core == 1, jnp.concatenate([pair[count:], squares], axis=0), moved(sent, other_core))
    update = updated(sent, turned, high, low, cols, float(rows * cols * tp))
    return kept[None], update


def solution(mesh):
    placed = (P("rep", None, "tp"), P("rep", None, "tp"), P(), P())
    return jax.shard_map(
        body,
        mesh=mesh,
        in_specs=placed,
        out_specs=(P("rep", None, "tp"), P(None, "tp")),
        check_vma=False,
    )
```

time: 36.7 us -> 36.2 us (0.986)
  Pallas kernels: 5.58 us -> 5.01 us
    pallas_call x2 -> x1, Pallas kernels: 1.71 us -> 1.37 us  [momentum_left(): pl.pallas_call(momentum_kernel, out_shape=[jax.ShapeDtypeStruct((rows, co...]
where the time goes in v4:
time: 36.2 us; the launch traced here: 36.1 us
  starting transfers between devices  18.7 us (52%)
  waiting for transfers between devices  11.5 us (32%)
  Pallas kernels  5.01 us (14%)
  between operations  0.68 us (2%)
    ppermute x11, starting transfers between devices, moved(): return lax.ppermute(v, ('rep', 'tp'), pairs)  18.7 us
    ppermute x11, waiting for transfers between devices, moved(): return lax.ppermute(v, ('rep', 'tp'), pairs)  11.5 us
    pallas_call x1, Pallas kernels, forward(): pl.pallas_call(forward_kernel, out_shape=[jax.ShapeDtypeStruct((packed_ro...  2.05 us
    pallas_call x1, Pallas kernels, updated(): pl.pallas_call(functools.partial(update_kernel, entries), out_shape=jax.S...  1.59 us
    pallas_call x1, Pallas kernels, momentum_left(): pl.pallas_call(momentum_kernel, out_shape=[jax.ShapeDtypeStruct((rows, co...  1.37 us
  transfers between devices with their start and end apart: 11, of which 9 were waited for; matrix products, arithmetic and copies ran while one was open for 0% of the time, Pallas kernels for 4%

profile of v4, /device:TPU:1, one launch (start us, length us, event | category | flops | bytes accessed | tf_op | source)
XLA Modules:
  0.0 36.1 jit_solution(18234954859754248400)
XLA Ops:
  0.6 2.0 %forward.1 = (f32[56,128]{1,0:T(8,128)S(1)}, f32[16,128]{1,0:T(8,128)S(1)}, bf16[128,128]{1,0:T(8,128)(2,1)S(1)}, bf16[128,128]{1,0:T(8,128)(2,1)S(1)}, bf16[256,3456]{1,0:T(8,128)(2,1)S(1)}) custom-call(s32[8]{0:T(128)} %fr_ref.1, s32[8]{0:T(128)} %fc_ref.1, bf16[128,3456]{1,0:T(8,128)(2,1)} %bitcast.3, bf16[128,3456]{1,0:T(8,128)(2,1)} %bitcast.4), custom_call_target="tpu_custom_call" | custom-call | flops 42467328 | bytes 1769472 | tf_op jit(solution)/shard_map/forward/pallas_call | solution.py:199
  2.7 3.3 %collective-permute-start = (f32[56,128]{1,0:T(8,128)S(1)}, f32[56,128]{1,0:T(8,128)S(1)}, u32[]{:S(2)}, u32[]{:S(2)}) collective-permute-start(f32[56,128]{1,0:T(8,128)S(1)} %get-tuple-element.12.c_ref), channel_id=1, source_target_pairs={{0,1},{1,0},{2,3},{3,2},{4,5},{5,4},{6,7},{7,6},{8,9},{9,8},{10,11... | collective-permute-start | bytes 86024 | tf_op jit(solution)/shard_map/ppermute | solution.py:257
  6.0 0.9 %collective-permute-done = f32[56,128]{1,0:T(8,128)S(1)} collective-permute-done((f32[56,128]{1,0:T(8,128)S(1)}, f32[56,128]{1,0:T(8,128)S(1)}, u32[]{:S(2)}, u32[]{:S(2)}) %collective-permute-start) | collective-permute-done | bytes 28704 | tf_op jit(solution)/shard_map/ppermute | solution.py:257
  6.9 1.3 %collective-permute-start.2 = (f32[112,128]{1,0:T(8,128)S(1)}, f32[112,128]{1,0:T(8,128)S(1)}, u32[]{:S(2)}, u32[]{:S(2)}) collective-permute-start(f32[112,128]{1,0:T(8,128)S(1)} %pad_maximum_fusion), channel_id=1, source_target_pairs={{0,32},{1,17},{2,34},{3,19},{4,36},{5,21},{6,38},{7,23},{8,40},{9,... | collective-permute-start | bytes 172040 | tf_op jit(solution)/shard_map/ppermute | solution.py:257
  8.1 0.8 %collective-permute-start.3 = (f32[112,128]{1,0:T(8,128)S(1)}, f32[112,128]{1,0:T(8,128)S(1)}, u32[]{:S(2)}, u32[]{:S(2)}) collective-permute-start(f32[112,128]{1,0:T(8,128)S(1)} %pad_maximum_fusion), channel_id=1, source_target_pairs={{0,32},{1,25},{2,34},{3,27},{4,36},{5,29},{6,38},{7,31},{8,40},{9,... | collective-permute-start | bytes 172040 | tf_op jit(solution)/shard_map/ppermute | solution.py:257
  8.9 0.7 %collective-permute-start.1 = (f32[112,128]{1,0:T(8,128)S(1)}, f32[112,128]{1,0:T(8,128)S(1)}, u32[]{:S(2)}, u32[]{:S(2)}) collective-permute-start(f32[112,128]{1,0:T(8,128)S(1)} %pad_maximum_fusion), channel_id=1, source_target_pairs={{0,32},{1,9},{2,34},{3,11},{4,36},{5,13},{6,38},{7,15},{8,40},{9,1... | collective-permute-start | bytes 172040 | tf_op jit(solution)/shard_map/ppermute | solution.py:257
  9.6 1.9 %collective-permute-done.2 = f32[112,128]{1,0:T(8,128)S(1)} collective-permute-done((f32[112,128]{1,0:T(8,128)S(1)}, f32[112,128]{1,0:T(8,128)S(1)}, u32[]{:S(2)}, u32[]{:S(2)}) %collective-permute-start.2) | collective-permute-done | bytes 57376 | tf_op jit(solution)/shard_map/ppermute | solution.py:257
  11.5 0.9 %collective-permute-done.3 = f32[112,128]{1,0:T(8,128)S(1)} collective-permute-done((f32[112,128]{1,0:T(8,128)S(1)}, f32[112,128]{1,0:T(8,128)S(1)}, u32[]{:S(2)}, u32[]{:S(2)}) %collective-permute-start.3) | collective-permute-done | bytes 57376 | tf_op jit(solution)/shard_map/ppermute | solution.py:257
  12.4 0.0 collective-permute-done.1
  12.4 3.1 %collective-permute-start.6 = (f32[112,128]{1,0:T(8,128)S(1)}, f32[112,128]{1,0:T(8,128)S(1)}, u32[]{:S(2)}, u32[]{:S(2)}) collective-permute-start(f32[112,128]{1,0:T(8,128)S(1)} %add_add_fusion.1), channel_id=1, source_target_pairs={{0,8},{1,65},{2,10},{3,67},{4,12},{5,69},{6,14},{7,71},{8,0},{9,73... | collective-permute-start | bytes 172040 | tf_op jit(solution)/shard_map/ppermute | solution.py:257
  15.5 1.5 %collective-permute-start.5 = (f32[112,128]{1,0:T(8,128)S(1)}, f32[112,128]{1,0:T(8,128)S(1)}, u32[]{:S(2)}, u32[]{:S(2)}) collective-permute-start(f32[112,128]{1,0:T(8,128)S(1)} %add_add_fusion.1), channel_id=1, source_target_pairs={{0,8},{1,97},{2,10},{3,99},{4,12},{5,101},{6,14},{7,103},{8,0},{9,... | collective-permute-start | bytes 172040 | tf_op jit(solution)/shard_map/ppermute | solution.py:257
  16.9 0.2 collective-permute-start.4
  17.1 0.0 collective-permute-done.6
  17.1 3.3 %collective-permute-done.5 = f32[112,128]{1,0:T(8,128)S(1)} collective-permute-done((f32[112,128]{1,0:T(8,128)S(1)}, f32[112,128]{1,0:T(8,128)S(1)}, u32[]{:S(2)}, u32[]{:S(2)}) %collective-permute-start.5) | collective-permute-done | bytes 57376 | tf_op jit(solution)/shard_map/ppermute | solution.py:257
  20.5 0.1 collective-permute-done.4
  20.6 3.7 %collective-permute-start.7 = (f32[112,128]{1,0:T(8,128)S(1)}, f32[112,128]{1,0:T(8,128)S(1)}, u32[]{:S(2)}, u32[]{:S(2)}) collective-permute-start(f32[112,128]{1,0:T(8,128)S(1)} %add_add_fusion), channel_id=1, source_target_pairs={{0,8},{1,193},{2,10},{3,195},{4,12},{5,197},{6,14},{7,199},{8,0},{... | collective-permute-start | bytes 172040 | tf_op jit(solution)/shard_map/ppermute | solution.py:257
  24.3 1.6 %collective-permute-done.7 = f32[112,128]{1,0:T(8,128)S(1)} collective-permute-done((f32[112,128]{1,0:T(8,128)S(1)}, f32[112,128]{1,0:T(8,128)S(1)}, u32[]{:S(2)}, u32[]{:S(2)}) %collective-permute-start.7) | collective-permute-done | bytes 57376 | tf_op jit(solution)/shard_map/ppermute | solution.py:257
  26.0 2.8 %collective-permute-start.8 = (f32[112,128]{1,0:T(8,128)S(1)}, f32[112,128]{1,0:T(8,128)S(1)}, u32[]{:S(2)}, u32[]{:S(2)}) collective-permute-start(f32[112,128]{1,0:T(8,128)S(1)} %add.77), channel_id=1, source_target_pairs={{0,8},{1,5},{2,10},{3,7},{4,12},{5,1},{6,14},{7,3},{8,0},{9,13},{1... | collective-permute-start | bytes 172040 | tf_op jit(solution)/shard_map/ppermute | solution.py:257
  28.8 1.4 %momentum.1 = (bf16[128,3456]{1,0:T(8,128)(2,1)}, bf16[128,48]{1,0:T(8,128)(2,1)S(1)}) custom-call(bf16[256,3456]{1,0:T(8,128)(2,1)S(1)} %get-tuple-element.13.both, f32[56,128]{1,0:T(8,128)S(1)} %get-tuple-element.12.c_ref, f32[16,128]{1,0:T(8,128)S(1)} %get-tuple-element.14.row_ref, bf16[128,128]{1,0:T(8,128)(2,1)S(1)} %get-tuple-element.15.high_ref, ...), custom_call_target="tpu_custom_call" | custom-call | flops 42467328 | bytes 884736 | tf_op jit(solution)/shard_map/momentum/pallas_call | solution.py:225
  30.2 0.4 %collective-permute-done.8 = f32[112,128]{1,0:T(8,128)S(1)} collective-permute-done((f32[112,128]{1,0:T(8,128)S(1)}, f32[112,128]{1,0:T(8,128)S(1)}, u32[]{:S(2)}, u32[]{:S(2)}) %collective-permute-start.8) | collective-permute-done | bytes 57376 | tf_op jit(solution)/shard_map/ppermute | solution.py:257
  30.6 1.3 %collective-permute-start.9 = (f32[8,128]{1,0:T(8,128)S(1)}, f32[8,128]{1,0:T(8,128)S(1)}, u32[]{:S(2)}, u32[]{:S(2)}) collective-permute-start(f32[8,128]{1,0:T(8,128)S(1)} %slice_add_fusion), channel_id=1, source_target_pairs={{0,2},{1,3},{2,0},{3,1},{4,6},{5,7},{6,4},{7,5},{8,10},{9,11},{10,... | collective-permute-start | bytes 12296 | tf_op jit(solution)/shard_map/ppermute | solution.py:257
  31.9 1.2 %collective-permute-done.9 = f32[8,128]{1,0:T(8,128)S(1)} collective-permute-done((f32[8,128]{1,0:T(8,128)S(1)}, f32[8,128]{1,0:T(8,128)S(1)}, u32[]{:S(2)}, u32[]{:S(2)}) %collective-permute-start.9) | collective-permute-done | bytes 4128 | tf_op jit(solution)/shard_map/ppermute | solution.py:257
  33.2 0.1 collective-permute-start.10
  33.3 1.2 %collective-permute-done.10 = f32[64,128]{1,0:T(8,128)S(1)} collective-permute-done((f32[64,128]{1,0:T(8,128)S(1)}, f32[64,128]{1,0:T(8,128)S(1)}, u32[]{:S(2)}, u32[]{:S(2)}) %collective-permute-start.10) | collective-permute-done | bytes 32800 | tf_op jit(solution)/shard_map/ppermute | solution.py:257
  34.5 1.6 %update.1 = f32[128,3456]{1,0:T(8,128)} custom-call(f32[64,128]{1,0:T(8,128)S(1)} %fusion.sent_ref, bf16[128,48]{1,0:T(8,128)(2,1)S(1)} %get-tuple-element.21.row_ref, bf16[128,128]{1,0:T(8,128)(2,1)S(1)} %get-tuple-element.15.high_ref, bf16[128,128]{1,0:T(8,128)(2,1)S(1)} %get-tuple-element.16.low_ref), custom_call_target="tpu_custom_call" | custom-call | flops 42467328 | bytes 1769472 | tf_op jit(solution)/shard_map/update/pallas_call | solution.py:239
  (11 shorter events, 0.1 us)
Async XLA Ops:
  2.7 4.2 %collective-permute-start = (f32[56,128]{1,0:T(8,128)S(1)}, f32[56,128]{1,0:T(8,128)S(1)}, u32[]{:S(2)}, u32[]{:S(2)}) collective-permute-start(f32[56,128]{1,0:T(8,128)S(1)} %get-tuple-element.12.c_ref), channel_id=1, source_target_pairs={{0,1},{1,0},{2,3},{3,2},{4,5},{5,4},{6,7},{7,6},{8,9},{9,8},{10,11... | collective-permute-start | bytes 86024 | tf_op jit(solution)/shard_map/ppermute | solution.py:257
  6.9 4.6 %collective-permute-start.2 = (f32[112,128]{1,0:T(8,128)S(1)}, f32[112,128]{1,0:T(8,128)S(1)}, u32[]{:S(2)}, u32[]{:S(2)}) collective-permute-start(f32[112,128]{1,0:T(8,128)S(1)} %pad_maximum_fusion), channel_id=1, source_target_pairs={{0,32},{1,17},{2,34},{3,19},{4,36},{5,21},{6,38},{7,23},{8,40},{9,... | collective-permute-start | bytes 172040 | tf_op jit(solution)/shard_map/ppermute | solution.py:257
  8.1 4.2 %collective-permute-start.3 = (f32[112,128]{1,0:T(8,128)S(1)}, f32[112,128]{1,0:T(8,128)S(1)}, u32[]{:S(2)}, u32[]{:S(2)}) collective-permute-start(f32[112,128]{1,0:T(8,128)S(1)} %pad_maximum_fusion), channel_id=1, source_target_pairs={{0,32},{1,25},{2,34},{3,27},{4,36},{5,29},{6,38},{7,31},{8,40},{9,... | collective-permute-start | bytes 172040 | tf_op jit(solution)/shard_map/ppermute | solution.py:257
  8.9 3.5 %collective-permute-start.1 = (f32[112,128]{1,0:T(8,128)S(1)}, f32[112,128]{1,0:T(8,128)S(1)}, u32[]{:S(2)}, u32[]{:S(2)}) collective-permute-start(f32[112,128]{1,0:T(8,128)S(1)} %pad_maximum_fusion), channel_id=1, source_target_pairs={{0,32},{1,9},{2,34},{3,11},{4,36},{5,13},{6,38},{7,15},{8,40},{9,1... | collective-permute-start | bytes 172040 | tf_op jit(solution)/shard_map/ppermute | solution.py:257
  12.4 4.7 %collective-permute-start.6 = (f32[112,128]{1,0:T(8,128)S(1)}, f32[112,128]{1,0:T(8,128)S(1)}, u32[]{:S(2)}, u32[]{:S(2)}) collective-permute-start(f32[112,128]{1,0:T(8,128)S(1)} %add_add_fusion.1), channel_id=1, source_target_pairs={{0,8},{1,65},{2,10},{3,67},{4,12},{5,69},{6,14},{7,71},{8,0},{9,73... | collective-permute-start | bytes 172040 | tf_op jit(solution)/shard_map/ppermute | solution.py:257
  15.5 5.0 %collective-permute-start.5 = (f32[112,128]{1,0:T(8,128)S(1)}, f32[112,128]{1,0:T(8,128)S(1)}, u32[]{:S(2)}, u32[]{:S(2)}) collective-permute-start(f32[112,128]{1,0:T(8,128)S(1)} %add_add_fusion.1), channel_id=1, source_target_pairs={{0,8},{1,97},{2,10},{3,99},{4,12},{5,101},{6,14},{7,103},{8,0},{9,... | collective-permute-start | bytes 172040 | tf_op jit(solution)/shard_map/ppermute | solution.py:257
  16.9 3.6 %collective-permute-start.4 = (f32[112,128]{1,0:T(8,128)S(1)}, f32[112,128]{1,0:T(8,128)S(1)}, u32[]{:S(2)}, u32[]{:S(2)}) collective-permute-start(f32[112,128]{1,0:T(8,128)S(1)} %add_add_fusion.1), channel_id=1, source_target_pairs={{0,8},{1,33},{2,10},{3,35},{4,12},{5,37},{6,14},{7,39},{8,0},{9,41... | collective-permute-start | bytes 172040 | tf_op jit(solution)/shard_map/ppermute | solution.py:257
  20.6 5.3 %collective-permute-start.7 = (f32[112,128]{1,0:T(8,128)S(1)}, f32[112,128]{1,0:T(8,128)S(1)}, u32[]{:S(2)}, u32[]{:S(2)}) collective-permute-start(f32[112,128]{1,0:T(8,128)S(1)} %add_add_fusion), channel_id=1, source_target_pairs={{0,8},{1,193},{2,10},{3,195},{4,12},{5,197},{6,14},{7,199},{8,0},{... | collective-permute-start | bytes 172040 | tf_op jit(solution)/shard_map/ppermute | solution.py:257
  26.0 4.6 %collective-permute-start.8 = (f32[112,128]{1,0:T(8,128)S(1)}, f32[112,128]{1,0:T(8,128)S(1)}, u32[]{:S(2)}, u32[]{:S(2)}) collective-permute-start(f32[112,128]{1,0:T(8,128)S(1)} %add.77), channel_id=1, source_target_pairs={{0,8},{1,5},{2,10},{3,7},{4,12},{5,1},{6,14},{7,3},{8,0},{9,13},{1... | collective-permute-start | bytes 172040 | tf_op jit(solution)/shard_map/ppermute | solution.py:257
  30.6 2.5 %collective-permute-start.9 = (f32[8,128]{1,0:T(8,128)S(1)}, f32[8,128]{1,0:T(8,128)S(1)}, u32[]{:S(2)}, u32[]{:S(2)}) collective-permute-start(f32[8,128]{1,0:T(8,128)S(1)} %slice_add_fusion), channel_id=1, source_target_pairs={{0,2},{1,3},{2,0},{3,1},{4,6},{5,7},{6,4},{7,5},{8,10},{9,11},{10,... | collective-permute-start | bytes 12296 | tf_op jit(solution)/shard_map/ppermute | solution.py:257
  33.2 1.3 %collective-permute-start.10 = (f32[64,128]{1,0:T(8,128)S(1)}, f32[64,128]{1,0:T(8,128)S(1)}, u32[]{:S(2)}, u32[]{:S(2)}) collective-permute-start(f32[64,128]{1,0:T(8,128)S(1)} %pad_maximum_fusion.1), channel_id=1, source_target_pairs={{0,1},{1,0},{2,3},{3,2},{4,5},{5,4},{6,7},{7,6},{8,9},{9,8},{10,11... | collective-permute-start | bytes 98312 | tf_op jit(solution)/shard_map/ppermute | solution.py:257

commit v5 on v4

--- a/solution.py
+++ b/solution.py
@@ -161,28 +161,31 @@
         copy.wait()
 
 
-def update_kernel(entries, sent_ref, row_ref, high_ref, low_ref, out_ref, held, sems):
-    rows = row_ref[...]
-    count = sent_ref.shape[0] - KEEP
-    c = unpack(sent_ref[:count])
-    squares = jnp.sum(sent_ref[count:])
-    scale = lax.rsqrt(jnp.full((LANES, LANES), squares, jnp.float32) * (1.0 / entries) + 1e-06)
-    first = WRITES[0][1]
-    halves = [
-        half_image(c, high_ref, low_ref, range(first // LANES)),
-        half_image(c, high_ref, low_ref, range(first // LANES, out_ref.shape[1] // LANES)),
-    ]
-    copies = []
-    for n, (start, width) in enumerate(WRITES):
-        here = slice(start, start + width)
-        half = halves[0] if n == 0 else halves[1][:, start - first : start - first + width]
-        image = dot(rows, half, ((1,), (0,)))
-        held[:, here] = image * jnp.concatenate([scale] * (width // LANES), axis=1)
-        copy = pltpu.make_async_copy(held.at[:, pl.ds(start, width)], out_ref.at[:, pl.ds(start, width)], sems.at[n])
-        copy.start()
-        copies.append(copy)
-    for copy in copies:
-        copy.wait()
+def update_kernel(entries, core, total_ref, squares_ref, row_ref, high_ref, low_ref, *refs):
+    out_ref, held, sems = refs[-3:]
+
+    @pl.when(lax.axis_index("tp") % 2 == core)
+    def _():
+        rows = row_ref[...]
+        c = unpack(total_ref[...])
+        squares = jnp.sum(squares_ref[...])
+        scale = lax.rsqrt(jnp.full((LANES, LANES), squares, jnp.float32) * (1.0 / entries) + 1e-06)
+        first = WRITES[0][1]
+        halves = [
+            half_image(c, high_ref, low_ref, range(first // LANES)),
+            half_image(c, high_ref, low_ref, range(first // LANES, out_ref.shape[1] // LANES)),
+        ]
+        copies = []
+        for n, (start, width) in enumerate(WRITES):
+            here = slice(start, start + width)
+            half = halves[0] if n == 0 else halves[1][:, start - first : start - first + width]
+            image = dot(rows, half, ((1,), (0,)))
+            held[:, here] = image * jnp.concatenate([scale] * (width // LANES), axis=1)
+            copy = pltpu.make_async_copy(held.at[:, pl.ds(start, width)], out_ref.at[:, pl.ds(start, width)], sems.at[n])
+            copy.start()
+            copies.append(copy)
+        for copy in copies:
+            copy.wait()
 
 
 VMEM = pl.BlockSpec(memory_space=pltpu.VMEM)
@@ -234,18 +237,20 @@
     )(both, coeffs, row, high, low)
 
 
-def updated(sent, row, high, low, cols, entries):
+def updated(core, total, squares, row, high, low, cols, entries, before=None):
     rows = row.shape[0]
+    given = [total, squares, row, high, low] + ([] if before is None else [before])
     return pl.pallas_call(
-        functools.partial(update_kernel, entries),
+        functools.partial(update_kernel, entries, core),
         out_shape=jax.ShapeDtypeStruct((rows, cols), jnp.float32),
-        in_specs=[VMEM] * 4,
+        in_specs=[VMEM] * 5 + [ANY] * (len(given) - 5),
         out_specs=ANY,
+        input_output_aliases={} if before is None else {5: 0},
         scratch_shapes=[pltpu.VMEM((rows, cols), jnp.float32), pltpu.SemaphoreType.DMA((len(WRITES),))],
         compiler_params=PARAMS,
         cost_estimate=pl.CostEstimate(flops=2 * 48 * rows * cols, bytes_accessed=4 * rows * cols, transcendentals=0),
         name="update",
-    )(sent, row, high, low)
+    )(*given)
 
 
 def moved(v, partner):
@@ -297,9 +302,10 @@
     squares = pair * pair
     squares = sum(squares[k : k + KEEP] for k in range(0, 2 * count, KEEP))
     squares = squares + moved(squares, next_chip)
-    sent = jnp.concatenate([pair[:count], squares], axis=0)
-    sent = jnp.where(core == 1, jnp.concatenate([pair[count:], squares], axis=0), moved(sent, other_core))
-    update = updated(sent, turned, high, low, cols, float(rows * cols * tp))
+    entries = float(rows * cols * tp)
+    sent = moved(jnp.concatenate([pair[:count], squares], axis=0), other_core)
+    update = updated(1, pair[count:], squares, turned, high, low, cols, entries)
+    update = updated(0, sent[:count], sent[count:], turned, high, low, cols, entries, update)
     return kept[None], update
 
 

time: 36.2 us -> 35.1 us (0.970)
  waiting for transfers between devices: 11.5 us -> 10.3 us
    ppermute x11, waiting for transfers between devices: 11.5 us -> 10.3 us  [moved(): return lax.ppermute(v, ('rep', 'tp'), pairs)]
    pallas_call x1 -> x2, Pallas kernels: 1.59 us -> 1.65 us  [updated(): pl.pallas_call(functools.partial(update_kernel, entries, core), out_shape...]
  transfers between devices with their start and end apart: 11 -> 11, of which waited for: 9 -> 8; matrix products, arithmetic and copies ran while one was open for 0% -> 0% of each run, Pallas kernels for 4% -> 9%
where the time goes in v5:
time: 35.1 us; the launch traced here: 35 us
  starting transfers between devices  18.7 us (53%)
  waiting for transfers between devices  10.3 us (29%)
  Pallas kernels  5.07 us (14%)
  between operations  0.71 us (2%)
    ppermute x11, starting transfers between devices, moved(): return lax.ppermute(v, ('rep', 'tp'), pairs)  18.7 us
    ppermute x11, waiting for transfers between devices, moved(): return lax.ppermute(v, ('rep', 'tp'), pairs)  10.3 us
    pallas_call x1, Pallas kernels, forward(): pl.pallas_call(forward_kernel, out_shape=[jax.ShapeDtypeStruct((packed_ro...  2.05 us
    pallas_call x2, Pallas kernels, updated(): pl.pallas_call(functools.partial(update_kernel, entries, core), out_shape...  1.65 us
    pallas_call x1, Pallas kernels, momentum_left(): pl.pallas_call(momentum_kernel, out_shape=[jax.ShapeDtypeStruct((rows, co...  1.37 us
  transfers between devices with their start and end apart: 11, of which 8 were waited for; matrix products, arithmetic and copies ran while one was open for 0% of the time, Pallas kernels for 9%

profile of v5, /device:TPU:1, one launch (start us, length us, event | category | flops | bytes accessed | tf_op | source)
XLA Modules:
  0.0 35.0 jit_solution(17927084600548184500)
XLA Ops:
  0.6 2.0 %forward.1 = (f32[56,128]{1,0:T(8,128)S(1)}, f32[16,128]{1,0:T(8,128)S(1)}, bf16[128,128]{1,0:T(8,128)(2,1)S(1)}, bf16[128,128]{1,0:T(8,128)(2,1)S(1)}, bf16[256,3456]{1,0:T(8,128)(2,1)S(1)}) custom-call(s32[8]{0:T(128)} %fr_ref.1, s32[8]{0:T(128)} %fc_ref.1, bf16[128,3456]{1,0:T(8,128)(2,1)} %bitcast.3, bf16[128,3456]{1,0:T(8,128)(2,1)} %bitcast.4), custom_call_target="tpu_custom_call" | custom-call | flops 42467328 | bytes 1769472 | tf_op jit(solution)/shard_map/forward/pallas_call | solution.py:202
  2.7 3.3 %collective-permute-start = (f32[56,128]{1,0:T(8,128)S(1)}, f32[56,128]{1,0:T(8,128)S(1)}, u32[]{:S(2)}, u32[]{:S(2)}) collective-permute-start(f32[56,128]{1,0:T(8,128)S(1)} %get-tuple-element.12.c_ref), channel_id=1, source_target_pairs={{0,1},{1,0},{2,3},{3,2},{4,5},{5,4},{6,7},{7,6},{8,9},{9,8},{10,11... | collective-permute-start | bytes 86024 | tf_op jit(solution)/shard_map/ppermute | solution.py:262
  6.0 0.9 %collective-permute-done = f32[56,128]{1,0:T(8,128)S(1)} collective-permute-done((f32[56,128]{1,0:T(8,128)S(1)}, f32[56,128]{1,0:T(8,128)S(1)}, u32[]{:S(2)}, u32[]{:S(2)}) %collective-permute-start) | collective-permute-done | bytes 28704 | tf_op jit(solution)/shard_map/ppermute | solution.py:262
  6.9 1.3 %collective-permute-start.2 = (f32[112,128]{1,0:T(8,128)S(1)}, f32[112,128]{1,0:T(8,128)S(1)}, u32[]{:S(2)}, u32[]{:S(2)}) collective-permute-start(f32[112,128]{1,0:T(8,128)S(1)} %pad_maximum_fusion), channel_id=1, source_target_pairs={{0,32},{1,17},{2,34},{3,19},{4,36},{5,21},{6,38},{7,23},{8,40},{9,... | collective-permute-start | bytes 172040 | tf_op jit(solution)/shard_map/ppermute | solution.py:262
  8.1 0.8 %collective-permute-start.3 = (f32[112,128]{1,0:T(8,128)S(1)}, f32[112,128]{1,0:T(8,128)S(1)}, u32[]{:S(2)}, u32[]{:S(2)}) collective-permute-start(f32[112,128]{1,0:T(8,128)S(1)} %pad_maximum_fusion), channel_id=1, source_target_pairs={{0,32},{1,25},{2,34},{3,27},{4,36},{5,29},{6,38},{7,31},{8,40},{9,... | collective-permute-start | bytes 172040 | tf_op jit(solution)/shard_map/ppermute | solution.py:262
  8.9 0.7 %collective-permute-start.1 = (f32[112,128]{1,0:T(8,128)S(1)}, f32[112,128]{1,0:T(8,128)S(1)}, u32[]{:S(2)}, u32[]{:S(2)}) collective-permute-start(f32[112,128]{1,0:T(8,128)S(1)} %pad_maximum_fusion), channel_id=1, source_target_pairs={{0,32},{1,9},{2,34},{3,11},{4,36},{5,13},{6,38},{7,15},{8,40},{9,1... | collective-permute-start | bytes 172040 | tf_op jit(solution)/shard_map/ppermute | solution.py:262
  9.6 1.9 %collective-permute-done.2 = f32[112,128]{1,0:T(8,128)S(1)} collective-permute-done((f32[112,128]{1,0:T(8,128)S(1)}, f32[112,128]{1,0:T(8,128)S(1)}, u32[]{:S(2)}, u32[]{:S(2)}) %collective-permute-start.2) | collective-permute-done | bytes 57376 | tf_op jit(solution)/shard_map/ppermute | solution.py:262
  11.5 0.9 %collective-permute-done.3 = f32[112,128]{1,0:T(8,128)S(1)} collective-permute-done((f32[112,128]{1,0:T(8,128)S(1)}, f32[112,128]{1,0:T(8,128)S(1)}, u32[]{:S(2)}, u32[]{:S(2)}) %collective-permute-start.3) | collective-permute-done | bytes 57376 | tf_op jit(solution)/shard_map/ppermute | solution.py:262
  12.4 0.0 collective-permute-done.1
  12.4 3.1 %collective-permute-start.6 = (f32[112,128]{1,0:T(8,128)S(1)}, f32[112,128]{1,0:T(8,128)S(1)}, u32[]{:S(2)}, u32[]{:S(2)}) collective-permute-start(f32[112,128]{1,0:T(8,128)S(1)} %add_add_fusion.1), channel_id=1, source_target_pairs={{0,8},{1,65},{2,10},{3,67},{4,12},{5,69},{6,14},{7,71},{8,0},{9,73... | collective-permute-start | bytes 172040 | tf_op jit(solution)/shard_map/ppermute | solution.py:262
  15.5 1.5 %collective-permute-start.5 = (f32[112,128]{1,0:T(8,128)S(1)}, f32[112,128]{1,0:T(8,128)S(1)}, u32[]{:S(2)}, u32[]{:S(2)}) collective-permute-start(f32[112,128]{1,0:T(8,128)S(1)} %add_add_fusion.1), channel_id=1, source_target_pairs={{0,8},{1,97},{2,10},{3,99},{4,12},{5,101},{6,14},{7,103},{8,0},{9,... | collective-permute-start | bytes 172040 | tf_op jit(solution)/shard_map/ppermute | solution.py:262
  16.9 0.2 collective-permute-start.4
  17.1 0.0 collective-permute-done.6
  17.1 3.3 %collective-permute-done.5 = f32[112,128]{1,0:T(8,128)S(1)} collective-permute-done((f32[112,128]{1,0:T(8,128)S(1)}, f32[112,128]{1,0:T(8,128)S(1)}, u32[]{:S(2)}, u32[]{:S(2)}) %collective-permute-start.5) | collective-permute-done | bytes 57376 | tf_op jit(solution)/shard_map/ppermute | solution.py:262
  20.5 0.1 collective-permute-done.4
  20.6 3.7 %collective-permute-start.7 = (f32[112,128]{1,0:T(8,128)S(1)}, f32[112,128]{1,0:T(8,128)S(1)}, u32[]{:S(2)}, u32[]{:S(2)}) collective-permute-start(f32[112,128]{1,0:T(8,128)S(1)} %add_add_fusion), channel_id=1, source_target_pairs={{0,8},{1,193},{2,10},{3,195},{4,12},{5,197},{6,14},{7,199},{8,0},{... | collective-permute-start | bytes 172040 | tf_op jit(solution)/shard_map/ppermute | solution.py:262
  24.3 1.6 %collective-permute-done.7 = f32[112,128]{1,0:T(8,128)S(1)} collective-permute-done((f32[112,128]{1,0:T(8,128)S(1)}, f32[112,128]{1,0:T(8,128)S(1)}, u32[]{:S(2)}, u32[]{:S(2)}) %collective-permute-start.7) | collective-permute-done | bytes 57376 | tf_op jit(solution)/shard_map/ppermute | solution.py:262
  26.0 2.8 %collective-permute-start.8 = (f32[112,128]{1,0:T(8,128)S(1)}, f32[112,128]{1,0:T(8,128)S(1)}, u32[]{:S(2)}, u32[]{:S(2)}) collective-permute-start(f32[112,128]{1,0:T(8,128)S(1)} %add.77), channel_id=1, source_target_pairs={{0,8},{1,5},{2,10},{3,7},{4,12},{5,1},{6,14},{7,3},{8,0},{9,13},{1... | collective-permute-start | bytes 172040 | tf_op jit(solution)/shard_map/ppermute | solution.py:262
  28.8 1.4 %momentum.1 = (bf16[128,3456]{1,0:T(8,128)(2,1)}, bf16[128,48]{1,0:T(8,128)(2,1)S(1)}) custom-call(bf16[256,3456]{1,0:T(8,128)(2,1)S(1)} %get-tuple-element.13.both, f32[56,128]{1,0:T(8,128)S(1)} %get-tuple-element.12.c_ref, f32[16,128]{1,0:T(8,128)S(1)} %get-tuple-element.14.row_ref, bf16[128,128]{1,0:T(8,128)(2,1)S(1)} %get-tuple-element.15.high_ref, ...), custom_call_target="tpu_custom_call" | custom-call | flops 42467328 | bytes 884736 | tf_op jit(solution)/shard_map/momentum/pallas_call | solution.py:228
  30.2 0.4 %collective-permute-done.8 = f32[112,128]{1,0:T(8,128)S(1)} collective-permute-done((f32[112,128]{1,0:T(8,128)S(1)}, f32[112,128]{1,0:T(8,128)S(1)}, u32[]{:S(2)}, u32[]{:S(2)}) %collective-permute-start.8) | collective-permute-done | bytes 57376 | tf_op jit(solution)/shard_map/ppermute | solution.py:262
  30.6 1.3 %collective-permute-start.9 = (f32[8,128]{1,0:T(8,128)S(1)}, f32[8,128]{1,0:T(8,128)S(1)}, u32[]{:S(2)}, u32[]{:S(2)}) collective-permute-start(f32[8,128]{1,0:T(8,128)S(1)} %slice_add_fusion), channel_id=1, source_target_pairs={{0,2},{1,3},{2,0},{3,1},{4,6},{5,7},{6,4},{7,5},{8,10},{9,11},{10,... | collective-permute-start | bytes 12296 | tf_op jit(solution)/shard_map/ppermute | solution.py:262
  31.9 1.2 %collective-permute-done.9 = f32[8,128]{1,0:T(8,128)S(1)} collective-permute-done((f32[8,128]{1,0:T(8,128)S(1)}, f32[8,128]{1,0:T(8,128)S(1)}, u32[]{:S(2)}, u32[]{:S(2)}) %collective-permute-start.9) | collective-permute-done | bytes 4128 | tf_op jit(solution)/shard_map/ppermute | solution.py:262
  33.2 0.1 collective-permute-start.10
  33.3 1.6 %update.2.refs_0_ = f32[128,3456]{1,0:T(8,128)} custom-call(f32[56,128]{1,0:T(8,128)S(1)} %get-tuple-element.24.total_ref, f32[8,128]{1,0:T(8,128)S(1)} %fusion.2.squares_ref, bf16[128,48]{1,0:T(8,128)(2,1)S(1)} %get-tuple-element.21.row_ref, bf16[128,128]{1,0:T(8,128)(2,1)S(1)} %get-tuple-element.15.high_ref, bf16[128,128]{1,0:T(8,128)(2,1)S(1)} %get-tuple-element.16.low_ref), custom_call_target="tpu_custom_call" | custom-call | flops 42467328 | bytes 1769472 | tf_op jit(solution)/shard_map/update/pallas_call | solution.py:243
  34.9 0.0 collective-permute-done.10
  (13 shorter events, 0.2 us)
Async XLA Ops:
  2.7 4.2 %collective-permute-start = (f32[56,128]{1,0:T(8,128)S(1)}, f32[56,128]{1,0:T(8,128)S(1)}, u32[]{:S(2)}, u32[]{:S(2)}) collective-permute-start(f32[56,128]{1,0:T(8,128)S(1)} %get-tuple-element.12.c_ref), channel_id=1, source_target_pairs={{0,1},{1,0},{2,3},{3,2},{4,5},{5,4},{6,7},{7,6},{8,9},{9,8},{10,11... | collective-permute-start | bytes 86024 | tf_op jit(solution)/shard_map/ppermute | solution.py:262
  6.9 4.6 %collective-permute-start.2 = (f32[112,128]{1,0:T(8,128)S(1)}, f32[112,128]{1,0:T(8,128)S(1)}, u32[]{:S(2)}, u32[]{:S(2)}) collective-permute-start(f32[112,128]{1,0:T(8,128)S(1)} %pad_maximum_fusion), channel_id=1, source_target_pairs={{0,32},{1,17},{2,34},{3,19},{4,36},{5,21},{6,38},{7,23},{8,40},{9,... | collective-permute-start | bytes 172040 | tf_op jit(solution)/shard_map/ppermute | solution.py:262
  8.1 4.2 %collective-permute-start.3 = (f32[112,128]{1,0:T(8,128)S(1)}, f32[112,128]{1,0:T(8,128)S(1)}, u32[]{:S(2)}, u32[]{:S(2)}) collective-permute-start(f32[112,128]{1,0:T(8,128)S(1)} %pad_maximum_fusion), channel_id=1, source_target_pairs={{0,32},{1,25},{2,34},{3,27},{4,36},{5,29},{6,38},{7,31},{8,40},{9,... | collective-permute-start | bytes 172040 | tf_op jit(solution)/shard_map/ppermute | solution.py:262
  8.9 3.5 %collective-permute-start.1 = (f32[112,128]{1,0:T(8,128)S(1)}, f32[112,128]{1,0:T(8,128)S(1)}, u32[]{:S(2)}, u32[]{:S(2)}) collective-permute-start(f32[112,128]{1,0:T(8,128)S(1)} %pad_maximum_fusion), channel_id=1, source_target_pairs={{0,32},{1,9},{2,34},{3,11},{4,36},{5,13},{6,38},{7,15},{8,40},{9,1... | collective-permute-start | bytes 172040 | tf_op jit(solution)/shard_map/ppermute | solution.py:262
  12.4 4.7 %collective-permute-start.6 = (f32[112,128]{1,0:T(8,128)S(1)}, f32[112,128]{1,0:T(8,128)S(1)}, u32[]{:S(2)}, u32[]{:S(2)}) collective-permute-start(f32[112,128]{1,0:T(8,128)S(1)} %add_add_fusion.1), channel_id=1, source_target_pairs={{0,8},{1,65},{2,10},{3,67},{4,12},{5,69},{6,14},{7,71},{8,0},{9,73... | collective-permute-start | bytes 172040 | tf_op jit(solution)/shard_map/ppermute | solution.py:262
  15.5 5.0 %collective-permute-start.5 = (f32[112,128]{1,0:T(8,128)S(1)}, f32[112,128]{1,0:T(8,128)S(1)}, u32[]{:S(2)}, u32[]{:S(2)}) collective-permute-start(f32[112,128]{1,0:T(8,128)S(1)} %add_add_fusion.1), channel_id=1, source_target_pairs={{0,8},{1,97},{2,10},{3,99},{4,12},{5,101},{6,14},{7,103},{8,0},{9,... | collective-permute-start | bytes 172040 | tf_op jit(solution)/shard_map/ppermute | solution.py:262
  16.9 3.6 %collective-permute-start.4 = (f32[112,128]{1,0:T(8,128)S(1)}, f32[112,128]{1,0:T(8,128)S(1)}, u32[]{:S(2)}, u32[]{:S(2)}) collective-permute-start(f32[112,128]{1,0:T(8,128)S(1)} %add_add_fusion.1), channel_id=1, source_target_pairs={{0,8},{1,33},{2,10},{3,35},{4,12},{5,37},{6,14},{7,39},{8,0},{9,41... | collective-permute-start | bytes 172040 | tf_op jit(solution)/shard_map/ppermute | solution.py:262
  20.6 5.3 %collective-permute-start.7 = (f32[112,128]{1,0:T(8,128)S(1)}, f32[112,128]{1,0:T(8,128)S(1)}, u32[]{:S(2)}, u32[]{:S(2)}) collective-permute-start(f32[112,128]{1,0:T(8,128)S(1)} %add_add_fusion), channel_id=1, source_target_pairs={{0,8},{1,193},{2,10},{3,195},{4,12},{5,197},{6,14},{7,199},{8,0},{... | collective-permute-start | bytes 172040 | tf_op jit(solution)/shard_map/ppermute | solution.py:262
  26.0 4.6 %collective-permute-start.8 = (f32[112,128]{1,0:T(8,128)S(1)}, f32[112,128]{1,0:T(8,128)S(1)}, u32[]{:S(2)}, u32[]{:S(2)}) collective-permute-start(f32[112,128]{1,0:T(8,128)S(1)} %add.77), channel_id=1, source_target_pairs={{0,8},{1,5},{2,10},{3,7},{4,12},{5,1},{6,14},{7,3},{8,0},{9,13},{1... | collective-permute-start | bytes 172040 | tf_op jit(solution)/shard_map/ppermute | solution.py:262
  30.6 2.5 %collective-permute-start.9 = (f32[8,128]{1,0:T(8,128)S(1)}, f32[8,128]{1,0:T(8,128)S(1)}, u32[]{:S(2)}, u32[]{:S(2)}) collective-permute-start(f32[8,128]{1,0:T(8,128)S(1)} %slice_add_fusion), channel_id=1, source_target_pairs={{0,2},{1,3},{2,0},{3,1},{4,6},{5,7},{6,4},{7,5},{8,10},{9,11},{10,... | collective-permute-start | bytes 12296 | tf_op jit(solution)/shard_map/ppermute | solution.py:262
  33.2 1.7 %collective-permute-start.10 = (f32[64,128]{1,0:T(8,128)S(1)}, f32[64,128]{1,0:T(8,128)S(1)}, u32[]{:S(2)}, u32[]{:S(2)}) collective-permute-start(f32[64,128]{1,0:T(8,128)S(1)} %pad_maximum_fusion.1), channel_id=1, source_target_pairs={{0,1},{1,0},{2,3},{3,2},{4,5},{5,4},{6,7},{7,6},{8,9},{9,8},{10,11... | collective-permute-start | bytes 98312 | tf_op jit(solution)/shard_map/ppermute | solution.py:262

commit v6 on v5

--- a/solution.py
+++ b/solution.py
@@ -284,6 +284,15 @@
     return (v + moved(v, replica(*a))) + (moved(v, replica(*b)) + moved(v, replica(*both)))
 
 
+def ring(dx, dnear):
+    def partner(z, y, x, near, core):
+        if core == 0:
+            return z, y ^ 1, x, near, core
+        return z, y, x ^ dx, near ^ dnear, core
+
+    return partner
+
+
 def body(momentum, grad, freq_rows, freq_cols):
     m, g = momentum[0], grad[0]
     rows, cols = m.shape
@@ -297,11 +306,14 @@
     pair = four_way(pair, (1, 0, 0), (3, 0, 0))
     pair = pair + moved(pair, replica(6, 0, 0))
     kept, turned = momentum_left(both, own, row, high, low)
-    other, kept, turned = lax.optimization_barrier((moved(pair, replica(0, 0, 1)), kept, turned))
-    pair = pair + other
-    squares = pair * pair
+    got = {}
+    for dx, dnear in [(0, 1), (1, 0), (1, 1)]:
+        got[dx, dnear] = moved(pair, ring(dx, dnear))
+    got, kept, turned = lax.optimization_barrier((got, kept, turned))
+    pair = pair + got[1, 0]
+    beside = got[0, 1] + got[1, 1]
+    squares = pair * pair + beside * beside
     squares = sum(squares[k : k + KEEP] for k in range(0, 2 * count, KEEP))
-    squares = squares + moved(squares, next_chip)
     entries = float(rows * cols * tp)
     sent = moved(jnp.concatenate([pair[:count], squares], axis=0), other_core)
     update = updated(1, pair[count:], squares, turned, high, low, cols, entries)

time: 35.1 us -> 35 us (level)
  waiting for transfers between devices: 10.3 us -> 11.1 us
  starting transfers between devices: 18.7 us -> 18 us
    ppermute x11 -> x12, starting transfers between devices: 18.7 us -> 18 us  [moved(): return lax.ppermute(v, ('rep', 'tp'), pairs)]
    ppermute x11 -> x12, waiting for transfers between devices: 10.3 us -> 11.1 us  [moved(): return lax.ppermute(v, ('rep', 'tp'), pairs)]
  transfers between devices with their start and end apart: 11 -> 12, of which waited for: 8 -> 7; matrix products, arithmetic and copies ran while one was open for 0% -> 0% of each run, Pallas kernels for 9% -> 9%
where the time goes in v6:
time: 35 us; the launch traced here: 34.9 us
  starting transfers between devices  18 us (51%)
  waiting for transfers between devices  11.1 us (32%)
  Pallas kernels  5.08 us (15%)
  between operations  0.73 us (2%)
    ppermute x12, starting transfers between devices, moved(): return lax.ppermute(v, ('rep', 'tp'), pairs)  18 us
    ppermute x12, waiting for transfers between devices, moved(): return lax.ppermute(v, ('rep', 'tp'), pairs)  11.1 us
    pallas_call x1, Pallas kernels, forward(): pl.pallas_call(forward_kernel, out_shape=[jax.ShapeDtypeStruct((packed_ro...  2.05 us
    pallas_call x2, Pallas kernels, updated(): pl.pallas_call(functools.partial(update_kernel, entries, core), out_shape...  1.66 us
    pallas_call x1, Pallas kernels, momentum_left(): pl.pallas_call(momentum_kernel, out_shape=[jax.ShapeDtypeStruct((rows, co...  1.37 us
  transfers between devices with their start and end apart: 12, of which 7 were waited for; matrix products, arithmetic and copies ran while one was open for 0% of the time, Pallas kernels for 9%

profile of v6, /device:TPU:1, one launch (start us, length us, event | category | flops | bytes accessed | tf_op | source)
XLA Modules:
  0.0 34.9 jit_solution(9973659153076969771)
XLA Ops:
  0.6 2.0 %forward.1 = (f32[56,128]{1,0:T(8,128)S(1)}, f32[16,128]{1,0:T(8,128)S(1)}, bf16[128,128]{1,0:T(8,128)(2,1)S(1)}, bf16[128,128]{1,0:T(8,128)(2,1)S(1)}, bf16[256,3456]{1,0:T(8,128)(2,1)S(1)}) custom-call(s32[8]{0:T(128)} %fr_ref.1, s32[8]{0:T(128)} %fc_ref.1, bf16[128,3456]{1,0:T(8,128)(2,1)} %bitcast.3, bf16[128,3456]{1,0:T(8,128)(2,1)} %bitcast.4), custom_call_target="tpu_custom_call" | custom-call | flops 42467328 | bytes 1769472 | tf_op jit(solution)/shard_map/forward/pallas_call | solution.py:202
  2.7 3.3 %collective-permute-start = (f32[56,128]{1,0:T(8,128)S(1)}, f32[56,128]{1,0:T(8,128)S(1)}, u32[]{:S(2)}, u32[]{:S(2)}) collective-permute-start(f32[56,128]{1,0:T(8,128)S(1)} %get-tuple-element.14.c_ref), channel_id=1, source_target_pairs={{0,1},{1,0},{2,3},{3,2},{4,5},{5,4},{6,7},{7,6},{8,9},{9,8},{10,11... | collective-permute-start | bytes 86024 | tf_op jit(solution)/shard_map/ppermute | solution.py:262
  6.0 0.9 %collective-permute-done = f32[56,128]{1,0:T(8,128)S(1)} collective-permute-done((f32[56,128]{1,0:T(8,128)S(1)}, f32[56,128]{1,0:T(8,128)S(1)}, u32[]{:S(2)}, u32[]{:S(2)}) %collective-permute-start) | collective-permute-done | bytes 28704 | tf_op jit(solution)/shard_map/ppermute | solution.py:262
  6.9 1.3 %collective-permute-start.2 = (f32[112,128]{1,0:T(8,128)S(1)}, f32[112,128]{1,0:T(8,128)S(1)}, u32[]{:S(2)}, u32[]{:S(2)}) collective-permute-start(f32[112,128]{1,0:T(8,128)S(1)} %pad_maximum_fusion), channel_id=1, source_target_pairs={{0,32},{1,17},{2,34},{3,19},{4,36},{5,21},{6,38},{7,23},{8,40},{9,... | collective-permute-start | bytes 172040 | tf_op jit(solution)/shard_map/ppermute | solution.py:262
  8.1 0.8 %collective-permute-start.3 = (f32[112,128]{1,0:T(8,128)S(1)}, f32[112,128]{1,0:T(8,128)S(1)}, u32[]{:S(2)}, u32[]{:S(2)}) collective-permute-start(f32[112,128]{1,0:T(8,128)S(1)} %pad_maximum_fusion), channel_id=1, source_target_pairs={{0,32},{1,25},{2,34},{3,27},{4,36},{5,29},{6,38},{7,31},{8,40},{9,... | collective-permute-start | bytes 172040 | tf_op jit(solution)/shard_map/ppermute | solution.py:262
  8.9 0.7 %collective-permute-start.1 = (f32[112,128]{1,0:T(8,128)S(1)}, f32[112,128]{1,0:T(8,128)S(1)}, u32[]{:S(2)}, u32[]{:S(2)}) collective-permute-start(f32[112,128]{1,0:T(8,128)S(1)} %pad_maximum_fusion), channel_id=1, source_target_pairs={{0,32},{1,9},{2,34},{3,11},{4,36},{5,13},{6,38},{7,15},{8,40},{9,1... | collective-permute-start | bytes 172040 | tf_op jit(solution)/shard_map/ppermute | solution.py:262
  9.6 1.9 %collective-permute-done.2 = f32[112,128]{1,0:T(8,128)S(1)} collective-permute-done((f32[112,128]{1,0:T(8,128)S(1)}, f32[112,128]{1,0:T(8,128)S(1)}, u32[]{:S(2)}, u32[]{:S(2)}) %collective-permute-start.2) | collective-permute-done | bytes 57376 | tf_op jit(solution)/shard_map/ppermute | solution.py:262
  11.5 0.9 %collective-permute-done.3 = f32[112,128]{1,0:T(8,128)S(1)} collective-permute-done((f32[112,128]{1,0:T(8,128)S(1)}, f32[112,128]{1,0:T(8,128)S(1)}, u32[]{:S(2)}, u32[]{:S(2)}) %collective-permute-start.3) | collective-permute-done | bytes 57376 | tf_op jit(solution)/shard_map/ppermute | solution.py:262
  12.4 0.0 collective-permute-done.1
  12.4 3.1 %collective-permute-start.6 = (f32[112,128]{1,0:T(8,128)S(1)}, f32[112,128]{1,0:T(8,128)S(1)}, u32[]{:S(2)}, u32[]{:S(2)}) collective-permute-start(f32[112,128]{1,0:T(8,128)S(1)} %add_add_fusion.1), channel_id=1, source_target_pairs={{0,8},{1,65},{2,10},{3,67},{4,12},{5,69},{6,14},{7,71},{8,0},{9,73... | collective-permute-start | bytes 172040 | tf_op jit(solution)/shard_map/ppermute | solution.py:262
  15.5 1.5 %collective-permute-start.5 = (f32[112,128]{1,0:T(8,128)S(1)}, f32[112,128]{1,0:T(8,128)S(1)}, u32[]{:S(2)}, u32[]{:S(2)}) collective-permute-start(f32[112,128]{1,0:T(8,128)S(1)} %add_add_fusion.1), channel_id=1, source_target_pairs={{0,8},{1,97},{2,10},{3,99},{4,12},{5,101},{6,14},{7,103},{8,0},{9,... | collective-permute-start | bytes 172040 | tf_op jit(solution)/shard_map/ppermute | solution.py:262
  16.9 0.2 collective-permute-start.4
  17.1 0.0 collective-permute-done.6
  17.1 3.3 %collective-permute-done.5 = f32[112,128]{1,0:T(8,128)S(1)} collective-permute-done((f32[112,128]{1,0:T(8,128)S(1)}, f32[112,128]{1,0:T(8,128)S(1)}, u32[]{:S(2)}, u32[]{:S(2)}) %collective-permute-start.5) | collective-permute-done | bytes 57376 | tf_op jit(solution)/shard_map/ppermute | solution.py:262
  20.5 0.1 collective-permute-done.4
  20.6 3.7 %collective-permute-start.7 = (f32[112,128]{1,0:T(8,128)S(1)}, f32[112,128]{1,0:T(8,128)S(1)}, u32[]{:S(2)}, u32[]{:S(2)}) collective-permute-start(f32[112,128]{1,0:T(8,128)S(1)} %add_add_fusion), channel_id=1, source_target_pairs={{0,8},{1,193},{2,10},{3,195},{4,12},{5,197},{6,14},{7,199},{8,0},{... | collective-permute-start | bytes 172040 | tf_op jit(solution)/shard_map/ppermute | solution.py:262
  24.3 1.6 %collective-permute-done.7 = f32[112,128]{1,0:T(8,128)S(1)} collective-permute-done((f32[112,128]{1,0:T(8,128)S(1)}, f32[112,128]{1,0:T(8,128)S(1)}, u32[]{:S(2)}, u32[]{:S(2)}) %collective-permute-start.7) | collective-permute-done | bytes 57376 | tf_op jit(solution)/shard_map/ppermute | solution.py:262
  26.0 2.6 %collective-permute-start.10 = (f32[112,128]{1,0:T(8,128)S(1)}, f32[112,128]{1,0:T(8,128)S(1)}, u32[]{:S(2)}, u32[]{:S(2)}) collective-permute-start(f32[112,128]{1,0:T(8,128)S(1)} %add.80), channel_id=1, source_target_pairs={{0,8},{1,7},{2,10},{3,5},{4,12},{5,3},{6,14},{7,1},{8,0},{9,15},{1... | collective-permute-start | bytes 172040 | tf_op jit(solution)/shard_map/ppermute | solution.py:262
  28.5 0.5 %collective-permute-start.9 = (f32[112,128]{1,0:T(8,128)S(1)}, f32[112,128]{1,0:T(8,128)S(1)}, u32[]{:S(2)}, u32[]{:S(2)}) collective-permute-start(f32[112,128]{1,0:T(8,128)S(1)} %add.80), channel_id=1, source_target_pairs={{0,8},{1,5},{2,10},{3,7},{4,12},{5,1},{6,14},{7,3},{8,0},{9,13},{1... | collective-permute-start | bytes 172040 | tf_op jit(solution)/shard_map/ppermute | solution.py:262
  29.0 0.3 collective-permute-start.8
  29.3 1.4 %momentum.1 = (bf16[128,3456]{1,0:T(8,128)(2,1)}, bf16[128,48]{1,0:T(8,128)(2,1)S(1)}) custom-call(bf16[256,3456]{1,0:T(8,128)(2,1)S(1)} %get-tuple-element.15.both, f32[56,128]{1,0:T(8,128)S(1)} %get-tuple-element.14.c_ref, f32[16,128]{1,0:T(8,128)S(1)} %get-tuple-element.16.row_ref, bf16[128,128]{1,0:T(8,128)(2,1)S(1)} %get-tuple-element.17.high_ref, ...), custom_call_target="tpu_custom_call" | custom-call | flops 42467328 | bytes 884736 | tf_op jit(solution)/shard_map/momentum/pallas_call | solution.py:228
  30.7 0.0 collective-permute-done.10
  30.7 2.4 %collective-permute-done.9 = f32[112,128]{1,0:T(8,128)S(1)} collective-permute-done((f32[112,128]{1,0:T(8,128)S(1)}, f32[112,128]{1,0:T(8,128)S(1)}, u32[]{:S(2)}, u32[]{:S(2)}) %collective-permute-start.9) | collective-permute-done | bytes 57376 | tf_op jit(solution)/shard_map/ppermute | solution.py:262
  33.1 0.0 collective-permute-done.8
  33.1 0.1 collective-permute-start.11
  33.2 1.6 %update.2.refs_0_ = f32[128,3456]{1,0:T(8,128)} custom-call(f32[56,128]{1,0:T(8,128)S(1)} %get-tuple-element.28.total_ref, f32[8,128]{1,0:T(8,128)S(1)} %slice_add_fusion.squares_ref, bf16[128,48]{1,0:T(8,128)(2,1)S(1)} %get-tuple-element.25.row_ref, bf16[128,128]{1,0:T(8,128)(2,1)S(1)} %get-tuple-element.17.high_ref, ...), custom_call_target="tpu_custom_call" | custom-call | flops 42467328 | bytes 1769472 | tf_op jit(solution)/shard_map/update/pallas_call | solution.py:243
  34.9 0.0 collective-permute-done.11
  (12 shorter events, 0.2 us)
Async XLA Ops:
  2.7 4.2 %collective-permute-start = (f32[56,128]{1,0:T(8,128)S(1)}, f32[56,128]{1,0:T(8,128)S(1)}, u32[]{:S(2)}, u32[]{:S(2)}) collective-permute-start(f32[56,128]{1,0:T(8,128)S(1)} %get-tuple-element.14.c_ref), channel_id=1, source_target_pairs={{0,1},{1,0},{2,3},{3,2},{4,5},{5,4},{6,7},{7,6},{8,9},{9,8},{10,11... | collective-permute-start | bytes 86024 | tf_op jit(solution)/shard_map/ppermute | solution.py:262
  6.9 4.6 %collective-permute-start.2 = (f32[112,128]{1,0:T(8,128)S(1)}, f32[112,128]{1,0:T(8,128)S(1)}, u32[]{:S(2)}, u32[]{:S(2)}) collective-permute-start(f32[112,128]{1,0:T(8,128)S(1)} %pad_maximum_fusion), channel_id=1, source_target_pairs={{0,32},{1,17},{2,34},{3,19},{4,36},{5,21},{6,38},{7,23},{8,40},{9,... | collective-permute-start | bytes 172040 | tf_op jit(solution)/shard_map/ppermute | solution.py:262
  8.1 4.2 %collective-permute-start.3 = (f32[112,128]{1,0:T(8,128)S(1)}, f32[112,128]{1,0:T(8,128)S(1)}, u32[]{:S(2)}, u32[]{:S(2)}) collective-permute-start(f32[112,128]{1,0:T(8,128)S(1)} %pad_maximum_fusion), channel_id=1, source_target_pairs={{0,32},{1,25},{2,34},{3,27},{4,36},{5,29},{6,38},{7,31},{8,40},{9,... | collective-permute-start | bytes 172040 | tf_op jit(solution)/shard_map/ppermute | solution.py:262
  8.9 3.5 %collective-permute-start.1 = (f32[112,128]{1,0:T(8,128)S(1)}, f32[112,128]{1,0:T(8,128)S(1)}, u32[]{:S(2)}, u32[]{:S(2)}) collective-permute-start(f32[112,128]{1,0:T(8,128)S(1)} %pad_maximum_fusion), channel_id=1, source_target_pairs={{0,32},{1,9},{2,34},{3,11},{4,36},{5,13},{6,38},{7,15},{8,40},{9,1... | collective-permute-start | bytes 172040 | tf_op jit(solution)/shard_map/ppermute | solution.py:262
  12.4 4.7 %collective-permute-start.6 = (f32[112,128]{1,0:T(8,128)S(1)}, f32[112,128]{1,0:T(8,128)S(1)}, u32[]{:S(2)}, u32[]{:S(2)}) collective-permute-start(f32[112,128]{1,0:T(8,128)S(1)} %add_add_fusion.1), channel_id=1, source_target_pairs={{0,8},{1,65},{2,10},{3,67},{4,12},{5,69},{6,14},{7,71},{8,0},{9,73... | collective-permute-start | bytes 172040 | tf_op jit(solution)/shard_map/ppermute | solution.py:262
  15.5 5.0 %collective-permute-start.5 = (f32[112,128]{1,0:T(8,128)S(1)}, f32[112,128]{1,0:T(8,128)S(1)}, u32[]{:S(2)}, u32[]{:S(2)}) collective-permute-start(f32[112,128]{1,0:T(8,128)S(1)} %add_add_fusion.1), channel_id=1, source_target_pairs={{0,8},{1,97},{2,10},{3,99},{4,12},{5,101},{6,14},{7,103},{8,0},{9,... | collective-permute-start | bytes 172040 | tf_op jit(solution)/shard_map/ppermute | solution.py:262
  16.9 3.6 %collective-permute-start.4 = (f32[112,128]{1,0:T(8,128)S(1)}, f32[112,128]{1,0:T(8,128)S(1)}, u32[]{:S(2)}, u32[]{:S(2)}) collective-permute-start(f32[112,128]{1,0:T(8,128)S(1)} %add_add_fusion.1), channel_id=1, source_target_pairs={{0,8},{1,33},{2,10},{3,35},{4,12},{5,37},{6,14},{7,39},{8,0},{9,41... | collective-permute-start | bytes 172040 | tf_op jit(solution)/shard_map/ppermute | solution.py:262
  20.6 5.3 %collective-permute-start.7 = (f32[112,128]{1,0:T(8,128)S(1)}, f32[112,128]{1,0:T(8,128)S(1)}, u32[]{:S(2)}, u32[]{:S(2)}) collective-permute-start(f32[112,128]{1,0:T(8,128)S(1)} %add_add_fusion), channel_id=1, source_target_pairs={{0,8},{1,193},{2,10},{3,195},{4,12},{5,197},{6,14},{7,199},{8,0},{... | collective-permute-start | bytes 172040 | tf_op jit(solution)/shard_map/ppermute | solution.py:262
  26.0 4.7 %collective-permute-start.10 = (f32[112,128]{1,0:T(8,128)S(1)}, f32[112,128]{1,0:T(8,128)S(1)}, u32[]{:S(2)}, u32[]{:S(2)}) collective-permute-start(f32[112,128]{1,0:T(8,128)S(1)} %add.80), channel_id=1, source_target_pairs={{0,8},{1,7},{2,10},{3,5},{4,12},{5,3},{6,14},{7,1},{8,0},{9,15},{1... | collective-permute-start | bytes 172040 | tf_op jit(solution)/shard_map/ppermute | solution.py:262
  28.5 4.5 %collective-permute-start.9 = (f32[112,128]{1,0:T(8,128)S(1)}, f32[112,128]{1,0:T(8,128)S(1)}, u32[]{:S(2)}, u32[]{:S(2)}) collective-permute-start(f32[112,128]{1,0:T(8,128)S(1)} %add.80), channel_id=1, source_target_pairs={{0,8},{1,5},{2,10},{3,7},{4,12},{5,1},{6,14},{7,3},{8,0},{9,13},{1... | collective-permute-start | bytes 172040 | tf_op jit(solution)/shard_map/ppermute | solution.py:262
  29.0 4.0 %collective-permute-start.8 = (f32[112,128]{1,0:T(8,128)S(1)}, f32[112,128]{1,0:T(8,128)S(1)}, u32[]{:S(2)}, u32[]{:S(2)}) collective-permute-start(f32[112,128]{1,0:T(8,128)S(1)} %add.80), channel_id=1, source_target_pairs={{0,8},{1,3},{2,10},{3,1},{4,12},{5,7},{6,14},{7,5},{8,0},{9,11},{1... | collective-permute-start | bytes 172040 | tf_op jit(solution)/shard_map/ppermute | solution.py:262
  33.1 1.7 %collective-permute-start.11 = (f32[64,128]{1,0:T(8,128)S(1)}, f32[64,128]{1,0:T(8,128)S(1)}, u32[]{:S(2)}, u32[]{:S(2)}) collective-permute-start(f32[64,128]{1,0:T(8,128)S(1)} %pad_maximum_fusion.1), channel_id=1, source_target_pairs={{0,1},{1,0},{2,3},{3,2},{4,5},{5,4},{6,7},{7,6},{8,9},{9,8},{10,11... | collective-permute-start | bytes 98312 | tf_op jit(solution)/shard_map/ppermute | solution.py:262

commit v7 on v5

--- a/solution.py
+++ b/solution.py
@@ -15,7 +15,7 @@
 VMEM_BYTES = 16 * 1024 * 1024
 TILES = SPAN // LANES
 WRITES = [(0, 512), (512, 1024), (1536, 1920)]
-READS = [(0, 2048), (2048, 1408)]
+READS = [(0, 1536), (1536, 1920)]
 
 
 def spans(cols):
@@ -111,8 +111,9 @@
         high_tiles += [high[:, k : k + LANES] for k in range(0, width, LANES)]
         low_tiles += [low[:, k : k + LANES] for k in range(0, width, LANES)]
     y_high = jnp.concatenate(high_tiles, axis=0)
-    c = dot(jnp.concatenate([y_high] + low_tiles, axis=0), high_ref[...], ((1,), (1,)))
-    c = c[: y_high.shape[0]] + c[y_high.shape[0] :] + dot(y_high, low_ref[...], ((1,), (1,)))
+    y_both = jnp.concatenate([y_high, jnp.concatenate(low_tiles, axis=0)], axis=1)
+    c = dot(y_both, jnp.concatenate([high_ref[...]] * 2, axis=1), ((1,), (1,)))
+    c = c + dot(y_high, low_ref[...], ((1,), (1,)))
     sums = []
     for first in range(0, cols // LANES, TILES):
         parts = [only(t - first, c[16 * t : 16 * t + 16]) for t in range(first, min(first + TILES, cols // LANES))]

time: 35.1 us -> 35 us (level)
  transfers between devices with their start and end apart: 11 -> 11, of which waited for: 8 -> 8; matrix products, arithmetic and copies ran while one was open for 0% -> 0% of each run, Pallas kernels for 9% -> 8%
where the time goes in v7:
time: 35 us; the launch traced here: 34.9 us
  starting transfers between devices  18.8 us (54%)
  waiting for transfers between devices  10.3 us (29%)
  Pallas kernels  4.98 us (14%)
  between operations  0.71 us (2%)
    ppermute x11, starting transfers between devices, moved(): return lax.ppermute(v, ('rep', 'tp'), pairs)  18.8 us
    ppermute x11, waiting for transfers between devices, moved(): return lax.ppermute(v, ('rep', 'tp'), pairs)  10.3 us
    pallas_call x1, Pallas kernels, forward(): pl.pallas_call(forward_kernel, out_shape=[jax.ShapeDtypeStruct((packed_ro...  1.97 us
    pallas_call x2, Pallas kernels, updated(): pl.pallas_call(functools.partial(update_kernel, entries, core), out_shape...  1.64 us
    pallas_call x1, Pallas kernels, momentum_left(): pl.pallas_call(momentum_kernel, out_shape=[jax.ShapeDtypeStruct((rows, co...  1.36 us
  transfers between devices with their start and end apart: 11, of which 8 were waited for; matrix products, arithmetic and copies ran while one was open for 0% of the time, Pallas kernels for 8%

profile of v7, /device:TPU:1, one launch (start us, length us, event | category | flops | bytes accessed | tf_op | source)
XLA Modules:
  0.0 34.9 jit_solution(4139443038842312017)
XLA Ops:
  0.6 2.0 %forward.1 = (f32[56,128]{1,0:T(8,128)S(1)}, f32[16,128]{1,0:T(8,128)S(1)}, bf16[128,128]{1,0:T(8,128)(2,1)S(1)}, bf16[128,128]{1,0:T(8,128)(2,1)S(1)}, bf16[256,3456]{1,0:T(8,128)(2,1)S(1)}) custom-call(s32[8]{0:T(128)} %fr_ref.1, s32[8]{0:T(128)} %fc_ref.1, bf16[128,3456]{1,0:T(8,128)(2,1)} %bitcast.3, bf16[128,3456]{1,0:T(8,128)(2,1)} %bitcast.4), custom_call_target="tpu_custom_call" | custom-call | flops 42467328 | bytes 1769472 | tf_op jit(solution)/shard_map/forward/pallas_call | solution.py:203
  2.6 3.3 %collective-permute-start = (f32[56,128]{1,0:T(8,128)S(1)}, f32[56,128]{1,0:T(8,128)S(1)}, u32[]{:S(2)}, u32[]{:S(2)}) collective-permute-start(f32[56,128]{1,0:T(8,128)S(1)} %get-tuple-element.12.c_ref), channel_id=1, source_target_pairs={{0,1},{1,0},{2,3},{3,2},{4,5},{5,4},{6,7},{7,6},{8,9},{9,8},{10,11... | collective-permute-start | bytes 86024 | tf_op jit(solution)/shard_map/ppermute | solution.py:263
  6.0 0.9 %collective-permute-done = f32[56,128]{1,0:T(8,128)S(1)} collective-permute-done((f32[56,128]{1,0:T(8,128)S(1)}, f32[56,128]{1,0:T(8,128)S(1)}, u32[]{:S(2)}, u32[]{:S(2)}) %collective-permute-start) | collective-permute-done | bytes 28704 | tf_op jit(solution)/shard_map/ppermute | solution.py:263
  6.8 1.3 %collective-permute-start.2 = (f32[112,128]{1,0:T(8,128)S(1)}, f32[112,128]{1,0:T(8,128)S(1)}, u32[]{:S(2)}, u32[]{:S(2)}) collective-permute-start(f32[112,128]{1,0:T(8,128)S(1)} %pad_maximum_fusion), channel_id=1, source_target_pairs={{0,32},{1,17},{2,34},{3,19},{4,36},{5,21},{6,38},{7,23},{8,40},{9,... | collective-permute-start | bytes 172040 | tf_op jit(solution)/shard_map/ppermute | solution.py:263
  8.1 0.8 %collective-permute-start.3 = (f32[112,128]{1,0:T(8,128)S(1)}, f32[112,128]{1,0:T(8,128)S(1)}, u32[]{:S(2)}, u32[]{:S(2)}) collective-permute-start(f32[112,128]{1,0:T(8,128)S(1)} %pad_maximum_fusion), channel_id=1, source_target_pairs={{0,32},{1,25},{2,34},{3,27},{4,36},{5,29},{6,38},{7,31},{8,40},{9,... | collective-permute-start | bytes 172040 | tf_op jit(solution)/shard_map/ppermute | solution.py:263
  8.9 0.7 %collective-permute-start.1 = (f32[112,128]{1,0:T(8,128)S(1)}, f32[112,128]{1,0:T(8,128)S(1)}, u32[]{:S(2)}, u32[]{:S(2)}) collective-permute-start(f32[112,128]{1,0:T(8,128)S(1)} %pad_maximum_fusion), channel_id=1, source_target_pairs={{0,32},{1,9},{2,34},{3,11},{4,36},{5,13},{6,38},{7,15},{8,40},{9,1... | collective-permute-start | bytes 172040 | tf_op jit(solution)/shard_map/ppermute | solution.py:263
  9.6 1.9 %collective-permute-done.2 = f32[112,128]{1,0:T(8,128)S(1)} collective-permute-done((f32[112,128]{1,0:T(8,128)S(1)}, f32[112,128]{1,0:T(8,128)S(1)}, u32[]{:S(2)}, u32[]{:S(2)}) %collective-permute-start.2) | collective-permute-done | bytes 57376 | tf_op jit(solution)/shard_map/ppermute | solution.py:263
  11.4 0.9 %collective-permute-done.3 = f32[112,128]{1,0:T(8,128)S(1)} collective-permute-done((f32[112,128]{1,0:T(8,128)S(1)}, f32[112,128]{1,0:T(8,128)S(1)}, u32[]{:S(2)}, u32[]{:S(2)}) %collective-permute-start.3) | collective-permute-done | bytes 57376 | tf_op jit(solution)/shard_map/ppermute | solution.py:263
  12.3 0.0 collective-permute-done.1
  12.3 3.1 %collective-permute-start.6 = (f32[112,128]{1,0:T(8,128)S(1)}, f32[112,128]{1,0:T(8,128)S(1)}, u32[]{:S(2)}, u32[]{:S(2)}) collective-permute-start(f32[112,128]{1,0:T(8,128)S(1)} %add_add_fusion.1), channel_id=1, source_target_pairs={{0,8},{1,65},{2,10},{3,67},{4,12},{5,69},{6,14},{7,71},{8,0},{9,73... | collective-permute-start | bytes 172040 | tf_op jit(solution)/shard_map/ppermute | solution.py:263
  15.4 1.5 %collective-permute-start.5 = (f32[112,128]{1,0:T(8,128)S(1)}, f32[112,128]{1,0:T(8,128)S(1)}, u32[]{:S(2)}, u32[]{:S(2)}) collective-permute-start(f32[112,128]{1,0:T(8,128)S(1)} %add_add_fusion.1), channel_id=1, source_target_pairs={{0,8},{1,97},{2,10},{3,99},{4,12},{5,101},{6,14},{7,103},{8,0},{9,... | collective-permute-start | bytes 172040 | tf_op jit(solution)/shard_map/ppermute | solution.py:263
  16.9 0.2 collective-permute-start.4
  17.1 0.0 collective-permute-done.6
  17.1 3.3 %collective-permute-done.5 = f32[112,128]{1,0:T(8,128)S(1)} collective-permute-done((f32[112,128]{1,0:T(8,128)S(1)}, f32[112,128]{1,0:T(8,128)S(1)}, u32[]{:S(2)}, u32[]{:S(2)}) %collective-permute-start.5) | collective-permute-done | bytes 57376 | tf_op jit(solution)/shard_map/ppermute | solution.py:263
  20.4 0.1 collective-permute-done.4
  20.5 3.7 %collective-permute-start.7 = (f32[112,128]{1,0:T(8,128)S(1)}, f32[112,128]{1,0:T(8,128)S(1)}, u32[]{:S(2)}, u32[]{:S(2)}) collective-permute-start(f32[112,128]{1,0:T(8,128)S(1)} %add_add_fusion), channel_id=1, source_target_pairs={{0,8},{1,193},{2,10},{3,195},{4,12},{5,197},{6,14},{7,199},{8,0},{... | collective-permute-start | bytes 172040 | tf_op jit(solution)/shard_map/ppermute | solution.py:263
  24.3 1.6 %collective-permute-done.7 = f32[112,128]{1,0:T(8,128)S(1)} collective-permute-done((f32[112,128]{1,0:T(8,128)S(1)}, f32[112,128]{1,0:T(8,128)S(1)}, u32[]{:S(2)}, u32[]{:S(2)}) %collective-permute-start.7) | collective-permute-done | bytes 57376 | tf_op jit(solution)/shard_map/ppermute | solution.py:263
  25.9 2.8 %collective-permute-start.8 = (f32[112,128]{1,0:T(8,128)S(1)}, f32[112,128]{1,0:T(8,128)S(1)}, u32[]{:S(2)}, u32[]{:S(2)}) collective-permute-start(f32[112,128]{1,0:T(8,128)S(1)} %add.77), channel_id=1, source_target_pairs={{0,8},{1,5},{2,10},{3,7},{4,12},{5,1},{6,14},{7,3},{8,0},{9,13},{1... | collective-permute-start | bytes 172040 | tf_op jit(solution)/shard_map/ppermute | solution.py:263
  28.7 1.4 %momentum.1 = (bf16[128,3456]{1,0:T(8,128)(2,1)}, bf16[128,48]{1,0:T(8,128)(2,1)S(1)}) custom-call(bf16[256,3456]{1,0:T(8,128)(2,1)S(1)} %get-tuple-element.13.both, f32[56,128]{1,0:T(8,128)S(1)} %get-tuple-element.12.c_ref, f32[16,128]{1,0:T(8,128)S(1)} %get-tuple-element.14.row_ref, bf16[128,128]{1,0:T(8,128)(2,1)S(1)} %get-tuple-element.15.high_ref, ...), custom_call_target="tpu_custom_call" | custom-call | flops 42467328 | bytes 884736 | tf_op jit(solution)/shard_map/momentum/pallas_call | solution.py:229
  30.1 0.4 %collective-permute-done.8 = f32[112,128]{1,0:T(8,128)S(1)} collective-permute-done((f32[112,128]{1,0:T(8,128)S(1)}, f32[112,128]{1,0:T(8,128)S(1)}, u32[]{:S(2)}, u32[]{:S(2)}) %collective-permute-start.8) | collective-permute-done | bytes 57376 | tf_op jit(solution)/shard_map/ppermute | solution.py:263
  30.5 1.3 %collective-permute-start.9 = (f32[8,128]{1,0:T(8,128)S(1)}, f32[8,128]{1,0:T(8,128)S(1)}, u32[]{:S(2)}, u32[]{:S(2)}) collective-permute-start(f32[8,128]{1,0:T(8,128)S(1)} %slice_add_fusion), channel_id=1, source_target_pairs={{0,2},{1,3},{2,0},{3,1},{4,6},{5,7},{6,4},{7,5},{8,10},{9,11},{10,... | collective-permute-start | bytes 12296 | tf_op jit(solution)/shard_map/ppermute | solution.py:263
  31.8 1.2 %collective-permute-done.9 = f32[8,128]{1,0:T(8,128)S(1)} collective-permute-done((f32[8,128]{1,0:T(8,128)S(1)}, f32[8,128]{1,0:T(8,128)S(1)}, u32[]{:S(2)}, u32[]{:S(2)}) %collective-permute-start.9) | collective-permute-done | bytes 4128 | tf_op jit(solution)/shard_map/ppermute | solution.py:263
  33.1 0.1 collective-permute-start.10
  33.2 1.6 %update.2.refs_0_ = f32[128,3456]{1,0:T(8,128)} custom-call(f32[56,128]{1,0:T(8,128)S(1)} %get-tuple-element.24.total_ref, f32[8,128]{1,0:T(8,128)S(1)} %fusion.2.squares_ref, bf16[128,48]{1,0:T(8,128)(2,1)S(1)} %get-tuple-element.21.row_ref, bf16[128,128]{1,0:T(8,128)(2,1)S(1)} %get-tuple-element.15.high_ref, bf16[128,128]{1,0:T(8,128)(2,1)S(1)} %get-tuple-element.16.low_ref), custom_call_target="tpu_custom_call" | custom-call | flops 42467328 | bytes 1769472 | tf_op jit(solution)/shard_map/update/pallas_call | solution.py:244
  34.8 0.0 collective-permute-done.10
  (13 shorter events, 0.2 us)
Async XLA Ops:
  2.6 4.2 %collective-permute-start = (f32[56,128]{1,0:T(8,128)S(1)}, f32[56,128]{1,0:T(8,128)S(1)}, u32[]{:S(2)}, u32[]{:S(2)}) collective-permute-start(f32[56,128]{1,0:T(8,128)S(1)} %get-tuple-element.12.c_ref), channel_id=1, source_target_pairs={{0,1},{1,0},{2,3},{3,2},{4,5},{5,4},{6,7},{7,6},{8,9},{9,8},{10,11... | collective-permute-start | bytes 86024 | tf_op jit(solution)/shard_map/ppermute | solution.py:263
  6.8 4.6 %collective-permute-start.2 = (f32[112,128]{1,0:T(8,128)S(1)}, f32[112,128]{1,0:T(8,128)S(1)}, u32[]{:S(2)}, u32[]{:S(2)}) collective-permute-start(f32[112,128]{1,0:T(8,128)S(1)} %pad_maximum_fusion), channel_id=1, source_target_pairs={{0,32},{1,17},{2,34},{3,19},{4,36},{5,21},{6,38},{7,23},{8,40},{9,... | collective-permute-start | bytes 172040 | tf_op jit(solution)/shard_map/ppermute | solution.py:263
  8.1 4.2 %collective-permute-start.3 = (f32[112,128]{1,0:T(8,128)S(1)}, f32[112,128]{1,0:T(8,128)S(1)}, u32[]{:S(2)}, u32[]{:S(2)}) collective-permute-start(f32[112,128]{1,0:T(8,128)S(1)} %pad_maximum_fusion), channel_id=1, source_target_pairs={{0,32},{1,25},{2,34},{3,27},{4,36},{5,29},{6,38},{7,31},{8,40},{9,... | collective-permute-start | bytes 172040 | tf_op jit(solution)/shard_map/ppermute | solution.py:263
  8.9 3.5 %collective-permute-start.1 = (f32[112,128]{1,0:T(8,128)S(1)}, f32[112,128]{1,0:T(8,128)S(1)}, u32[]{:S(2)}, u32[]{:S(2)}) collective-permute-start(f32[112,128]{1,0:T(8,128)S(1)} %pad_maximum_fusion), channel_id=1, source_target_pairs={{0,32},{1,9},{2,34},{3,11},{4,36},{5,13},{6,38},{7,15},{8,40},{9,1... | collective-permute-start | bytes 172040 | tf_op jit(solution)/shard_map/ppermute | solution.py:263
  12.3 4.7 %collective-permute-start.6 = (f32[112,128]{1,0:T(8,128)S(1)}, f32[112,128]{1,0:T(8,128)S(1)}, u32[]{:S(2)}, u32[]{:S(2)}) collective-permute-start(f32[112,128]{1,0:T(8,128)S(1)} %add_add_fusion.1), channel_id=1, source_target_pairs={{0,8},{1,65},{2,10},{3,67},{4,12},{5,69},{6,14},{7,71},{8,0},{9,73... | collective-permute-start | bytes 172040 | tf_op jit(solution)/shard_map/ppermute | solution.py:263
  15.4 5.0 %collective-permute-start.5 = (f32[112,128]{1,0:T(8,128)S(1)}, f32[112,128]{1,0:T(8,128)S(1)}, u32[]{:S(2)}, u32[]{:S(2)}) collective-permute-start(f32[112,128]{1,0:T(8,128)S(1)} %add_add_fusion.1), channel_id=1, source_target_pairs={{0,8},{1,97},{2,10},{3,99},{4,12},{5,101},{6,14},{7,103},{8,0},{9,... | collective-permute-start | bytes 172040 | tf_op jit(solution)/shard_map/ppermute | solution.py:263
  16.9 3.6 %collective-permute-start.4 = (f32[112,128]{1,0:T(8,128)S(1)}, f32[112,128]{1,0:T(8,128)S(1)}, u32[]{:S(2)}, u32[]{:S(2)}) collective-permute-start(f32[112,128]{1,0:T(8,128)S(1)} %add_add_fusion.1), channel_id=1, source_target_pairs={{0,8},{1,33},{2,10},{3,35},{4,12},{5,37},{6,14},{7,39},{8,0},{9,41... | collective-permute-start | bytes 172040 | tf_op jit(solution)/shard_map/ppermute | solution.py:263
  20.5 5.3 %collective-permute-start.7 = (f32[112,128]{1,0:T(8,128)S(1)}, f32[112,128]{1,0:T(8,128)S(1)}, u32[]{:S(2)}, u32[]{:S(2)}) collective-permute-start(f32[112,128]{1,0:T(8,128)S(1)} %add_add_fusion), channel_id=1, source_target_pairs={{0,8},{1,193},{2,10},{3,195},{4,12},{5,197},{6,14},{7,199},{8,0},{... | collective-permute-start | bytes 172040 | tf_op jit(solution)/shard_map/ppermute | solution.py:263
  25.9 4.6 %collective-permute-start.8 = (f32[112,128]{1,0:T(8,128)S(1)}, f32[112,128]{1,0:T(8,128)S(1)}, u32[]{:S(2)}, u32[]{:S(2)}) collective-permute-start(f32[112,128]{1,0:T(8,128)S(1)} %add.77), channel_id=1, source_target_pairs={{0,8},{1,5},{2,10},{3,7},{4,12},{5,1},{6,14},{7,3},{8,0},{9,13},{1... | collective-permute-start | bytes 172040 | tf_op jit(solution)/shard_map/ppermute | solution.py:263
  30.5 2.5 %collective-permute-start.9 = (f32[8,128]{1,0:T(8,128)S(1)}, f32[8,128]{1,0:T(8,128)S(1)}, u32[]{:S(2)}, u32[]{:S(2)}) collective-permute-start(f32[8,128]{1,0:T(8,128)S(1)} %slice_add_fusion), channel_id=1, source_target_pairs={{0,2},{1,3},{2,0},{3,1},{4,6},{5,7},{6,4},{7,5},{8,10},{9,11},{10,... | collective-permute-start | bytes 12296 | tf_op jit(solution)/shard_map/ppermute | solution.py:263
  33.1 1.7 %collective-permute-start.10 = (f32[64,128]{1,0:T(8,128)S(1)}, f32[64,128]{1,0:T(8,128)S(1)}, u32[]{:S(2)}, u32[]{:S(2)}) collective-permute-start(f32[64,128]{1,0:T(8,128)S(1)} %pad_maximum_fusion.1), channel_id=1, source_target_pairs={{0,1},{1,0},{2,3},{3,2},{4,5},{5,4},{6,7},{7,6},{8,9},{9,8},{10,11... | collective-permute-start | bytes 98312 | tf_op jit(solution)/shard_map/ppermute | solution.py:263

commit v8 on v7

--- a/solution.py
+++ b/solution.py
@@ -289,17 +289,16 @@
     m, g = momentum[0], grad[0]
     rows, cols = m.shape
     tp = lax.axis_size("tp")
-    core = lax.axis_index("tp") % 2
     own, row, high, low, both = forward(freq_rows, freq_cols, m, g)
     count = own.shape[0]
     other = moved(own, other_core)
-    pair = jnp.concatenate([jnp.where(core == 1, other, own), jnp.where(core == 1, own, other)], axis=0)
+    pair = jnp.concatenate([other, own], axis=0)
     pair = four_way(pair, (0, 1, 0), (0, 2, 0))
     pair = four_way(pair, (1, 0, 0), (3, 0, 0))
-    pair = pair + moved(pair, replica(6, 0, 0))
     kept, turned = momentum_left(both, own, row, high, low)
-    other, kept, turned = lax.optimization_barrier((moved(pair, replica(0, 0, 1)), kept, turned))
+    other, kept, turned = lax.optimization_barrier((moved(pair, replica(6, 0, 0)), kept, turned))
     pair = pair + other
+    pair = pair + moved(pair, replica(0, 0, 1))
     squares = pair * pair
     squares = sum(squares[k : k + KEEP] for k in range(0, 2 * count, KEEP))
     squares = squares + moved(squares, next_chip)

time: 35 us -> 35 us (level)
  transfers between devices with their start and end apart: 11 -> 11, of which waited for: 8 -> 9; matrix products, arithmetic and copies ran while one was open for 0% -> 0% of each run, Pallas kernels for 8% -> 9%
where the time goes in v8:
time: 35 us; the launch traced here: 34.9 us
  starting transfers between devices  19.1 us (55%)
  waiting for transfers between devices  10 us (29%)
  Pallas kernels  5.02 us (14%)
  between operations  0.71 us (2%)
    ppermute x11, starting transfers between devices, moved(): return lax.ppermute(v, ('rep', 'tp'), pairs)  19.1 us
    ppermute x11, waiting for transfers between devices, moved(): return lax.ppermute(v, ('rep', 'tp'), pairs)  10 us
    pallas_call x1, Pallas kernels, forward(): pl.pallas_call(forward_kernel, out_shape=[jax.ShapeDtypeStruct((packed_ro...  1.97 us
    pallas_call x2, Pallas kernels, updated(): pl.pallas_call(functools.partial(update_kernel, entries, core), out_shape...  1.66 us
    pallas_call x1, Pallas kernels, momentum_left(): pl.pallas_call(momentum_kernel, out_shape=[jax.ShapeDtypeStruct((rows, co...  1.38 us
  transfers between devices with their start and end apart: 11, of which 9 were waited for; matrix products, arithmetic and copies ran while one was open for 0% of the time, Pallas kernels for 9%

profile of v8, /device:TPU:1, one launch (start us, length us, event | category | flops | bytes accessed | tf_op | source)
XLA Modules:
  0.0 34.9 jit_solution(8564782904776012384)
XLA Ops:
  0.6 2.0 %forward.1 = (f32[56,128]{1,0:T(8,128)S(1)}, f32[16,128]{1,0:T(8,128)S(1)}, bf16[128,128]{1,0:T(8,128)(2,1)S(1)}, bf16[128,128]{1,0:T(8,128)(2,1)S(1)}, bf16[256,3456]{1,0:T(8,128)(2,1)S(1)}) custom-call(s32[8]{0:T(128)} %fr_ref.1, s32[8]{0:T(128)} %fc_ref.1, bf16[128,3456]{1,0:T(8,128)(2,1)} %bitcast.3, bf16[128,3456]{1,0:T(8,128)(2,1)} %bitcast.4), custom_call_target="tpu_custom_call" | custom-call | flops 42467328 | bytes 1769472 | tf_op jit(solution)/shard_map/forward/pallas_call | solution.py:203
  2.6 3.3 %collective-permute-start = (f32[56,128]{1,0:T(8,128)S(1)}, f32[56,128]{1,0:T(8,128)S(1)}, u32[]{:S(2)}, u32[]{:S(2)}) collective-permute-start(f32[56,128]{1,0:T(8,128)S(1)} %get-tuple-element.12.c_ref), channel_id=1, source_target_pairs={{0,1},{1,0},{2,3},{3,2},{4,5},{5,4},{6,7},{7,6},{8,9},{9,8},{10,11... | collective-permute-start | bytes 86024 | tf_op jit(solution)/shard_map/ppermute | solution.py:263
  6.0 0.9 %collective-permute-done = f32[56,128]{1,0:T(8,128)S(1)} collective-permute-done((f32[56,128]{1,0:T(8,128)S(1)}, f32[56,128]{1,0:T(8,128)S(1)}, u32[]{:S(2)}, u32[]{:S(2)}) %collective-permute-start) | collective-permute-done | bytes 28704 | tf_op jit(solution)/shard_map/ppermute | solution.py:263
  6.8 1.0 %collective-permute-start.3 = (f32[112,128]{1,0:T(8,128)S(1)}, f32[112,128]{1,0:T(8,128)S(1)}, u32[]{:S(2)}, u32[]{:S(2)}) collective-permute-start(f32[112,128]{1,0:T(8,128)S(1)} %constant_dynamic-update-slice_fusion), channel_id=1, source_target_pairs={{0,32},{1,25},{2,34},{3,27},{4,36},{5,29},{6,38},{7,31},{8,40},{9,... | collective-permute-start | bytes 172040 | tf_op jit(solution)/shard_map/ppermute | solution.py:263
  7.8 0.4 %collective-permute-start.2 = (f32[112,128]{1,0:T(8,128)S(1)}, f32[112,128]{1,0:T(8,128)S(1)}, u32[]{:S(2)}, u32[]{:S(2)}) collective-permute-start(f32[112,128]{1,0:T(8,128)S(1)} %constant_dynamic-update-slice_fusion), channel_id=1, source_target_pairs={{0,32},{1,17},{2,34},{3,19},{4,36},{5,21},{6,38},{7,23},{8,40},{9,... | collective-permute-start | bytes 172040 | tf_op jit(solution)/shard_map/ppermute | solution.py:263
  8.2 1.9 %collective-permute-start.1 = (f32[112,128]{1,0:T(8,128)S(1)}, f32[112,128]{1,0:T(8,128)S(1)}, u32[]{:S(2)}, u32[]{:S(2)}) collective-permute-start(f32[112,128]{1,0:T(8,128)S(1)} %constant_dynamic-update-slice_fusion), channel_id=1, source_target_pairs={{0,32},{1,9},{2,34},{3,11},{4,36},{5,13},{6,38},{7,15},{8,40},{9,1... | collective-permute-start | bytes 172040 | tf_op jit(solution)/shard_map/ppermute | solution.py:263
  10.1 1.0 %collective-permute-done.3 = f32[112,128]{1,0:T(8,128)S(1)} collective-permute-done((f32[112,128]{1,0:T(8,128)S(1)}, f32[112,128]{1,0:T(8,128)S(1)}, u32[]{:S(2)}, u32[]{:S(2)}) %collective-permute-start.3) | collective-permute-done | bytes 57376 | tf_op jit(solution)/shard_map/ppermute | solution.py:263
  11.1 1.3 %collective-permute-done.2 = f32[112,128]{1,0:T(8,128)S(1)} collective-permute-done((f32[112,128]{1,0:T(8,128)S(1)}, f32[112,128]{1,0:T(8,128)S(1)}, u32[]{:S(2)}, u32[]{:S(2)}) %collective-permute-start.2) | collective-permute-done | bytes 57376 | tf_op jit(solution)/shard_map/ppermute | solution.py:263
  12.3 0.2 collective-permute-done.1
  12.6 2.9 %collective-permute-start.6 = (f32[112,128]{1,0:T(8,128)S(1)}, f32[112,128]{1,0:T(8,128)S(1)}, u32[]{:S(2)}, u32[]{:S(2)}) collective-permute-start(f32[112,128]{1,0:T(8,128)S(1)} %add_add_fusion.1), channel_id=1, source_target_pairs={{0,8},{1,65},{2,10},{3,67},{4,12},{5,69},{6,14},{7,71},{8,0},{9,73... | collective-permute-start | bytes 172040 | tf_op jit(solution)/shard_map/ppermute | solution.py:263
  15.4 1.5 %collective-permute-start.5 = (f32[112,128]{1,0:T(8,128)S(1)}, f32[112,128]{1,0:T(8,128)S(1)}, u32[]{:S(2)}, u32[]{:S(2)}) collective-permute-start(f32[112,128]{1,0:T(8,128)S(1)} %add_add_fusion.1), channel_id=1, source_target_pairs={{0,8},{1,97},{2,10},{3,99},{4,12},{5,101},{6,14},{7,103},{8,0},{9,... | collective-permute-start | bytes 172040 | tf_op jit(solution)/shard_map/ppermute | solution.py:263
  16.9 0.2 collective-permute-start.4
  17.1 0.0 collective-permute-done.6
  17.1 3.3 %collective-permute-done.5 = f32[112,128]{1,0:T(8,128)S(1)} collective-permute-done((f32[112,128]{1,0:T(8,128)S(1)}, f32[112,128]{1,0:T(8,128)S(1)}, u32[]{:S(2)}, u32[]{:S(2)}) %collective-permute-start.5) | collective-permute-done | bytes 57376 | tf_op jit(solution)/shard_map/ppermute | solution.py:263
  20.4 0.1 collective-permute-done.4
  20.5 3.7 %collective-permute-start.7 = (f32[112,128]{1,0:T(8,128)S(1)}, f32[112,128]{1,0:T(8,128)S(1)}, u32[]{:S(2)}, u32[]{:S(2)}) collective-permute-start(f32[112,128]{1,0:T(8,128)S(1)} %add_add_fusion), channel_id=1, source_target_pairs={{0,8},{1,193},{2,10},{3,195},{4,12},{5,197},{6,14},{7,199},{8,0},{... | collective-permute-start | bytes 172040 | tf_op jit(solution)/shard_map/ppermute | solution.py:263
  24.3 1.4 %momentum.1 = (bf16[128,3456]{1,0:T(8,128)(2,1)}, bf16[128,48]{1,0:T(8,128)(2,1)S(1)}) custom-call(bf16[256,3456]{1,0:T(8,128)(2,1)S(1)} %get-tuple-element.13.both, f32[56,128]{1,0:T(8,128)S(1)} %get-tuple-element.12.c_ref, f32[16,128]{1,0:T(8,128)S(1)} %get-tuple-element.14.row_ref, bf16[128,128]{1,0:T(8,128)(2,1)S(1)} %get-tuple-element.15.high_ref, ...), custom_call_target="tpu_custom_call" | custom-call | flops 42467328 | bytes 884736 | tf_op jit(solution)/shard_map/momentum/pallas_call | solution.py:229
  25.7 0.2 collective-permute-done.7
  25.9 2.8 %collective-permute-start.8 = (f32[112,128]{1,0:T(8,128)S(1)}, f32[112,128]{1,0:T(8,128)S(1)}, u32[]{:S(2)}, u32[]{:S(2)}) collective-permute-start(f32[112,128]{1,0:T(8,128)S(1)} %add.72), channel_id=1, source_target_pairs={{0,8},{1,5},{2,10},{3,7},{4,12},{5,1},{6,14},{7,3},{8,0},{9,13},{1... | collective-permute-start | bytes 172040 | tf_op jit(solution)/shard_map/ppermute | solution.py:263
  28.7 1.8 %collective-permute-done.8 = f32[112,128]{1,0:T(8,128)S(1)} collective-permute-done((f32[112,128]{1,0:T(8,128)S(1)}, f32[112,128]{1,0:T(8,128)S(1)}, u32[]{:S(2)}, u32[]{:S(2)}) %collective-permute-start.8) | collective-permute-done | bytes 57376 | tf_op jit(solution)/shard_map/ppermute | solution.py:263
  30.6 1.3 %collective-permute-start.9 = (f32[8,128]{1,0:T(8,128)S(1)}, f32[8,128]{1,0:T(8,128)S(1)}, u32[]{:S(2)}, u32[]{:S(2)}) collective-permute-start(f32[8,128]{1,0:T(8,128)S(1)} %slice_add_fusion), channel_id=1, source_target_pairs={{0,2},{1,3},{2,0},{3,1},{4,6},{5,7},{6,4},{7,5},{8,10},{9,11},{10,... | collective-permute-start | bytes 12296 | tf_op jit(solution)/shard_map/ppermute | solution.py:263
  31.9 1.2 %collective-permute-done.9 = f32[8,128]{1,0:T(8,128)S(1)} collective-permute-done((f32[8,128]{1,0:T(8,128)S(1)}, f32[8,128]{1,0:T(8,128)S(1)}, u32[]{:S(2)}, u32[]{:S(2)}) %collective-permute-start.9) | collective-permute-done | bytes 4128 | tf_op jit(solution)/shard_map/ppermute | solution.py:263
  33.1 0.1 collective-permute-start.10
  33.2 1.6 %update.2.refs_0_ = f32[128,3456]{1,0:T(8,128)} custom-call(f32[56,128]{1,0:T(8,128)S(1)} %get-tuple-element.24.total_ref, f32[8,128]{1,0:T(8,128)S(1)} %fusion.2.squares_ref, bf16[128,48]{1,0:T(8,128)(2,1)S(1)} %get-tuple-element.21.row_ref, bf16[128,128]{1,0:T(8,128)(2,1)S(1)} %get-tuple-element.15.high_ref, bf16[128,128]{1,0:T(8,128)(2,1)S(1)} %get-tuple-element.16.low_ref), custom_call_target="tpu_custom_call" | custom-call | flops 42467328 | bytes 1769472 | tf_op jit(solution)/shard_map/update/pallas_call | solution.py:244
  34.9 0.0 collective-permute-done.10
  (13 shorter events, 0.2 us)
Async XLA Ops:
  2.6 4.2 %collective-permute-start = (f32[56,128]{1,0:T(8,128)S(1)}, f32[56,128]{1,0:T(8,128)S(1)}, u32[]{:S(2)}, u32[]{:S(2)}) collective-permute-start(f32[56,128]{1,0:T(8,128)S(1)} %get-tuple-element.12.c_ref), channel_id=1, source_target_pairs={{0,1},{1,0},{2,3},{3,2},{4,5},{5,4},{6,7},{7,6},{8,9},{9,8},{10,11... | collective-permute-start | bytes 86024 | tf_op jit(solution)/shard_map/ppermute | solution.py:263
  6.8 4.2 %collective-permute-start.3 = (f32[112,128]{1,0:T(8,128)S(1)}, f32[112,128]{1,0:T(8,128)S(1)}, u32[]{:S(2)}, u32[]{:S(2)}) collective-permute-start(f32[112,128]{1,0:T(8,128)S(1)} %constant_dynamic-update-slice_fusion), channel_id=1, source_target_pairs={{0,32},{1,25},{2,34},{3,27},{4,36},{5,29},{6,38},{7,31},{8,40},{9,... | collective-permute-start | bytes 172040 | tf_op jit(solution)/shard_map/ppermute | solution.py:263
  7.8 4.5 %collective-permute-start.2 = (f32[112,128]{1,0:T(8,128)S(1)}, f32[112,128]{1,0:T(8,128)S(1)}, u32[]{:S(2)}, u32[]{:S(2)}) collective-permute-start(f32[112,128]{1,0:T(8,128)S(1)} %constant_dynamic-update-slice_fusion), channel_id=1, source_target_pairs={{0,32},{1,17},{2,34},{3,19},{4,36},{5,21},{6,38},{7,23},{8,40},{9,... | collective-permute-start | bytes 172040 | tf_op jit(solution)/shard_map/ppermute | solution.py:263
  8.2 4.4 %collective-permute-start.1 = (f32[112,128]{1,0:T(8,128)S(1)}, f32[112,128]{1,0:T(8,128)S(1)}, u32[]{:S(2)}, u32[]{:S(2)}) collective-permute-start(f32[112,128]{1,0:T(8,128)S(1)} %constant_dynamic-update-slice_fusion), channel_id=1, source_target_pairs={{0,32},{1,9},{2,34},{3,11},{4,36},{5,13},{6,38},{7,15},{8,40},{9,1... | collective-permute-start | bytes 172040 | tf_op jit(solution)/shard_map/ppermute | solution.py:263
  12.6 4.5 %collective-permute-start.6 = (f32[112,128]{1,0:T(8,128)S(1)}, f32[112,128]{1,0:T(8,128)S(1)}, u32[]{:S(2)}, u32[]{:S(2)}) collective-permute-start(f32[112,128]{1,0:T(8,128)S(1)} %add_add_fusion.1), channel_id=1, source_target_pairs={{0,8},{1,65},{2,10},{3,67},{4,12},{5,69},{6,14},{7,71},{8,0},{9,73... | collective-permute-start | bytes 172040 | tf_op jit(solution)/shard_map/ppermute | solution.py:263
  15.4 5.0 %collective-permute-start.5 = (f32[112,128]{1,0:T(8,128)S(1)}, f32[112,128]{1,0:T(8,128)S(1)}, u32[]{:S(2)}, u32[]{:S(2)}) collective-permute-start(f32[112,128]{1,0:T(8,128)S(1)} %add_add_fusion.1), channel_id=1, source_target_pairs={{0,8},{1,97},{2,10},{3,99},{4,12},{5,101},{6,14},{7,103},{8,0},{9,... | collective-permute-start | bytes 172040 | tf_op jit(solution)/shard_map/ppermute | solution.py:263
  16.9 3.6 %collective-permute-start.4 = (f32[112,128]{1,0:T(8,128)S(1)}, f32[112,128]{1,0:T(8,128)S(1)}, u32[]{:S(2)}, u32[]{:S(2)}) collective-permute-start(f32[112,128]{1,0:T(8,128)S(1)} %add_add_fusion.1), channel_id=1, source_target_pairs={{0,8},{1,33},{2,10},{3,35},{4,12},{5,37},{6,14},{7,39},{8,0},{9,41... | collective-permute-start | bytes 172040 | tf_op jit(solution)/shard_map/ppermute | solution.py:263
  20.5 5.3 %collective-permute-start.7 = (f32[112,128]{1,0:T(8,128)S(1)}, f32[112,128]{1,0:T(8,128)S(1)}, u32[]{:S(2)}, u32[]{:S(2)}) collective-permute-start(f32[112,128]{1,0:T(8,128)S(1)} %add_add_fusion), channel_id=1, source_target_pairs={{0,8},{1,193},{2,10},{3,195},{4,12},{5,197},{6,14},{7,199},{8,0},{... | collective-permute-start | bytes 172040 | tf_op jit(solution)/shard_map/ppermute | solution.py:263
  25.9 4.6 %collective-permute-start.8 = (f32[112,128]{1,0:T(8,128)S(1)}, f32[112,128]{1,0:T(8,128)S(1)}, u32[]{:S(2)}, u32[]{:S(2)}) collective-permute-start(f32[112,128]{1,0:T(8,128)S(1)} %add.72), channel_id=1, source_target_pairs={{0,8},{1,5},{2,10},{3,7},{4,12},{5,1},{6,14},{7,3},{8,0},{9,13},{1... | collective-permute-start | bytes 172040 | tf_op jit(solution)/shard_map/ppermute | solution.py:263
  30.6 2.5 %collective-permute-start.9 = (f32[8,128]{1,0:T(8,128)S(1)}, f32[8,128]{1,0:T(8,128)S(1)}, u32[]{:S(2)}, u32[]{:S(2)}) collective-permute-start(f32[8,128]{1,0:T(8,128)S(1)} %slice_add_fusion), channel_id=1, source_target_pairs={{0,2},{1,3},{2,0},{3,1},{4,6},{5,7},{6,4},{7,5},{8,10},{9,11},{10,... | collective-permute-start | bytes 12296 | tf_op jit(solution)/shard_map/ppermute | solution.py:263
  33.1 1.7 %collective-permute-start.10 = (f32[64,128]{1,0:T(8,128)S(1)}, f32[64,128]{1,0:T(8,128)S(1)}, u32[]{:S(2)}, u32[]{:S(2)}) collective-permute-start(f32[64,128]{1,0:T(8,128)S(1)} %pad_maximum_fusion), channel_id=1, source_target_pairs={{0,1},{1,0},{2,3},{3,2},{4,5},{5,4},{6,7},{7,6},{8,9},{9,8},{10,11... | collective-permute-start | bytes 98312 | tf_op jit(solution)/shard_map/ppermute | solution.py:263

commit v9 on v8

--- a/solution.py
+++ b/solution.py
@@ -266,7 +266,7 @@
 def replica(dz, dy, dx):
     def partner(z, y, x, near, core):
         if core == 0:
-            return (z ^ 1, y, x, near, core) if dy else (z, y ^ 1, x, near, core)
+            return (z, y ^ 1, x, near, core) if dx else (z, y, x, 1 - near, core)
         return z ^ dz, y ^ dy, x ^ dx, near, core
 
     return partner

time: 35 us -> 35 us (level)
  no operation moved by 1% of the time
where the time goes in v9:
time: 35 us; the launch traced here: 34.9 us
  starting transfers between devices  19.1 us (55%)
  waiting for transfers between devices  9.98 us (29%)
  Pallas kernels  5.02 us (14%)
  between operations  0.71 us (2%)
    ppermute x11, starting transfers between devices, moved(): return lax.ppermute(v, ('rep', 'tp'), pairs)  19.1 us
    ppermute x11, waiting for transfers between devices, moved(): return lax.ppermute(v, ('rep', 'tp'), pairs)  9.98 us
    pallas_call x1, Pallas kernels, forward(): pl.pallas_call(forward_kernel, out_shape=[jax.ShapeDtypeStruct((packed_ro...  1.97 us
    pallas_call x2, Pallas kernels, updated(): pl.pallas_call(functools.partial(update_kernel, entries, core), out_shape...  1.66 us
    pallas_call x1, Pallas kernels, momentum_left(): pl.pallas_call(momentum_kernel, out_shape=[jax.ShapeDtypeStruct((rows, co...  1.38 us
  transfers between devices with their start and end apart: 11, of which 9 were waited for; matrix products, arithmetic and copies ran while one was open for 0% of the time, Pallas kernels for 9%

profile of v9, /device:TPU:1, one launch (start us, length us, event | category | flops | bytes accessed | tf_op | source)
XLA Modules:
  0.0 34.9 jit_solution(1758890567131970534)
XLA Ops:
  0.6 2.0 %forward.1 = (f32[56,128]{1,0:T(8,128)S(1)}, f32[16,128]{1,0:T(8,128)S(1)}, bf16[128,128]{1,0:T(8,128)(2,1)S(1)}, bf16[128,128]{1,0:T(8,128)(2,1)S(1)}, bf16[256,3456]{1,0:T(8,128)(2,1)S(1)}) custom-call(s32[8]{0:T(128)} %fr_ref.1, s32[8]{0:T(128)} %fc_ref.1, bf16[128,3456]{1,0:T(8,128)(2,1)} %bitcast.3, bf16[128,3456]{1,0:T(8,128)(2,1)} %bitcast.4), custom_call_target="tpu_custom_call" | custom-call | flops 42467328 | bytes 1769472 | tf_op jit(solution)/shard_map/forward/pallas_call | solution.py:203
  2.6 3.3 %collective-permute-start = (f32[56,128]{1,0:T(8,128)S(1)}, f32[56,128]{1,0:T(8,128)S(1)}, u32[]{:S(2)}, u32[]{:S(2)}) collective-permute-start(f32[56,128]{1,0:T(8,128)S(1)} %get-tuple-element.12.c_ref), channel_id=1, source_target_pairs={{0,1},{1,0},{2,3},{3,2},{4,5},{5,4},{6,7},{7,6},{8,9},{9,8},{10,11... | collective-permute-start | bytes 86024 | tf_op jit(solution)/shard_map/ppermute | solution.py:263
  6.0 0.9 %collective-permute-done = f32[56,128]{1,0:T(8,128)S(1)} collective-permute-done((f32[56,128]{1,0:T(8,128)S(1)}, f32[56,128]{1,0:T(8,128)S(1)}, u32[]{:S(2)}, u32[]{:S(2)}) %collective-permute-start) | collective-permute-done | bytes 28704 | tf_op jit(solution)/shard_map/ppermute | solution.py:263
  6.8 1.0 %collective-permute-start.3 = (f32[112,128]{1,0:T(8,128)S(1)}, f32[112,128]{1,0:T(8,128)S(1)}, u32[]{:S(2)}, u32[]{:S(2)}) collective-permute-start(f32[112,128]{1,0:T(8,128)S(1)} %constant_dynamic-update-slice_fusion), channel_id=1, source_target_pairs={{0,2},{1,25},{2,0},{3,27},{4,6},{5,29},{6,4},{7,31},{8,10},{9,17},... | collective-permute-start | bytes 172040 | tf_op jit(solution)/shard_map/ppermute | solution.py:263
  7.8 0.4 %collective-permute-start.2 = (f32[112,128]{1,0:T(8,128)S(1)}, f32[112,128]{1,0:T(8,128)S(1)}, u32[]{:S(2)}, u32[]{:S(2)}) collective-permute-start(f32[112,128]{1,0:T(8,128)S(1)} %constant_dynamic-update-slice_fusion), channel_id=1, source_target_pairs={{0,2},{1,17},{2,0},{3,19},{4,6},{5,21},{6,4},{7,23},{8,10},{9,25},... | collective-permute-start | bytes 172040 | tf_op jit(solution)/shard_map/ppermute | solution.py:263
  8.2 1.9 %collective-permute-start.1 = (f32[112,128]{1,0:T(8,128)S(1)}, f32[112,128]{1,0:T(8,128)S(1)}, u32[]{:S(2)}, u32[]{:S(2)}) collective-permute-start(f32[112,128]{1,0:T(8,128)S(1)} %constant_dynamic-update-slice_fusion), channel_id=1, source_target_pairs={{0,2},{1,9},{2,0},{3,11},{4,6},{5,13},{6,4},{7,15},{8,10},{9,1},{1... | collective-permute-start | bytes 172040 | tf_op jit(solution)/shard_map/ppermute | solution.py:263
  10.1 1.0 %collective-permute-done.3 = f32[112,128]{1,0:T(8,128)S(1)} collective-permute-done((f32[112,128]{1,0:T(8,128)S(1)}, f32[112,128]{1,0:T(8,128)S(1)}, u32[]{:S(2)}, u32[]{:S(2)}) %collective-permute-start.3) | collective-permute-done | bytes 57376 | tf_op jit(solution)/shard_map/ppermute | solution.py:263
  11.1 1.3 %collective-permute-done.2 = f32[112,128]{1,0:T(8,128)S(1)} collective-permute-done((f32[112,128]{1,0:T(8,128)S(1)}, f32[112,128]{1,0:T(8,128)S(1)}, u32[]{:S(2)}, u32[]{:S(2)}) %collective-permute-start.2) | collective-permute-done | bytes 57376 | tf_op jit(solution)/shard_map/ppermute | solution.py:263
  12.3 0.2 collective-permute-done.1
  12.6 2.9 %collective-permute-start.6 = (f32[112,128]{1,0:T(8,128)S(1)}, f32[112,128]{1,0:T(8,128)S(1)}, u32[]{:S(2)}, u32[]{:S(2)}) collective-permute-start(f32[112,128]{1,0:T(8,128)S(1)} %add_add_fusion.1), channel_id=1, source_target_pairs={{0,2},{1,65},{2,0},{3,67},{4,6},{5,69},{6,4},{7,71},{8,10},{9,73},... | collective-permute-start | bytes 172040 | tf_op jit(solution)/shard_map/ppermute | solution.py:263
  15.4 1.5 %collective-permute-start.5 = (f32[112,128]{1,0:T(8,128)S(1)}, f32[112,128]{1,0:T(8,128)S(1)}, u32[]{:S(2)}, u32[]{:S(2)}) collective-permute-start(f32[112,128]{1,0:T(8,128)S(1)} %add_add_fusion.1), channel_id=1, source_target_pairs={{0,2},{1,97},{2,0},{3,99},{4,6},{5,101},{6,4},{7,103},{8,10},{9,10... | collective-permute-start | bytes 172040 | tf_op jit(solution)/shard_map/ppermute | solution.py:263
  16.9 0.2 collective-permute-start.4
  17.1 0.0 collective-permute-done.6
  17.1 3.3 %collective-permute-done.5 = f32[112,128]{1,0:T(8,128)S(1)} collective-permute-done((f32[112,128]{1,0:T(8,128)S(1)}, f32[112,128]{1,0:T(8,128)S(1)}, u32[]{:S(2)}, u32[]{:S(2)}) %collective-permute-start.5) | collective-permute-done | bytes 57376 | tf_op jit(solution)/shard_map/ppermute | solution.py:263
  20.4 0.1 collective-permute-done.4
  20.5 3.7 %collective-permute-start.7 = (f32[112,128]{1,0:T(8,128)S(1)}, f32[112,128]{1,0:T(8,128)S(1)}, u32[]{:S(2)}, u32[]{:S(2)}) collective-permute-start(f32[112,128]{1,0:T(8,128)S(1)} %add_add_fusion), channel_id=1, source_target_pairs={{0,2},{1,193},{2,0},{3,195},{4,6},{5,197},{6,4},{7,199},{8,10},{9,... | collective-permute-start | bytes 172040 | tf_op jit(solution)/shard_map/ppermute | solution.py:263
  24.3 1.4 %momentum.1 = (bf16[128,3456]{1,0:T(8,128)(2,1)}, bf16[128,48]{1,0:T(8,128)(2,1)S(1)}) custom-call(bf16[256,3456]{1,0:T(8,128)(2,1)S(1)} %get-tuple-element.13.both, f32[56,128]{1,0:T(8,128)S(1)} %get-tuple-element.12.c_ref, f32[16,128]{1,0:T(8,128)S(1)} %get-tuple-element.14.row_ref, bf16[128,128]{1,0:T(8,128)(2,1)S(1)} %get-tuple-element.15.high_ref, ...), custom_call_target="tpu_custom_call" | custom-call | flops 42467328 | bytes 884736 | tf_op jit(solution)/shard_map/momentum/pallas_call | solution.py:229
  25.7 0.2 collective-permute-done.7
  25.9 2.8 %collective-permute-start.8 = (f32[112,128]{1,0:T(8,128)S(1)}, f32[112,128]{1,0:T(8,128)S(1)}, u32[]{:S(2)}, u32[]{:S(2)}) collective-permute-start(f32[112,128]{1,0:T(8,128)S(1)} %add.72), channel_id=1, source_target_pairs={{0,8},{1,5},{2,10},{3,7},{4,12},{5,1},{6,14},{7,3},{8,0},{9,13},{1... | collective-permute-start | bytes 172040 | tf_op jit(solution)/shard_map/ppermute | solution.py:263
  28.7 1.8 %collective-permute-done.8 = f32[112,128]{1,0:T(8,128)S(1)} collective-permute-done((f32[112,128]{1,0:T(8,128)S(1)}, f32[112,128]{1,0:T(8,128)S(1)}, u32[]{:S(2)}, u32[]{:S(2)}) %collective-permute-start.8) | collective-permute-done | bytes 57376 | tf_op jit(solution)/shard_map/ppermute | solution.py:263
  30.6 1.3 %collective-permute-start.9 = (f32[8,128]{1,0:T(8,128)S(1)}, f32[8,128]{1,0:T(8,128)S(1)}, u32[]{:S(2)}, u32[]{:S(2)}) collective-permute-start(f32[8,128]{1,0:T(8,128)S(1)} %slice_add_fusion), channel_id=1, source_target_pairs={{0,2},{1,3},{2,0},{3,1},{4,6},{5,7},{6,4},{7,5},{8,10},{9,11},{10,... | collective-permute-start | bytes 12296 | tf_op jit(solution)/shard_map/ppermute | solution.py:263
  31.9 1.2 %collective-permute-done.9 = f32[8,128]{1,0:T(8,128)S(1)} collective-permute-done((f32[8,128]{1,0:T(8,128)S(1)}, f32[8,128]{1,0:T(8,128)S(1)}, u32[]{:S(2)}, u32[]{:S(2)}) %collective-permute-start.9) | collective-permute-done | bytes 4128 | tf_op jit(solution)/shard_map/ppermute | solution.py:263
  33.1 0.1 collective-permute-start.10
  33.2 1.6 %update.2.refs_0_ = f32[128,3456]{1,0:T(8,128)} custom-call(f32[56,128]{1,0:T(8,128)S(1)} %get-tuple-element.24.total_ref, f32[8,128]{1,0:T(8,128)S(1)} %fusion.2.squares_ref, bf16[128,48]{1,0:T(8,128)(2,1)S(1)} %get-tuple-element.21.row_ref, bf16[128,128]{1,0:T(8,128)(2,1)S(1)} %get-tuple-element.15.high_ref, bf16[128,128]{1,0:T(8,128)(2,1)S(1)} %get-tuple-element.16.low_ref), custom_call_target="tpu_custom_call" | custom-call | flops 42467328 | bytes 1769472 | tf_op jit(solution)/shard_map/update/pallas_call | solution.py:244
  34.9 0.0 collective-permute-done.10
  (13 shorter events, 0.2 us)
Async XLA Ops:
  2.6 4.2 %collective-permute-start = (f32[56,128]{1,0:T(8,128)S(1)}, f32[56,128]{1,0:T(8,128)S(1)}, u32[]{:S(2)}, u32[]{:S(2)}) collective-permute-start(f32[56,128]{1,0:T(8,128)S(1)} %get-tuple-element.12.c_ref), channel_id=1, source_target_pairs={{0,1},{1,0},{2,3},{3,2},{4,5},{5,4},{6,7},{7,6},{8,9},{9,8},{10,11... | collective-permute-start | bytes 86024 | tf_op jit(solution)/shard_map/ppermute | solution.py:263
  6.8 4.2 %collective-permute-start.3 = (f32[112,128]{1,0:T(8,128)S(1)}, f32[112,128]{1,0:T(8,128)S(1)}, u32[]{:S(2)}, u32[]{:S(2)}) collective-permute-start(f32[112,128]{1,0:T(8,128)S(1)} %constant_dynamic-update-slice_fusion), channel_id=1, source_target_pairs={{0,2},{1,25},{2,0},{3,27},{4,6},{5,29},{6,4},{7,31},{8,10},{9,17},... | collective-permute-start | bytes 172040 | tf_op jit(solution)/shard_map/ppermute | solution.py:263
  7.8 4.5 %collective-permute-start.2 = (f32[112,128]{1,0:T(8,128)S(1)}, f32[112,128]{1,0:T(8,128)S(1)}, u32[]{:S(2)}, u32[]{:S(2)}) collective-permute-start(f32[112,128]{1,0:T(8,128)S(1)} %constant_dynamic-update-slice_fusion), channel_id=1, source_target_pairs={{0,2},{1,17},{2,0},{3,19},{4,6},{5,21},{6,4},{7,23},{8,10},{9,25},... | collective-permute-start | bytes 172040 | tf_op jit(solution)/shard_map/ppermute | solution.py:263
  8.2 4.4 %collective-permute-start.1 = (f32[112,128]{1,0:T(8,128)S(1)}, f32[112,128]{1,0:T(8,128)S(1)}, u32[]{:S(2)}, u32[]{:S(2)}) collective-permute-start(f32[112,128]{1,0:T(8,128)S(1)} %constant_dynamic-update-slice_fusion), channel_id=1, source_target_pairs={{0,2},{1,9},{2,0},{3,11},{4,6},{5,13},{6,4},{7,15},{8,10},{9,1},{1... | collective-permute-start | bytes 172040 | tf_op jit(solution)/shard_map/ppermute | solution.py:263
  12.6 4.5 %collective-permute-start.6 = (f32[112,128]{1,0:T(8,128)S(1)}, f32[112,128]{1,0:T(8,128)S(1)}, u32[]{:S(2)}, u32[]{:S(2)}) collective-permute-start(f32[112,128]{1,0:T(8,128)S(1)} %add_add_fusion.1), channel_id=1, source_target_pairs={{0,2},{1,65},{2,0},{3,67},{4,6},{5,69},{6,4},{7,71},{8,10},{9,73},... | collective-permute-start | bytes 172040 | tf_op jit(solution)/shard_map/ppermute | solution.py:263
  15.4 5.0 %collective-permute-start.5 = (f32[112,128]{1,0:T(8,128)S(1)}, f32[112,128]{1,0:T(8,128)S(1)}, u32[]{:S(2)}, u32[]{:S(2)}) collective-permute-start(f32[112,128]{1,0:T(8,128)S(1)} %add_add_fusion.1), channel_id=1, source_target_pairs={{0,2},{1,97},{2,0},{3,99},{4,6},{5,101},{6,4},{7,103},{8,10},{9,10... | collective-permute-start | bytes 172040 | tf_op jit(solution)/shard_map/ppermute | solution.py:263
  16.9 3.6 %collective-permute-start.4 = (f32[112,128]{1,0:T(8,128)S(1)}, f32[112,128]{1,0:T(8,128)S(1)}, u32[]{:S(2)}, u32[]{:S(2)}) collective-permute-start(f32[112,128]{1,0:T(8,128)S(1)} %add_add_fusion.1), channel_id=1, source_target_pairs={{0,2},{1,33},{2,0},{3,35},{4,6},{5,37},{6,4},{7,39},{8,10},{9,41},... | collective-permute-start | bytes 172040 | tf_op jit(solution)/shard_map/ppermute | solution.py:263
  20.5 5.3 %collective-permute-start.7 = (f32[112,128]{1,0:T(8,128)S(1)}, f32[112,128]{1,0:T(8,128)S(1)}, u32[]{:S(2)}, u32[]{:S(2)}) collective-permute-start(f32[112,128]{1,0:T(8,128)S(1)} %add_add_fusion), channel_id=1, source_target_pairs={{0,2},{1,193},{2,0},{3,195},{4,6},{5,197},{6,4},{7,199},{8,10},{9,... | collective-permute-start | bytes 172040 | tf_op jit(solution)/shard_map/ppermute | solution.py:263
  25.9 4.6 %collective-permute-start.8 = (f32[112,128]{1,0:T(8,128)S(1)}, f32[112,128]{1,0:T(8,128)S(1)}, u32[]{:S(2)}, u32[]{:S(2)}) collective-permute-start(f32[112,128]{1,0:T(8,128)S(1)} %add.72), channel_id=1, source_target_pairs={{0,8},{1,5},{2,10},{3,7},{4,12},{5,1},{6,14},{7,3},{8,0},{9,13},{1... | collective-permute-start | bytes 172040 | tf_op jit(solution)/shard_map/ppermute | solution.py:263
  30.6 2.5 %collective-permute-start.9 = (f32[8,128]{1,0:T(8,128)S(1)}, f32[8,128]{1,0:T(8,128)S(1)}, u32[]{:S(2)}, u32[]{:S(2)}) collective-permute-start(f32[8,128]{1,0:T(8,128)S(1)} %slice_add_fusion), channel_id=1, source_target_pairs={{0,2},{1,3},{2,0},{3,1},{4,6},{5,7},{6,4},{7,5},{8,10},{9,11},{10,... | collective-permute-start | bytes 12296 | tf_op jit(solution)/shard_map/ppermute | solution.py:263
  33.1 1.7 %collective-permute-start.10 = (f32[64,128]{1,0:T(8,128)S(1)}, f32[64,128]{1,0:T(8,128)S(1)}, u32[]{:S(2)}, u32[]{:S(2)}) collective-permute-start(f32[64,128]{1,0:T(8,128)S(1)} %pad_maximum_fusion), channel_id=1, source_target_pairs={{0,1},{1,0},{2,3},{3,2},{4,5},{5,4},{6,7},{7,6},{8,9},{9,8},{10,11... | collective-permute-start | bytes 98312 | tf_op jit(solution)/shard_map/ppermute | solution.py:263
